TPU v7x, 128 devices: a whole 4x4x4 slice. The times are simulated.
128 devices in a mesh: fsdp: 16 (over x_hi, z, core), tp: 8 (over y, x_lo).
Axes of the slice: x: 4 (x_hi: 2, x_lo: 2; x = x_hi * 2 + x_lo), y: 4, z: 4, core: 2. Of those that a mesh axis runs over, the one named last changes fastest.
Arguments:
- token_ids: int32 [2, 2560], replicated, may hold values from 0 to 76031
- embedding: bfloat16 [76032, 8192], P('fsdp', 'tp'), may hold values from -6 to 6
- cache_lengths: int32 [2560], P('fsdp'), may hold values from 2 to 128, as said below
- q_weight: bfloat16 [8192, 8192], P(('fsdp', 'tp')), may hold values from -6 to 6
- q_bias: bfloat16 [8192], P('tp'), may hold values from -10 to 10
- kv_bias: bfloat16 [2, 1024], P(None, 'tp'), may hold values from -3 to 3
- kv_master: float32 [8192, 2, 1024], P(('fsdp', 'tp')), may hold values from -6 to 6
- kv_moment1: float32 [8192, 2, 1024], P(('fsdp', 'tp')), may hold values from -0.6 to 0.6
- kv_moment2: float32 [8192, 2, 1024], P(('fsdp', 'tp')), may hold values from 0.01 to 4
- kv_grad: bfloat16 [8192, 2, 1024], P(('fsdp', 'tp')), may hold values from -6 to 6
- k_cache: bfloat16 [2560, 128, 1024], P('fsdp', None, 'tp'), may hold values from -16 to 16
- v_cache: bfloat16 [2560, 128, 1024], P('fsdp', None, 'tp'), may hold values from -6 to 6
Outputs:
- context: bfloat16 [2, 2560, 8192], P(None, 'fsdp', 'tp')
- kv_master_new: float32 [8192, 2, 1024], P(('fsdp', 'tp'))
- kv_moment1_new: float32 [8192, 2, 1024], P(('fsdp', 'tp'))
- kv_moment2_new: float32 [8192, 2, 1024], P(('fsdp', 'tp'))
Inputs may be any that keep to these rules, and one draw needn't show every extreme that they name: Row r's cache holds keys and values at its first cache_lengths[r] positions only; some row holds 128.
All inputs are finite; a program needn't handle non-finite values.
Results may differ from a plain program's by a relative error of at most 0.02.
Values may be sent and summed in bfloat16 or wider, within the bound.
No kernel may reach another device: no remote copies, remote signals or barrier semaphores. Data moves between devices by JAX's collectives and lax.ppermute only.
A program may use at most 128 MiB of HBM per device.

v0:
```python
import math

import jax
import jax.numpy as jnp
from jax import lax
from jax.sharding import PartitionSpec as P

D = 8192
HEAD = 128
ADAM_STEP = 10


def adamw_update(master, moment1, moment2, gradient):
    gradient = gradient.astype(jnp.float32)
    moment1_new = 0.9 * moment1 + 0.1 * gradient
    moment2_new = 0.95 * moment2 + 0.05 * gradient * gradient
    first_fix = 1.0 - 0.9**ADAM_STEP
    second_fix = 1.0 - 0.95**ADAM_STEP
    update = moment1_new / first_fix / (jnp.sqrt(moment2_new / second_fix) + 1e-08)
    master_new = master - 0.01 * (update + 0.1 * master)
    return (master_new, moment1_new, moment2_new)


def rotate_half(field, positions):
    half = field.shape[-1] // 2
    freqs = jnp.exp(jnp.arange(half, dtype=jnp.float32) * (-math.log(1000000.0) / half))
    angles = positions[:, :, None].astype(jnp.float32) * freqs
    cosine = jnp.cos(angles)[:, :, None, :]
    sine = jnp.sin(angles)[:, :, None, :]
    first = field[..., :half]
    second = field[..., half:]
    return jnp.concatenate(
        [first * cosine - second * sine, second * cosine + first * sine], axis=-1
    )


def per_device(
    token_ids,
    embedding,
    cache_lengths,
    q_weight,
    q_bias,
    kv_bias,
    kv_master,
    kv_moment1,
    kv_moment2,
    kv_grad,
    k_cache,
    v_cache,
):
    vocab_rows = embedding.shape[0]
    local_ids = token_ids - lax.axis_index("fsdp") * vocab_rows
    inside = (local_ids >= 0) & (local_ids < vocab_rows)
    picked = jnp.take(embedding, jnp.clip(local_ids, 0, vocab_rows - 1), axis=0)
    picked = jnp.where(inside[:, :, None], picked.astype(jnp.float32), 0.0)
    embedded_part = lax.psum_scatter(
        picked.astype(jnp.bfloat16), "fsdp", scatter_dimension=1, tiled=True
    )
    embedded = lax.all_gather(embedded_part, "tp", axis=2, tiled=True)
    group_rows = embedded.shape[1]
    widened = embedded.astype(jnp.float32)
    stats = jnp.mean(widened * widened, axis=-1, keepdims=True)
    normed = (widened * lax.rsqrt(stats + 1e-06)).astype(jnp.bfloat16)
    tokens = normed.reshape(2 * group_rows, D)
    master_new, moment1_new, moment2_new = adamw_update(kv_master, kv_moment1, kv_moment2, kv_grad)
    rollout = master_new.astype(jnp.bfloat16)
    query_part, pair_part = (
        lax.all_to_all(q_weight[:, None, :], "tp", split_axis=2, concat_axis=0, tiled=True),
        lax.all_to_all(rollout, "tp", split_axis=2, concat_axis=0, tiled=True),
    )
    query_cols = query_part.shape[2]
    pair_cols = 2 * pair_part.shape[2]
    pieces = (
        lax.all_gather(query_part, "fsdp", axis=0, tiled=True),
        lax.all_gather(pair_part, "fsdp", axis=0, tiled=True),
    )
    piece_rows = pieces[0].shape[0]
    query_piece = pieces[0].reshape(piece_rows, query_cols)
    pair_piece = pieces[1].reshape(piece_rows, pair_cols)
    query_raw = jnp.dot(tokens, query_piece, preferred_element_type=jnp.float32)
    pair_raw = jnp.dot(tokens, pair_piece, preferred_element_type=jnp.float32)
    query_raw = query_raw / math.sqrt(D) + q_bias.astype(jnp.float32)
    pair_raw = pair_raw / math.sqrt(D) + kv_bias.reshape(pair_cols).astype(jnp.float32)
    head_count = query_cols // HEAD
    kv_count = pair_cols // (2 * HEAD)
    positions = cache_lengths[None, :] + jnp.arange(2, dtype=jnp.int32)[:, None]
    queries = rotate_half(query_raw.reshape(2, group_rows, head_count, HEAD), positions).astype(
        jnp.bfloat16
    )
    new_keys = rotate_half(
        pair_raw[:, : pair_cols // 2].reshape(2, group_rows, kv_count, HEAD), positions
    ).astype(jnp.bfloat16)
    new_values = (
        pair_raw[:, pair_cols // 2 :].reshape(2, group_rows, kv_count, HEAD).astype(jnp.bfloat16)
    )
    grouped = queries.reshape(2, group_rows, kv_count, head_count // kv_count, HEAD)
    cache_size = k_cache.shape[1]
    cache_keys = k_cache.reshape(group_rows, cache_size, kv_count, HEAD)
    cache_values = v_cache.reshape(group_rows, cache_size, kv_count, HEAD)
    cache_scores = jnp.einsum(
        "srkgd,rlkd->srkgl", grouped, cache_keys, preferred_element_type=jnp.float32
    ) / math.sqrt(HEAD)
    new_scores = jnp.einsum(
        "srkgd,urkd->srkgu", grouped, new_keys, preferred_element_type=jnp.float32
    ) / math.sqrt(HEAD)
    cache_valid = (jnp.arange(cache_size)[None, :] < cache_lengths[:, None])[None, :, None, None, :]
    new_valid = (jnp.arange(2)[None, :] <= jnp.arange(2)[:, None])[:, None, None, None, :]
    cache_scores = jnp.where(cache_valid, cache_scores, -1e30)
    new_scores = jnp.where(new_valid, new_scores, -1e30)
    peak = jnp.maximum(
        jnp.max(cache_scores, axis=-1, keepdims=True), jnp.max(new_scores, axis=-1, keepdims=True)
    )
    cache_exp = jnp.exp(cache_scores - peak)
    new_exp = jnp.exp(new_scores - peak)
    total = jnp.sum(cache_exp, axis=-1, keepdims=True) + jnp.sum(new_exp, axis=-1, keepdims=True)
    cache_weights = (cache_exp / total).astype(jnp.bfloat16)
    new_weights = (new_exp / total).astype(jnp.bfloat16)
    context = jnp.einsum(
        "srkgl,rlkd->srkgd", cache_weights, cache_values, preferred_element_type=jnp.float32
    )
    context = context + jnp.einsum(
        "srkgu,urkd->srkgd", new_weights, new_values, preferred_element_type=jnp.float32
    )
    context = context.reshape(2, group_rows, query_cols).astype(jnp.bfloat16)
    return (context, master_new, moment1_new, moment2_new)


def solution(mesh):
    placed = (
        P(),
        P("fsdp", "tp"),
        P("fsdp"),
        P(("fsdp", "tp"), None),
        P("tp"),
        P(None, "tp"),
        P(("fsdp", "tp"), None, None),
        P(("fsdp", "tp"), None, None),
        P(("fsdp", "tp"), None, None),
        P(("fsdp", "tp"), None, None),
        P("fsdp", None, "tp"),
        P("fsdp", None, "tp"),
    )
    return jax.shard_map(
        per_device,
        mesh=mesh,
        in_specs=placed,
        out_specs=(
            P(None, "fsdp", "tp"),
            P(("fsdp", "tp"), None, None),
            P(("fsdp", "tp"), None, None),
            P(("fsdp", "tp"), None, None),
        ),
        check_vma=False,
    )
```

profile of v0, /device:TPU:64, one launch (start us, length us, event | category | flops | bytes accessed | tf_op | source)
XLA Modules:
  0.0 475.0 jit_solution(15493994658733034030)
XLA Ops:
  7.2 0.0 reduce-scatter.2.cloned.1.call-start
  7.2 0.8 compare_and_fusion
  8.0 30.8 %gather_fusion = bf16[5120,1024]{1,0:T(8,128)(2,1)} fusion(bf16[4752,1024]{1,0:T(8,128)(2,1)} %param.13, s32[5120]{0:T(1024)S(1)} %broadcast_clamp_fusion), kind=kCustom, calls=%fused_computation | custom fusion | bytes 20992000 | tf_op jit(solution)/shard_map/jit(_take)/gather | solution.py:54
  38.9 10.9 %select_convert_fusion = bf16[2,2560,1024]{2,1,0:T(8,128)(2,1)} fusion(bf16[2,2560,1024]{2,1,0:T(8,128)(2,1)} %bitcast.162, pred[2,2560]{1,0:T(4,128)(4,1)S(1)} %get-tuple-element.40, pred[2,2560]{1,0:T(4,128)(4,1)S(1)} %get-tuple-element.50), kind=kLoop, calls=%fused_computation.1 | loop fusion | flops 20971520 | bytes 20981760 | tf_op jit(solution)/shard_map/convert_element_type | solution.py:57
  49.8 0.0 reduce-scatter.2.cloned.1.call-update
  49.8 0.0 all-gather.8.cloned.1.call-start
  49.9 1.0 copy-done.7
  50.8 0.2 copy-done.8
  51.0 0.2 copy-done.9
  51.1 0.1 copy-done.10
  51.2 1.8 fusion.67
  53.0 0.4 copy.152
  53.4 0.4 reshape.227
  53.8 12.5 %all_to_all.36 = bf16[8,2,8192]{2,1,0:T(2,128)(2,1)S(1)} all-to-all(bf16[8,2,8192]{2,1,0:T(2,128)(2,1)S(1)} %reshape.227), channel_id=1, replica_groups=mesh['fsdp'=16,'tp'=8] {'tp'}, dimensions={0} | all-to-all | bytes 524288 | tf_op jit(solution)/shard_map/all_to_all | solution.py:69
  66.2 0.3 reshape.228
  66.6 1.0 copy.173
  67.6 0.0 all-gather.4.cloned.1.call-start
  67.7 94.5 %reduce-scatter.2.cloned.1.call-done = bf16[2,160,1024]{2,1,0:T(8,128)(2,1)} async-done(((bf16[2,2560,1024]{2,1,0:T(8,128)(2,1)}), bf16[2,160,1024]{2,1,0:T(8,128)(2,1)}) %reduce-scatter.2.cloned.1.call-update) | async-done | bytes 655376 | tf_op jit(solution)/shard_map/reduce_scatter | solution.py:56
  162.2 0.0 all-gather.6.cloned.1.call-start
  162.3 6.8 %copy.141 = bf16[64,1,8192]{0,1,2:T(2,128)(2,1)} copy(bf16[64,1,8192]{2,0,1:T(8,128)(2,1)S(1)} %bitcast.175) | data formatting | bytes 2097152 | tf_op jit(solution)/shard_map/broadcast_in_dim | solution.py:68
  169.1 0.5 broadcast.112
  169.6 45.2 %reduce.4 = bf16[8192,64]{1,0:T(8,128)(2,1)S(1)} reduce(bf16[8192,1,64]{2,1,0:T(2,128)(2,1)} %bitcast.163, bf16[]{:T(256)} %broadcast.112), dimensions={1}, to_apply=%bitcast.154.reduce_sub_computation | reduce | bytes 2097154
  214.8 1.7 reshape.229
  216.5 24.2 %all_to_all.37 = bf16[8,2,32768]{2,1,0:T(2,128)(2,1)S(1)} all-to-all(bf16[8,2,32768]{2,1,0:T(2,128)(2,1)S(1)} %reshape.229), channel_id=1, replica_groups=mesh['fsdp'=16,'tp'=8] {'tp'}, dimensions={0} | all-to-all | bytes 2097152 | tf_op jit(solution)/shard_map/all_to_all | solution.py:68
  240.6 4.3 reshape.230
  245.0 8.2 %copy.142 = bf16[64,1,8192]{2,0,1:T(8,128)(2,1)S(1)} copy(bf16[64,1,8192]{0,1,2:T(2,128)(2,1)} %bitcast.164) | data formatting | bytes 2097152 | tf_op jit(solution)/shard_map/all_to_all | solution.py:68
  253.1 0.6 copy.182
  253.8 1.5 copy.143
  255.4 0.1 copy.145
  255.5 1.2 copy.165
  256.7 1.2 copy.166
  257.9 1.2 copy.167
  259.2 0.1 iota_compare_fusion
  259.3 2.7 multiply_cosine_fusion
  262.0 0.0 all-gather.8.cloned.1.call-done
  262.0 6.4 %copy.155 = bf16[8192,2,128]{0,2,1:T(8,128)(2,1)} copy(bf16[8192,2,128]{2,0,1:T(8,128)(2,1)} %all-gather.8.cloned.1.call-done) | data formatting | bytes 8388608 | tf_op jit(solution)/shard_map/all_gather | solution.py:75
  268.4 64.5 %all-gather.4.cloned.1.call-done = bf16[2,160,8192]{2,1,0:T(8,128)(2,1)} async-done(((bf16[2,160,1024]{2,1,0:T(8,128)(2,1)}), bf16[2,160,8192]{2,1,0:T(8,128)(2,1)}) %all-gather.4.cloned.1.call-update) | async-done | bytes 5242896 | tf_op jit(solution)/shard_map/all_gather | solution.py:59
  332.9 3.8 fusion.2
  336.7 0.3 copy-done
  336.9 1.5 fusion.3
  338.4 0.7 copy-done.2
  339.1 1.5 fusion.40
  340.7 0.0 copy-done.1
  340.8 0.1 fusion.71
  340.9 0.1 copy.180
  341.0 0.1 copy.181
  341.1 0.6 fusion.64
  341.7 0.6 fusion.63
  342.3 0.1 copy.169
  342.4 100.4 %all-gather.6.cloned.1.call-done = bf16[8192,1,1024]{2,0,1:T(8,128)(2,1)} async-done(((bf16[512,1,1024]{2,0,1:T(8,128)(2,1)}), bf16[8192,1,1024]{2,0,1:T(8,128)(2,1)}) %all-gather.6.cloned.1.call-update) | async-done | bytes 16777232 | tf_op jit(solution)/shard_map/all_gather | solution.py:74
  442.8 11.0 %fusion.26 = f32[40,8,8,128]{3,1,2,0:T(8,128)S(1)} fusion(bf16[320,8192]{1,0:T(8,128)(2,1)} %bitcast.167, bf16[8192,1,1024]{2,0,1:T(8,128)(2,1)} %all-gather.6.cloned.1.call-done, f32[1024]{0:T(1024)S(1)} %convert_element_type.77), kind=kOutput, calls=%fused_computation.18 | convolution fusion | flops 5369364480 | bytes 23334912 | tf_op jit(solution)/shard_map/dot_general | solution.py:80
  453.8 0.3 copy.183
  454.1 0.4 fusion.70
  454.5 0.4 subtract_convert_fusion
  454.9 3.2 fusion.72
  458.1 5.2 %bitcast_reduce_fusion = (f32[2,160,8]{2,0,1:T(2,128)S(1)}, f32[160,1,128,2,8]{2,4,3,0,1:T(8,128)S(1)}) fusion(bf16[160,128,128]{2,1,0:T(8,128)(2,1)} %param.22, bf16[2,160,8,64]{3,2,0,1:T(8,128)(2,1)S(1)} %get-tuple-element.43, bf16[2,160,8,64]{3,2,0,1:T(8,128)(2,1)S(1)} %get-tuple-element.42, pred[160,128]{1,0:T(8,128)(4,1)S(1)} %iota_compare_fusion), kind=kOutput, calls=%fused_computation.21 | convolution fusion | flops 86177280 | bytes 7239680 | tf_op jit(solution)/shard_map/srkgd,rlkd->srkgl/dot_general | solution.py:100
  463.4 0.1 max.12
  463.5 0.6 fusion.49
  464.1 0.9 fusion.41
  465.0 0.1 add.103
  465.1 0.6 fusion.50
  465.7 1.6 fusion.36
  467.3 0.2 convert_element_type.89
  467.4 1.0 copy.164
  (40 shorter events, 0.2 us)
Async XLA Ops:
  7.2 155.1 %reduce-scatter.2.cloned.1.call-start = ((), (), s32[]{:S(2)}) async-start(), calls=%async_computation.3 | async-start | bytes 11141120 | tf_op jit(solution)/shard_map/reduce_scatter | solution.py:56
  49.8 1.0 copy-start.7
  49.8 1.2 copy-start.8
  49.8 1.4 copy-start.9
  49.8 1.4 copy-start.10
  49.8 212.2 %all-gather.8.cloned.1.call-start = ((), (), s32[]{:S(2)}) async-start(), calls=%async_computation.6 | async-start | bytes 4456448 | tf_op jit(solution)/shard_map/all_gather | solution.py:75
  53.4 108.9 %copy-start.6 = (bf16[64,8192]{1,0:T(8,128)(2,1)S(1)}, bf16[64,8192]{1,0:T(8,128)(2,1)}, u32[]{:S(2)}) copy-start(bf16[64,8192]{1,0:T(8,128)(2,1)} %param.15) | copy-start | bytes 3145732
  67.6 265.3 %all-gather.4.cloned.1.call-start = ((), (), s32[]{:S(2)}) async-start(), calls=%async_computation.4 | async-start | bytes 5898240 | tf_op jit(solution)/shard_map/all_gather | solution.py:59
  162.2 280.6 %all-gather.6.cloned.1.call-start = ((), (), s32[]{:S(2)}) async-start(), calls=%async_computation.5 | async-start | bytes 17825792 | tf_op jit(solution)/shard_map/all_gather | solution.py:74
  253.8 1.6 copy-start.12
  253.8 1.6 copy-start.11
  253.8 1.7 copy-start.5
  253.8 2.9 copy-start.4
  255.3 2.6 copy-start.3
  255.3 3.8 copy-start.13
  332.9 4.0 copy-start
  336.9 2.2 copy-start.2
  338.4 2.3 copy-start.1
  458.1 7.6 %slice-start = ((s8[5242880]{0:T(1024)(128)(4,1)}), s8[4194304]{0:T(1024)(128)(4,1)S(1)}, s32[]{:S(2)}) async-start(s8[5242880]{0:T(1024)(128)(4,1)} %bitcast.178), calls=%async_computation.7 | async-start | bytes 8388608
  463.3 2.4 slice-start.1
Sparse Core Ops, SparseCore 0:
  49.9 112.2 reduce-scatter.1
  164.7 54.1 all-gather.7
  220.6 112.2 all-gather.3
  335.2 107.5 all-gather.5
where the time goes:
time: 480 us; the launch traced here: 475 us
  waiting for transfers between devices  260 us (54%)
  local copies, waits for them, and re-layouts  71.4 us (15%)
  other arithmetic  70 us (15%)
  blocking collectives  36.6 us (8%)
  matrix products  23.1 us (5%)
  between operations  14.2 us (3%)
    all_gather x1, waiting for transfers between devices, per_device(): lax.all_gather(query_part, 'fsdp', axis=0, tiled=True)  100 us
    reduce_scatter x1, waiting for transfers between devices, per_device(): lax.psum_scatter(picked.astype(jnp.bfloat16), 'fsdp', scatter_dimension=1...  94.5 us
    all_gather x1, waiting for transfers between devices, per_device(): embedded = lax.all_gather(embedded_part, 'tp', axis=2, tiled=True)  64.5 us
    unnamed x2, other arithmetic  45.2 us
    gather x1, local copies, waits for them, and re-layouts, per_device(): picked = jnp.take(embedding, jnp.clip(local_ids, 0, vocab_rows - 1), axis=0)  30.8 us
    all_to_all x1, blocking collectives, per_device(): lax.all_to_all(q_weight[:, None, :], 'tp', split_axis=2, concat_axis=0, t...  24.2 us
    unnamed x45, local copies, waits for them, and re-layouts  15.3 us
    all_to_all x1, blocking collectives, per_device(): lax.all_to_all(rollout, 'tp', split_axis=2, concat_axis=0, tiled=True)  12.5 us
  transfers between devices with their start and end apart: 4, of which 3 were waited for; matrix products, arithmetic and copies ran while one was open for 20% of the time, Pallas kernels for 0%

commit v1 on v0

v1 whole, which is shorter than its diff:
```python
import functools
import math

import jax
import jax.numpy as jnp
from jax import lax
from jax.experimental import pallas as pl
from jax.experimental.pallas import tpu as pltpu
from jax.sharding import Mesh
from jax.sharding import PartitionSpec as P

D = 8192
HEAD = 128
ADAM_STEP = 10

NAMES = ("xh", "z", "c", "y", "xl")
SIZES = (2, 4, 2, 4, 2)
FSDP = ("xh", "z", "c")
TP = ("y", "xl")
OWNERS = 16
PAIRS = 8
ROWS = 160
TOKENS = 4 * ROWS
HALF = 512
SLOTS = 64
COLS = 1280


def pairs_of(move):
    found = []
    total = math.prod(SIZES)
    for index in range(total):
        rest, coords = index, []
        for size in reversed(SIZES):
            coords.append(rest % size)
            rest //= size
        target = 0
        for value, size in zip(move(*reversed(coords)), SIZES):
            target = target * size + value
        found.append((index, target))
    return found


def send(array, move):
    return lax.ppermute(array, NAMES, pairs_of(move))


def along_y(step):
    return lambda xh, z, c, y, xl: (xh, z, c, (y + step) % 4, xl)


def other_xl(xh, z, c, y, xl):
    return (xh, z, c, y, 1 - xl)


def other_xh(xh, z, c, y, xl):
    return (1 - xh, z, c, y, xl)


def swap_xh_core(xh, z, c, y, xl):
    return (c, z, xh, y, xl)


def adamw_update(master, moment1, moment2, gradient):
    gradient = gradient.astype(jnp.float32)
    moment1_new = 0.9 * moment1 + 0.1 * gradient
    moment2_new = 0.95 * moment2 + 0.05 * gradient * gradient
    first_fix = 1.0 - 0.9**ADAM_STEP
    second_fix = 1.0 - 0.95**ADAM_STEP
    update = moment1_new / first_fix / (jnp.sqrt(moment2_new / second_fix) + 1e-08)
    master_new = master - 0.01 * (update + 0.1 * master)
    return (master_new, moment1_new, moment2_new)


def rotation(positions):
    half = HEAD // 2
    freqs = jnp.exp(jnp.arange(half, dtype=jnp.float32) * (-math.log(1000000.0) / half))
    angles = positions[:, :, None].astype(jnp.float32) * freqs
    return jnp.cos(angles)[:, :, None, :], jnp.sin(angles)[:, :, None, :]


def rotate_half(field, cosine, sine):
    half = field.shape[-1] // 2
    first = field[..., :half]
    second = field[..., half:]
    return jnp.concatenate(
        [first * cosine - second * sine, second * cosine + first * sine], axis=-1
    )


def pack_kernel(query_ref, key_ref, value_ref, out_ref):
    out_ref[0, :, 0:1024] = query_ref[...]
    out_ref[0, :, 1024:1152] = key_ref[...]
    out_ref[0, :, 1152:1280] = value_ref[...]


def pack_columns(q_weight, keys, values):
    rows = q_weight.shape[0]
    return pl.pallas_call(
        pack_kernel,
        grid=(8,),
        in_specs=[
            pl.BlockSpec((rows, 1024), lambda t: (0, t)),
            pl.BlockSpec((rows, 128), lambda t: (0, t)),
            pl.BlockSpec((rows, 128), lambda t: (0, t)),
        ],
        out_specs=pl.BlockSpec((1, rows, COLS), lambda t: (t, 0, 0)),
        out_shape=jax.ShapeDtypeStruct((8, rows, COLS), jnp.bfloat16),
    )(q_weight, keys, values)


def project_kernel(place_ref, *refs):
    blocks = refs[:8]
    w_ref, mine_ref, other_ref, held, total, squares, sems = refs[8:]
    step = pl.program_id(0)
    copies = []
    for index in range(6):
        copies.append((pltpu.make_async_copy(blocks[index], held.at[index], sems.at[index]),))
    half = TOKENS // 2
    lower, upper = refs[6], refs[7]
    for index in range(2):
        copies.append(
            (
                pltpu.make_async_copy(
                    lower.at[index], held.at[6 + index, pl.ds(0, half)], sems.at[6 + 2 * index]
                ),
                pltpu.make_async_copy(
                    upper.at[index], held.at[6 + index, pl.ds(half, half)], sems.at[7 + 2 * index]
                ),
            )
        )

    @pl.when(step == 0)
    def _():
        for group in copies:
            for copy in group:
                copy.start()
        total[...] = jnp.zeros_like(total)
        squares[...] = jnp.zeros_like(squares)

    for index in range(8):

        @pl.when(step == index)
        def _(index=index):
            for copy in copies[index]:
                copy.wait()

    tokens = held.at[step]

    def tile(index, carry):
        columns = pl.ds(pl.multiple_of(index * 256, 256), 256)
        total[:, columns] += jnp.dot(
            tokens[...], w_ref[0, :, columns], preferred_element_type=jnp.float32
        )
        return carry

    lax.fori_loop(0, COLS // 256, tile, 0)
    for start in range(0, HALF, 128):
        part = tokens[:, start : start + 128].astype(jnp.float32)
        squares[...] += part * part

    @pl.when(step == 7)
    def _():
        xh = place_ref[8]
        own = pl.ds(pl.multiple_of(xh * half, half), half)
        partner = pl.ds(pl.multiple_of((1 - xh) * half, half), half)
        mine_ref[:, 0:COLS] = total[own, :]
        own_sum = jnp.sum(squares[own, :], axis=1, keepdims=True)
        mine_ref[:, COLS:] = jnp.broadcast_to(own_sum, (half, 128))
        other_ref[:, 0:COLS] = total[partner, :].astype(jnp.bfloat16)
        sums = jnp.sum(squares[partner, :], axis=1, keepdims=True)
        high = sums.astype(jnp.bfloat16).astype(jnp.float32)
        lanes = lax.broadcasted_iota(jnp.int32, (half, 128), 1)
        other_ref[:, COLS:] = jnp.where(lanes < 64, high, sums - high).astype(jnp.bfloat16)


def project(place, blocks, lower, upper, weights):
    half = TOKENS // 2
    anywhere = pl.BlockSpec(memory_space=pl.ANY)
    return pl.pallas_call(
        project_kernel,
        grid_spec=pltpu.PrefetchScalarGridSpec(
            num_scalar_prefetch=1,
            grid=(8,),
            in_specs=[anywhere] * 8
            + [pl.BlockSpec((1, HALF, COLS), lambda k, place: (place[k], 0, 0))],
            out_specs=[
                pl.BlockSpec((half, COLS + 128), lambda k, place: (0, 0)),
                pl.BlockSpec((half, COLS + 128), lambda k, place: (0, 0)),
            ],
            scratch_shapes=[
                pltpu.VMEM((8, TOKENS, HALF), jnp.bfloat16),
                pltpu.VMEM((TOKENS, COLS), jnp.float32),
                pltpu.VMEM((TOKENS, 128), jnp.float32),
                pltpu.SemaphoreType.DMA((10,)),
            ],
        ),
        out_shape=[
            jax.ShapeDtypeStruct((half, COLS + 128), jnp.float32),
            jax.ShapeDtypeStruct((half, COLS + 128), jnp.bfloat16),
        ],
        compiler_params=pltpu.CompilerParams(vmem_limit_bytes=48 << 20),
        cost_estimate=pl.CostEstimate(
            flops=2 * TOKENS * 4096 * COLS, bytes_accessed=20 << 20, transcendentals=0
        ),
    )(place, *blocks, lower, upper, weights)


def per_device(
    token_ids,
    embedding,
    cache_lengths,
    q_weight,
    q_bias,
    kv_bias,
    kv_master,
    kv_moment1,
    kv_moment2,
    kv_grad,
    k_cache,
    v_cache,
):
    xh, z, c = (lax.axis_index(name) for name in FSDP)
    y, xl = (lax.axis_index(name) for name in TP)
    fsdp_index = (xh * 4 + z) * 2 + c
    pair = z * 2 + c
    vocab_rows = embedding.shape[0]

    master_new, moment1_new, moment2_new = adamw_update(kv_master, kv_moment1, kv_moment2, kv_grad)
    rollout = master_new.astype(jnp.bfloat16)
    packed = pack_columns(q_weight, rollout[:, 0, :], rollout[:, 1, :])
    columns = lax.all_to_all(packed, TP, split_axis=0, concat_axis=0)
    columns = send(columns.reshape(512, COLS), swap_xh_core)
    weights = lax.all_gather(columns, ("z", "c"))

    paired = token_ids.reshape(2, 2, PAIRS, ROWS).transpose(2, 1, 0, 3).reshape(PAIRS, TOKENS)
    owners = paired // vocab_rows
    order = jnp.arange(TOKENS, dtype=jnp.int32)
    earlier = order[:, None] < order[None, :]
    same_id = paired[:, :, None] == paired[:, None, :]
    first = ~jnp.any(same_id & earlier[None], axis=1)
    first_owner = jnp.where(first, owners, -1)
    ranks = jnp.sum(
        ((first_owner[:, :, None] == owners[:, None, :]) & earlier[None]).astype(jnp.int32), axis=1
    )
    rounds = (jnp.max(jnp.where(first, ranks, 0)) + SLOTS) // SLOTS

    local = paired - fsdp_index * vocab_rows
    sent_rank = jnp.where(first_owner == fsdp_index, ranks, -1)
    own_ids = lax.dynamic_index_in_dim(paired, pair, 0, keepdims=False)
    own_first = lax.dynamic_index_in_dim(first, pair, 0, keepdims=False)
    own_ranks = lax.dynamic_index_in_dim(ranks, pair, 0, keepdims=False)
    own_owners = lax.dynamic_index_in_dim(owners, pair, 0, keepdims=False)
    got_rank = jnp.sum(
        jnp.where(
            (own_ids[:, None] == own_ids[None, :]) & own_first[:, None], own_ranks[:, None], 0
        ),
        axis=0,
    )

    def fetch(turn):
        slots = turn * SLOTS + jnp.arange(SLOTS, dtype=jnp.int32)
        wanted = jnp.sum(
            jnp.where(sent_rank[:, :, None] == slots[None, None, :], local[:, :, None], 0), axis=1
        )
        rows = embedding.at[wanted.reshape(-1)].get(mode="promise_in_bounds")
        rows = rows.reshape(PAIRS, SLOTS, 2, HALF).transpose(2, 0, 1, 3)
        rows = rows.reshape(OWNERS, SLOTS, HALF)
        rows = lax.all_to_all(rows, FSDP, split_axis=0, concat_axis=0)
        slot = got_rank - turn * SLOTS
        inside = (slot >= 0) & (slot < SLOTS)
        spot = jnp.where(inside, own_owners * SLOTS + slot, -1)
        pick = spot[:, None] == jnp.arange(OWNERS * SLOTS, dtype=jnp.int32)[None, :]
        return jnp.dot(
            pick.astype(jnp.bfloat16),
            rows.reshape(OWNERS * SLOTS, HALF),
            preferred_element_type=jnp.float32,
        ).astype(jnp.bfloat16)

    own = fetch(0)
    _, own = lax.while_loop(
        lambda state: state[0] < rounds,
        lambda state: (state[0] + 1, state[1] + fetch(state[0])),
        (jnp.int32(1), own),
    )

    half = TOKENS // 2
    across = send(own, other_xl)
    below = send(own, along_y(1))
    above = send(own, along_y(-1))
    far_low = send(below[:half], along_y(1))
    far_high = send(above[half:], along_y(-1))
    below_across = send(across, along_y(1))
    above_across = send(across, along_y(-1))
    far_low_across = send(far_low, other_xl)
    far_high_across = send(far_high, other_xl)
    members = [
        y * 2 + xl,
        y * 2 + 1 - xl,
        (y + 3) % 4 * 2 + xl,
        (y + 1) % 4 * 2 + xl,
        (y + 3) % 4 * 2 + 1 - xl,
        (y + 1) % 4 * 2 + 1 - xl,
        (y + 2) % 4 * 2 + xl,
        (y + 2) % 4 * 2 + 1 - xl,
    ]
    place = jnp.stack([member % 4 * 2 + member // 4 for member in members] + [xh]).astype(jnp.int32)
    mine, other = project(
        place,
        (own, across, below, above, below_across, above_across),
        jnp.stack([far_low, far_low_across]),
        jnp.stack([far_high, far_high_across]),
        weights,
    )
    arrived = send(other, other_xh).astype(jnp.float32)

    group_rows = ROWS
    sums = mine[:, COLS] + arrived[:, COLS] + arrived[:, COLS + 64]
    scale = lax.rsqrt(sums / D + 1e-06) / math.sqrt(D)
    bias = jnp.concatenate([q_bias, kv_bias.reshape(256)]).astype(jnp.float32)
    raw = (mine[:, :COLS] + arrived[:, :COLS]) * scale[:, None] + bias
    positions = cache_lengths[None, :] + jnp.arange(2, dtype=jnp.int32)[:, None]
    cosine, sine = rotation(positions)
    queries = rotate_half(raw[:, :1024].reshape(2, group_rows, 8, HEAD), cosine, sine).astype(
        jnp.bfloat16
    )
    new_keys = rotate_half(raw[:, 1024:1152].reshape(2, group_rows, 1, HEAD), cosine, sine).astype(
        jnp.bfloat16
    )
    new_values = raw[:, 1152:].reshape(2, group_rows, 1, HEAD).astype(jnp.bfloat16)
    grouped = queries.reshape(2, group_rows, 1, 8, HEAD)
    cache_size = k_cache.shape[1]
    cache_keys = k_cache.reshape(group_rows, cache_size, 1, HEAD)
    cache_values = v_cache.reshape(group_rows, cache_size, 1, HEAD)
    cache_scores = jnp.einsum(
        "srkgd,rlkd->srkgl", grouped, cache_keys, preferred_element_type=jnp.float32
    ) / math.sqrt(HEAD)
    new_scores = jnp.einsum(
        "srkgd,urkd->srkgu", grouped, new_keys, preferred_element_type=jnp.float32
    ) / math.sqrt(HEAD)
    cache_valid = (jnp.arange(cache_size)[None, :] < cache_lengths[:, None])[None, :, None, None, :]
    new_valid = (jnp.arange(2)[None, :] <= jnp.arange(2)[:, None])[:, None, None, None, :]
    cache_scores = jnp.where(cache_valid, cache_scores, -1e30)
    new_scores = jnp.where(new_valid, new_scores, -1e30)
    peak = jnp.maximum(
        jnp.max(cache_scores, axis=-1, keepdims=True), jnp.max(new_scores, axis=-1, keepdims=True)
    )
    cache_exp = jnp.exp(cache_scores - peak)
    new_exp = jnp.exp(new_scores - peak)
    total = jnp.sum(cache_exp, axis=-1, keepdims=True) + jnp.sum(new_exp, axis=-1, keepdims=True)
    cache_weights = (cache_exp / total).astype(jnp.bfloat16)
    new_weights = (new_exp / total).astype(jnp.bfloat16)
    context = jnp.einsum(
        "srkgl,rlkd->srkgd", cache_weights, cache_values, preferred_element_type=jnp.float32
    )
    context = context + jnp.einsum(
        "srkgu,urkd->srkgd", new_weights, new_values, preferred_element_type=jnp.float32
    )
    context = context.reshape(2, group_rows, 1024).astype(jnp.bfloat16)
    return (context, master_new, moment1_new, moment2_new)


def solution(mesh):
    parts = Mesh(mesh.devices.reshape(SIZES), NAMES)
    placed = (
        P(),
        P(FSDP, TP),
        P(FSDP),
        P(NAMES, None),
        P(TP),
        P(None, TP),
        P(NAMES, None, None),
        P(NAMES, None, None),
        P(NAMES, None, None),
        P(NAMES, None, None),
        P(FSDP, None, TP),
        P(FSDP, None, TP),
    )
    return jax.shard_map(
        per_device,
        mesh=parts,
        in_specs=placed,
        out_specs=(
            P(None, FSDP, TP),
            P(NAMES, None, None),
            P(NAMES, None, None),
            P(NAMES, None, None),
        ),
        check_vma=False,
    )
```

time: 480 us -> 223 us (0.46)
  waiting for transfers between devices: 260 us -> 62.1 us
  other arithmetic: 70 us -> 20.2 us
  local copies, waits for them, and re-layouts: 71.4 us -> 21.9 us
  starting transfers between devices: 0.16 us -> 38.7 us
  Pallas kernels: 0 us -> 25.5 us
  blocking collectives: 36.6 us -> 24.1 us
  matrix products: 23.1 us -> 12.2 us
    all_gather x3 -> x1, waiting for transfers between devices: 165 us -> 0.02 us  [per_device(): weights = lax.all_gather(columns, ('z', 'c'))]
    reduce_scatter x1 -> x0, waiting for transfers between devices: 94.5 us -> none  [per_device(): lax.psum_scatter(picked.astype(jnp.bfloat16), 'fsdp', scatter_dimension=1...]
    unnamed x2 -> x1, other arithmetic: 45.2 us -> 0.01 us
    ppermute x0 -> x11, waiting for transfers between devices: none -> 44.2 us  [send(): return lax.ppermute(array, NAMES, pairs_of(move))]
    all_to_all x0 -> x1, starting transfers between devices: none -> 27.8 us  [fetch(): rows = lax.all_to_all(rows, FSDP, split_axis=0, concat_axis=0)]
    pallas_call x0 -> x2, Pallas kernels: none -> 25.5 us  [the longest x1 20.1 us: project(): pl.pallas_call(project_kernel, grid_spec=pltpu.PrefetchScalarGridSpec(num...]
    gather x1, local copies, waits for them, and re-layouts: 30.8 us -> 7.74 us  [fetch(): rows = embedding.at[wanted.reshape(-1)].get(mode='promise_in_bounds')]
    all_to_all x0 -> x1, waiting for transfers between devices: none -> 17.8 us  [fetch(): rows = lax.all_to_all(rows, FSDP, split_axis=0, concat_axis=0)]
  transfers between devices with their start and end apart: 4 -> 13, of which waited for: 3 -> 7; matrix products, arithmetic and copies ran while one was open for 20% -> 14% of each run, Pallas kernels for 0% -> 0%
where the time goes in v1:
time: 223 us; the launch traced here: 220 us
  waiting for transfers between devices  62.1 us (28%)
  starting transfers between devices  38.7 us (17%)
  Pallas kernels  25.5 us (11%)
  blocking collectives  24.1 us (11%)
  local copies, waits for them, and re-layouts  21.9 us (10%)
  other arithmetic  20.2 us (9%)
  between operations  15.2 us (7%)
  matrix products  12.2 us (5%)
    ppermute x11, waiting for transfers between devices, send(): return lax.ppermute(array, NAMES, pairs_of(move))  44.2 us
    all_to_all x1, starting transfers between devices, fetch(): rows = lax.all_to_all(rows, FSDP, split_axis=0, concat_axis=0)  27.8 us
    all_to_all x1, blocking collectives, per_device(): columns = lax.all_to_all(packed, TP, split_axis=0, concat_axis=0)  24.1 us
    pallas_call x1, Pallas kernels, project(): pl.pallas_call(project_kernel, grid_spec=pltpu.PrefetchScalarGridSpec(num...  20.1 us
    all_to_all x1, waiting for transfers between devices, fetch(): rows = lax.all_to_all(rows, FSDP, split_axis=0, concat_axis=0)  17.8 us
    ppermute x11, starting transfers between devices, send(): return lax.ppermute(array, NAMES, pairs_of(move))  10.9 us
    unnamed x42, local copies, waits for them, and re-layouts  10 us
    gather x1, local copies, waits for them, and re-layouts, fetch(): rows = embedding.at[wanted.reshape(-1)].get(mode='promise_in_bounds')  7.74 us
  transfers between devices with their start and end apart: 13, of which 7 were waited for; matrix products, arithmetic and copies ran while one was open for 14% of the time, Pallas kernels for 0%

profile of v1, /device:TPU:64, one launch (start us, length us, event | category | flops | bytes accessed | tf_op | source)
XLA Modules:
  0.0 219.8 jit_solution(12450083478135260775)
XLA Ops:
  7.2 3.2 %fusion.69 = (bf16[64,2,1024]{2,0,1:T(8,128)(2,1)S(1)}, f32[64,2,1024]{2,0,1:T(8,128)}, f32[64,2,1024]{2,0,1:T(8,128)}, f32[64,2,1024]{2,0,1:T(8,128)}) fusion(f32[64,2,1024]{2,1,0:T(2,128)} %param.20, bf16[64,2,1024]{2,1,0:T(2,128)(2,1)} %param.23, f32[64,2,1024]{2,1,0:T(2,128)} %param.21, f32[64,2,1024]{2,1,0:T(2,128)} %param.22), kind=kLoop, calls=%fused_computation.118 | loop fusion | flops 2228224 | bytes 3670016 | tf_op jit(solution)/shard_map/convert_element_type | solution.py:230
  10.4 0.7 slice_bitcast_fusion.1
  11.1 5.3 %shard_map.147 = bf16[8,64,1280]{2,1,0:T(8,128)(2,1)} custom-call(bf16[64,8192]{1,0:T(8,128)(2,1)} %query_ref.1, bf16[64,1024]{1,0:T(8,128)(2,1)} %get-tuple-element.93.key_ref, bf16[64,1024]{1,0:T(8,128)(2,1)} %get-tuple-element.92.value_ref), custom_call_target="tpu_custom_call" | custom-call | tf_op jit(solution)/shard_map/pallas_call | solution.py:99
  16.5 24.1 %all_to_all.16 = bf16[8,64,1280]{2,1,0:T(8,128)(2,1)S(1)} all-to-all(bf16[8,64,1280]{2,1,0:T(8,128)(2,1)} %shard_map.147), channel_id=1, replica_groups=mesh['xh'=2,'z'=4,'c'=2,'y'=4,'xl'=2] {'y','xl'}, dimensions={0} | all-to-all | bytes 2621440 | tf_op jit(solution)/shard_map/all_to_all | solution.py:232
  40.5 0.9 collective-permute-start.9
  41.4 1.1 copy-done.5
  42.8 0.1 iota_compare_fusion.8
  42.9 2.7 %and_reduce_fusion = pred[8,640]{1,0:T(8,128)(4,1)S(1)} fusion(s32[8,640]{1,0:T(8,128)S(1)} %reshape.386, pred[640,640]{1,0:T(8,128)(4,1)S(1)} %iota_compare_fusion.8), kind=kLoop, calls=%fused_computation.13 | loop fusion | flops 9825280 | bytes 435200 | tf_op jit(solution)/shard_map/reduce_or | solution.py:241
  45.6 2.7 %convert_reduce_fusion = s32[8,640]{1,0:T(8,128)S(1)} fusion(s32[8,640]{1,0:T(8,128)S(1)} %get-tuple-element.101, s32[8,640]{1,0:T(8,128)S(1)} %get-tuple-element.100, pred[640,640]{1,0:T(8,128)(4,1)S(1)} %iota_compare_fusion.8), kind=kLoop, calls=%fused_computation.12 | loop fusion | flops 13102080 | bytes 471040 | tf_op jit(solution)/shard_map/reduce_sum | solution.py:243
  48.3 0.6 select_reduce_fusion.3
  48.9 0.2 select_reduce_fusion.2
  49.2 7.7 %gather_fusion.1 = bf16[512,1024]{1,0:T(8,128)(2,1)S(1)} fusion(bf16[4752,1024]{1,0:T(8,128)(2,1)} %param.15, s32[1024]{0:T(1024)S(1)} %pad_clamp_fusion.1), kind=kCustom, calls=%fused_computation.1 | custom fusion | bytes 2099200 | tf_op jit(solution)/shard_map/gather | solution.py:266
  57.0 0.8 reshape.388
  57.8 1.2 copy.67
  59.0 27.8 %all-to-all-start.1 = ((bf16[16,64,512]{2,1,0:T(8,128)(2,1)}), bf16[16,64,512]{2,1,0:T(8,128)(2,1)S(1)}, u32[]{:S(2)}, u32[]{:S(2)}) async-start(bf16[16,64,512]{2,1,0:T(8,128)(2,1)} %bitcast.16), calls=%async_computation.1 | async-start | bytes 2097152 | tf_op jit(solution)/shard_map/all_to_all | solution.py:269
  87.5 0.4 select_reduce_fusion.1
  88.0 17.8 %all-to-all-done.1 = bf16[16,64,512]{2,1,0:T(8,128)(2,1)S(1)} async-done(((bf16[16,64,512]{2,1,0:T(8,128)(2,1)}), bf16[16,64,512]{2,1,0:T(8,128)(2,1)S(1)}, u32[]{:S(2)}, u32[]{:S(2)}) %all-to-all-start.1) | async-done | bytes 1048608 | tf_op jit(solution)/shard_map/all_to_all | solution.py:269
  105.8 1.7 fusion.26
  107.5 2.0 collective-permute-start.1
  109.5 15.6 %collective-permute-done.2.refs_3_ = bf16[640,512]{1,0:T(8,128)(2,1)S(1)} collective-permute-done((bf16[640,512]{1,0:T(8,128)(2,1)}, bf16[640,512]{1,0:T(8,128)(2,1)S(1)}, u32[]{:S(2)}, u32[]{:S(2)}) %collective-permute-start.2) | collective-permute-done | bytes 655392 | tf_op jit(solution)/shard_map/ppermute | solution.py:45
  125.1 1.4 collective-permute-start.7
  126.6 0.7 collective-permute-start.5
  127.4 3.1 %collective-permute-start.4 = (bf16[640,512]{1,0:T(8,128)(2,1)S(1)}, bf16[640,512]{1,0:T(8,128)(2,1)}, u32[]{:S(2)}, u32[]{:S(2)}) collective-permute-start(bf16[640,512]{1,0:T(8,128)(2,1)S(1)} %collective-permute-done.refs_1_), channel_id=1, source_target_pairs={{0,6},{1,7},{2,0},{3,1},{4,2},{5,3},{6,4},{7,5},{8,14},{9,15},{10,... | collective-permute-start | bytes 1966088 | tf_op jit(solution)/shard_map/ppermute | solution.py:45
  130.6 5.2 %collective-permute-done.7 = bf16[320,512]{1,0:T(8,128)(2,1)S(1)} collective-permute-done((bf16[320,512]{1,0:T(8,128)(2,1)S(1)}, bf16[320,512]{1,0:T(8,128)(2,1)S(1)}, u32[]{:S(2)}, u32[]{:S(2)}) %collective-permute-start.7) | collective-permute-done | bytes 327712 | tf_op jit(solution)/shard_map/ppermute | solution.py:45
  135.8 2.7 %collective-permute-done.5 = bf16[320,512]{1,0:T(8,128)(2,1)S(1)} collective-permute-done((bf16[320,512]{1,0:T(8,128)(2,1)S(1)}, bf16[320,512]{1,0:T(8,128)(2,1)S(1)}, u32[]{:S(2)}, u32[]{:S(2)}) %collective-permute-start.5) | collective-permute-done | bytes 327712 | tf_op jit(solution)/shard_map/ppermute | solution.py:45
  138.5 0.5 collective-permute-start.6
  139.0 7.4 %collective-permute-done.8 = bf16[320,512]{1,0:T(8,128)(2,1)S(1)} collective-permute-done((bf16[320,512]{1,0:T(8,128)(2,1)S(1)}, bf16[320,512]{1,0:T(8,128)(2,1)S(1)}, u32[]{:S(2)}, u32[]{:S(2)}) %collective-permute-start.8) | collective-permute-done | bytes 327712 | tf_op jit(solution)/shard_map/ppermute | solution.py:45
  146.4 0.7 copy-done.9
  147.2 1.0 pad_maximum_fusion.1.refs_7_
  148.2 2.5 %collective-permute-done.6 = bf16[320,512]{1,0:T(8,128)(2,1)} collective-permute-done((bf16[320,512]{1,0:T(8,128)(2,1)S(1)}, bf16[320,512]{1,0:T(8,128)(2,1)}, u32[]{:S(2)}, u32[]{:S(2)}) %collective-permute-start.6) | collective-permute-done | bytes 327712 | tf_op jit(solution)/shard_map/ppermute | solution.py:45
  150.7 1.1 pad_maximum_fusion.refs_6_
  151.9 1.1 copy-done.1
  153.0 20.1 %shard_map.148 = (f32[320,1408]{1,0:T(8,128)}, bf16[320,1408]{1,0:T(8,128)(2,1)S(1)}) custom-call(s32[9]{0:T(128)S(1)} %stack.57.place_ref, bf16[640,512]{1,0:T(8,128)(2,1)} %get-tuple-element.49.refs_0_, bf16[640,512]{1,0:T(8,128)(2,1)S(1)} %copy-done.1, bf16[640,512]{1,0:T(8,128)(2,1)S(1)} %collective-permute-done.1.refs_2_, ...), custom_call_target="tpu_custom_call" | custom-call | flops 6710886400 | bytes 20971520 | tf_op jit(solution)/shard_map/pallas_call | solution.py:180
  173.2 2.2 collective-permute-start.10
  175.4 0.1 copy.74
  175.5 2.2 %copy.85 = f32[64,2,1024]{2,1,0:T(2,128)} copy(f32[64,2,1024]{2,0,1:T(8,128)} %get-tuple-element.85) | data formatting | bytes 1048576
  177.7 1.2 copy.86
  178.9 1.2 copy.87
  180.2 0.7 iota_compare_fusion.12
  180.9 3.5 %multiply_cosine_fusion = (f32[2,160,64]{2,0,1:T(2,128)}, f32[2,160,64]{2,0,1:T(2,128)}) fusion(f32[64]{0:T(128)S(1)} %multiply_exponential_fusion, f32[2,160]{0,1:T(8,128)S(1)} %copy.74), kind=kLoop, calls=%fused_computation.62 | loop fusion | flops 20480 | bytes 165376 | tf_op jit(solution)/shard_map/cos | solution.py:79
  184.3 10.9 %collective-permute-done.10 = bf16[320,1408]{1,0:T(8,128)(2,1)S(1)} collective-permute-done((bf16[320,1408]{1,0:T(8,128)(2,1)S(1)}, bf16[320,1408]{1,0:T(8,128)(2,1)S(1)}, u32[]{:S(2)}, u32[]{:S(2)}) %collective-permute-start.10) | collective-permute-done | bytes 901152 | tf_op jit(solution)/shard_map/ppermute | solution.py:45
  195.2 0.1 convert_element_type.72
  195.3 0.2 fusion.49
  195.6 0.3 fusion.10
  195.9 0.2 slice_bitcast_fusion
  196.0 0.1 fusion.73
  196.2 0.1 copy.98
  196.3 0.1 copy.99
  196.4 0.6 fusion.64
  197.0 0.6 fusion.63
  197.5 0.3 copy.100
  197.8 0.4 fusion.72
  198.3 0.1 copy.89
  198.4 0.3 copy-done.6
  198.8 0.3 subtract_convert_fusion
  199.2 0.4 copy-done.10
  199.5 5.1 %bitcast_reduce_fusion = (f32[2,160,8]{2,0,1:T(2,128)S(1)}, f32[160,1,128,2,8]{2,4,3,0,1:T(8,128)S(1)}) fusion(bf16[160,128,128]{2,1,0:T(8,128)(2,1)} %param.24, bf16[2,160,8,64]{3,2,0,1:T(8,128)(2,1)S(1)} %get-tuple-element.89, bf16[2,160,8,64]{3,2,0,1:T(8,128)(2,1)S(1)} %get-tuple-element.88, pred[160,128]{1,0:T(8,128)(4,1)S(1)} %copy-done.10), kind=kOutput, calls=%fused_computation.33 | convolution fusion | flops 86177280 | bytes 7239680 | tf_op jit(solution)/shard_map/srkgd,rlkd->srkgl/dot_general | solution.py:335
  204.7 3.2 %fusion.74 = (f32[2,160,8]{2,0,1:T(2,128)S(1)}, f32[2,160,1,8,2]{3,4,0,1,2:T(2,128)S(1)}) fusion(bf16[2,160,128,1]{2,0,3,1:T(2,128)(2,1)S(1)} %copy.89, bf16[2,160,8,64]{3,2,0,1:T(8,128)(2,1)S(1)} %get-tuple-element.89, bf16[2,160,8,64]{3,2,0,1:T(8,128)(2,1)S(1)} %get-tuple-element.88, pred[2,2]{1,0:T(4,128)(4,1)S(1)} %iota_compare_fusion.13), kind=kOutput, calls=%fused_computation.121 | convolution fusion | flops 2634240 | bytes 768004 | tf_op jit(solution)/shard_map/srkgd,urkd->srkgu/dot_general | solution.py:338
  208.0 0.6 fusion.44
  208.6 0.9 fusion.36
  209.6 0.6 fusion.50
  210.2 1.6 fusion.32
  211.8 0.2 convert_element_type.81
  212.0 1.0 copy.84
  (66 shorter events, 1.1 us)
Async XLA Ops:
  7.2 144.8 %all-gather.3.cloned.1.call-start = ((), (), s32[]{:S(2)}) async-start(), calls=%async_computation.3 | async-start | bytes 11796480 | tf_op jit(solution)/shard_map/all_gather | solution.py:234
  40.5 2.0 copy-start.11
  40.5 0.9 collective-permute-start.9
  41.4 1.1 copy-start.5
  59.0 46.8 %all-to-all-start.1 = ((bf16[16,64,512]{2,1,0:T(8,128)(2,1)}), bf16[16,64,512]{2,1,0:T(8,128)(2,1)S(1)}, u32[]{:S(2)}, u32[]{:S(2)}) async-start(bf16[16,64,512]{2,1,0:T(8,128)(2,1)} %bitcast.16), calls=%async_computation.1 | async-start | bytes 2097152 | tf_op jit(solution)/shard_map/all_to_all | solution.py:269
  107.5 17.6 %collective-permute-start.2 = (bf16[640,512]{1,0:T(8,128)(2,1)}, bf16[640,512]{1,0:T(8,128)(2,1)S(1)}, u32[]{:S(2)}, u32[]{:S(2)}) collective-permute-start(bf16[640,512]{1,0:T(8,128)(2,1)} %get-tuple-element.49.refs_0_), channel_id=1, source_target_pairs={{0,6},{1,7},{2,0},{3,1},{4,2},{5,3},{6,4},{7,5},{8,14},{9,15},{10,... | collective-permute-start | bytes 1966088 | tf_op jit(solution)/shard_map/ppermute | solution.py:45
  107.5 19.1 %collective-permute-start.1 = (bf16[640,512]{1,0:T(8,128)(2,1)}, bf16[640,512]{1,0:T(8,128)(2,1)S(1)}, u32[]{:S(2)}, u32[]{:S(2)}) collective-permute-start(bf16[640,512]{1,0:T(8,128)(2,1)} %get-tuple-element.49.refs_0_), channel_id=1, source_target_pairs={{0,2},{1,3},{2,4},{3,5},{4,6},{5,7},{6,0},{7,1},{8,10},{9,11},{10,... | collective-permute-start | bytes 1966088 | tf_op jit(solution)/shard_map/ppermute | solution.py:45
  109.5 17.8 %collective-permute-start = (bf16[640,512]{1,0:T(8,128)(2,1)}, bf16[640,512]{1,0:T(8,128)(2,1)S(1)}, u32[]{:S(2)}, u32[]{:S(2)}) collective-permute-start(bf16[640,512]{1,0:T(8,128)(2,1)} %get-tuple-element.49.refs_0_), channel_id=1, source_target_pairs={{0,1},{1,0},{2,3},{3,2},{4,5},{5,4},{6,7},{7,6},{8,9},{9,8},{10,11... | collective-permute-start | bytes 1966088 | tf_op jit(solution)/shard_map/ppermute | solution.py:45
  125.1 10.6 %collective-permute-start.7 = (bf16[320,512]{1,0:T(8,128)(2,1)S(1)}, bf16[320,512]{1,0:T(8,128)(2,1)S(1)}, u32[]{:S(2)}, u32[]{:S(2)}) collective-permute-start(bf16[320,512]{1,0:T(8,128)(2,1)S(1)} %slice.70), channel_id=1, source_target_pairs={{0,6},{1,7},{2,0},{3,1},{4,2},{5,3},{6,4},{7,5},{8,14},{9,15},{10,... | collective-permute-start | bytes 983048 | tf_op jit(solution)/shard_map/ppermute | solution.py:45
  126.6 11.9 %collective-permute-start.5 = (bf16[320,512]{1,0:T(8,128)(2,1)S(1)}, bf16[320,512]{1,0:T(8,128)(2,1)S(1)}, u32[]{:S(2)}, u32[]{:S(2)}) collective-permute-start(bf16[320,512]{1,0:T(8,128)(2,1)S(1)} %slice.69), channel_id=1, source_target_pairs={{0,2},{1,3},{2,4},{3,5},{4,6},{5,7},{6,0},{7,1},{8,10},{9,11},{10,... | collective-permute-start | bytes 983048 | tf_op jit(solution)/shard_map/ppermute | solution.py:45
  127.3 24.5 %copy-start = (bf16[640,512]{1,0:T(8,128)(2,1)}, bf16[640,512]{1,0:T(8,128)(2,1)S(1)}, u32[]{:S(2)}) copy-start(bf16[640,512]{1,0:T(8,128)(2,1)S(1)} %collective-permute-done.refs_1_) | copy-start | bytes 1966084
  127.3 24.5 %collective-permute-start.3 = (bf16[640,512]{1,0:T(8,128)(2,1)S(1)}, bf16[640,512]{1,0:T(8,128)(2,1)}, u32[]{:S(2)}, u32[]{:S(2)}) collective-permute-start(bf16[640,512]{1,0:T(8,128)(2,1)S(1)} %collective-permute-done.refs_1_), channel_id=1, source_target_pairs={{0,2},{1,3},{2,4},{3,5},{4,6},{5,7},{6,0},{7,1},{8,10},{9,11},{10,... | collective-permute-start | bytes 1966088 | tf_op jit(solution)/shard_map/ppermute | solution.py:45
  127.4 24.4 %collective-permute-start.4 = (bf16[640,512]{1,0:T(8,128)(2,1)S(1)}, bf16[640,512]{1,0:T(8,128)(2,1)}, u32[]{:S(2)}, u32[]{:S(2)}) collective-permute-start(bf16[640,512]{1,0:T(8,128)(2,1)S(1)} %collective-permute-done.refs_1_), channel_id=1, source_target_pairs={{0,6},{1,7},{2,0},{3,1},{4,2},{5,3},{6,4},{7,5},{8,14},{9,15},{10,... | collective-permute-start | bytes 1966088 | tf_op jit(solution)/shard_map/ppermute | solution.py:45
  135.8 10.6 %collective-permute-start.8 = (bf16[320,512]{1,0:T(8,128)(2,1)S(1)}, bf16[320,512]{1,0:T(8,128)(2,1)S(1)}, u32[]{:S(2)}, u32[]{:S(2)}) collective-permute-start(bf16[320,512]{1,0:T(8,128)(2,1)S(1)} %collective-permute-done.7), channel_id=1, source_target_pairs={{0,1},{1,0},{2,3},{3,2},{4,5},{5,4},{6,7},{7,6},{8,9},{9,8},{10,11... | collective-permute-start | bytes 983048 | tf_op jit(solution)/shard_map/ppermute | solution.py:45
  138.5 12.2 %copy-start.8 = (bf16[320,512]{1,0:T(8,128)(2,1)}, bf16[320,512]{1,0:T(8,128)(2,1)S(1)}, u32[]{:S(2)}) copy-start(bf16[320,512]{1,0:T(8,128)(2,1)S(1)} %collective-permute-done.5) | copy-start | bytes 983044
  138.5 12.2 %collective-permute-start.6 = (bf16[320,512]{1,0:T(8,128)(2,1)S(1)}, bf16[320,512]{1,0:T(8,128)(2,1)}, u32[]{:S(2)}, u32[]{:S(2)}) collective-permute-start(bf16[320,512]{1,0:T(8,128)(2,1)S(1)} %collective-permute-done.5), channel_id=1, source_target_pairs={{0,1},{1,0},{2,3},{3,2},{4,5},{5,4},{6,7},{7,6},{8,9},{9,8},{10,11... | collective-permute-start | bytes 983048 | tf_op jit(solution)/shard_map/ppermute | solution.py:45
  146.4 0.7 copy-start.9
  151.9 1.1 copy-start.1
  153.0 22.3 %copy-start.12 = (s32[160]{0:T(256)S(1)}, s32[160]{0:T(256)}, u32[]{:S(2)}) copy-start(s32[160]{0:T(256)} %param.16) | copy-start | bytes 1924
  173.2 4.6 %copy-start.3 = (f32[64,2,1024]{2,0,1:T(8,128)S(1)}, f32[64,2,1024]{2,0,1:T(8,128)}, u32[]{:S(2)}) copy-start(f32[64,2,1024]{2,0,1:T(8,128)} %get-tuple-element.86) | copy-start | bytes 1572868
  173.2 5.8 %copy-start.2 = (f32[64,2,1024]{2,0,1:T(8,128)S(1)}, f32[64,2,1024]{2,0,1:T(8,128)}, u32[]{:S(2)}) copy-start(f32[64,2,1024]{2,0,1:T(8,128)} %get-tuple-element.87) | copy-start | bytes 1572868
  173.2 22.0 %collective-permute-start.10 = (bf16[320,1408]{1,0:T(8,128)(2,1)S(1)}, bf16[320,1408]{1,0:T(8,128)(2,1)S(1)}, u32[]{:S(2)}, u32[]{:S(2)}) collective-permute-start(bf16[320,1408]{1,0:T(8,128)(2,1)S(1)} %get-tuple-element.51), channel_id=1, source_target_pairs={{0,64},{1,65},{2,66},{3,67},{4,68},{5,69},{6,70},{7,71},{8,72},{9,... | collective-permute-start | bytes 2703368 | tf_op jit(solution)/shard_map/ppermute | solution.py:45
  177.7 2.4 %copy-start.13 = (bf16[1024]{0:T(1024)(128)(2,1)S(1)}, bf16[1024]{0:T(1024)(128)(2,1)}, u32[]{:S(2)}) copy-start(bf16[1024]{0:T(1024)(128)(2,1)} %param.18) | copy-start | bytes 6148
  177.7 2.4 %copy-start.14 = (bf16[2,128]{1,0:T(2,128)(2,1)S(1)}, bf16[2,128]{1,0:T(2,128)(2,1)}, u32[]{:S(2)}) copy-start(bf16[2,128]{1,0:T(2,128)(2,1)} %param.19) | copy-start | bytes 1540
  184.3 11.0 %copy-start.4 = (f32[320,1408]{1,0:T(8,128)S(1)}, f32[320,1408]{1,0:T(8,128)}, u32[]{:S(2)}) copy-start(f32[320,1408]{1,0:T(8,128)} %get-tuple-element.50) | copy-start | bytes 5406724
  197.8 0.9 copy-start.6
  197.8 1.0 copy-start.7
  198.8 0.7 copy-start.10
  199.5 10.7 %slice-start = ((s8[5242880]{0:T(1024)(128)(4,1)}), s8[1048576]{0:T(1024)(128)(4,1)S(1)}, s32[]{:S(2)}) async-start(s8[5242880]{0:T(1024)(128)(4,1)} %bitcast.182), calls=%async_computation.4 | async-start | bytes 2097152
  204.7 5.5 %slice-start.1 = ((s8[5242880]{0:T(1024)(128)(4,1)}), s8[4194304]{0:T(1024)(128)(4,1)S(1)}, s32[]{:S(2)}) async-start(s8[5242880]{0:T(1024)(128)(4,1)} %bitcast.182), calls=%async_computation.5 | async-start | bytes 8388608
Sparse Core Ops, SparseCore 0:
  42.6 87.7 all-gather.2

commit v2 on v1

v2 whole, which is shorter than its diff:
```python
import functools
import functools
import math

import jax
import jax.numpy as jnp
from jax import lax
from jax.experimental import pallas as pl
from jax.experimental.pallas import tpu as pltpu
from jax.sharding import Mesh
from jax.sharding import PartitionSpec as P

D = 8192
HEAD = 128
ADAM_STEP = 10

NAMES = ("xh", "z", "c", "y", "xl")
SIZES = (2, 4, 2, 4, 2)
FSDP = ("xh", "z", "c")
TP = ("y", "xl")
OWNERS = 16
PAIRS = 8
ROWS = 160
TOKENS = 4 * ROWS
HALF = 512
SLOTS = 64
PART = 512
FIRST = 768


def pairs_of(move):
    found = []
    total = math.prod(SIZES)
    for index in range(total):
        rest, coords = index, []
        for size in reversed(SIZES):
            coords.append(rest % size)
            rest //= size
        target = 0
        for value, size in zip(move(*reversed(coords)), SIZES):
            target = target * size + value
        found.append((index, target))
    return found


def send(array, move):
    return lax.ppermute(array, NAMES, pairs_of(move))


def along_y(step):
    return lambda xh, z, c, y, xl: (xh, z, c, (y + step) % 4, xl)


def other_xl(xh, z, c, y, xl):
    return (xh, z, c, y, 1 - xl)


def other_xh(xh, z, c, y, xl):
    return (1 - xh, z, c, y, xl)


def swap_xh_core(xh, z, c, y, xl):
    return (c, z, xh, y, xl)


def adamw_update(master, moment1, moment2, gradient):
    gradient = gradient.astype(jnp.float32)
    moment1_new = 0.9 * moment1 + 0.1 * gradient
    moment2_new = 0.95 * moment2 + 0.05 * gradient * gradient
    first_fix = 1.0 - 0.9**ADAM_STEP
    second_fix = 1.0 - 0.95**ADAM_STEP
    update = moment1_new / first_fix / (jnp.sqrt(moment2_new / second_fix) + 1e-08)
    master_new = master - 0.01 * (update + 0.1 * master)
    return (master_new, moment1_new, moment2_new)


def rotation(positions):
    half = HEAD // 2
    freqs = jnp.exp(jnp.arange(half, dtype=jnp.float32) * (-math.log(1000000.0) / half))
    angles = positions[:, :, None].astype(jnp.float32) * freqs
    cosine, sine = jnp.cos(angles), jnp.sin(angles)
    return jnp.concatenate([cosine, cosine], axis=-1), jnp.concatenate([-sine, sine], axis=-1)


def pack_kernel(query_ref, key_ref, value_ref, first_ref, second_ref):
    for member in range(8):
        start = member * 1024
        own = slice(member * 128, member * 128 + 128)
        first_ref[member, :, 0:PART] = query_ref[:, start : start + PART]
        first_ref[member, :, PART : PART + 128] = key_ref[:, own]
        first_ref[member, :, PART + 128 : FIRST] = value_ref[:, own]
        second_ref[member] = query_ref[:, start + PART : start + 1024]


def pack_columns(q_weight, keys, values):
    rows = q_weight.shape[0]
    whole = pl.BlockSpec(memory_space=pltpu.VMEM)
    return pl.pallas_call(
        pack_kernel,
        in_specs=[whole] * 3,
        out_specs=[whole] * 2,
        out_shape=[
            jax.ShapeDtypeStruct((8, rows, FIRST), jnp.bfloat16),
            jax.ShapeDtypeStruct((8, rows, PART), jnp.bfloat16),
        ],
        compiler_params=pltpu.CompilerParams(vmem_limit_bytes=16 << 20),
        cost_estimate=pl.CostEstimate(flops=0, bytes_accessed=3 << 20, transcendentals=0),
    )(q_weight, keys, values)


def project_kernel(place_ref, *refs):
    blocks, w_ref, mine_ref, other_ref, tokens_ref, held, total, sems = refs[:10], *refs[10:17]
    half = TOKENS // 2
    width = w_ref.shape[1]
    columns = mine_ref.shape[1] - 128
    keep = pltpu.make_async_copy(held, tokens_ref, sems.at[10])
    step = pl.program_id(0)

    @pl.when(step == 0)
    def _():
        copies = []
        for index in range(10):
            member = index if index < 6 else 6 + (index - 6) // 2
            features = pl.ds(pl.multiple_of(place_ref[member] * HALF, HALF), HALF)
            if index < 6:
                target = held.at[:, features]
            else:
                target = held.at[pl.ds((index - 6) % 2 * half, half), features]
            copies.append(pltpu.make_async_copy(blocks[index], target, sems.at[index]))
        for copy in copies:
            copy.start()
        for copy in copies:
            copy.wait()
        keep.start()

    xh = place_ref[8]
    own = pl.ds(pl.multiple_of(xh * half, half), half)
    partner = pl.ds(pl.multiple_of((1 - xh) * half, half), half)
    tile = pl.ds(pl.multiple_of(step * width, width), width)
    total[...] = jnp.dot(held[...], w_ref[...], preferred_element_type=jnp.float32)
    other_ref[:, tile] = total[partner, :].astype(jnp.bfloat16)
    mine_ref[:, tile] = total[own, :]

    @pl.when(step == 0)
    def _():
        def sums(rows):
            parts = jnp.zeros((half, 128), jnp.float32)
            for start in range(0, 8 * HALF, 128):
                part = held[rows, start : start + 128].astype(jnp.float32)
                parts += part * part
            return jnp.sum(parts, axis=1, keepdims=True)

        mine_ref[:, columns:] = jnp.broadcast_to(sums(own), (half, 128))
        partner_sums = sums(partner)
        high = partner_sums.astype(jnp.bfloat16).astype(jnp.float32)
        lanes = lax.broadcasted_iota(jnp.int32, (half, 128), 1)
        other_ref[:, columns:] = jnp.where(lanes < 64, high, partner_sums - high).astype(
            jnp.bfloat16
        )

    @pl.when(step == pl.num_programs(0) - 1)
    def _():
        keep.wait()


def project(place, blocks, weights):
    half = TOKENS // 2
    columns = weights.shape[1]
    width = columns + 128
    anywhere = pl.BlockSpec(memory_space=pltpu.HBM)
    return pl.pallas_call(
        project_kernel,
        grid_spec=pltpu.PrefetchScalarGridSpec(
            num_scalar_prefetch=1,
            grid=(columns // 256,),
            in_specs=[anywhere] * 10 + [pl.BlockSpec((8 * HALF, 256), lambda n, place: (0, n))],
            out_specs=[
                pl.BlockSpec((half, width), lambda n, place: (0, 0)),
                pl.BlockSpec((half, width), lambda n, place: (0, 0)),
                anywhere,
            ],
            scratch_shapes=[
                pltpu.VMEM((TOKENS, 8 * HALF), jnp.bfloat16),
                pltpu.VMEM((TOKENS, 256), jnp.float32),
                pltpu.SemaphoreType.DMA((11,)),
            ],
        ),
        out_shape=[
            jax.ShapeDtypeStruct((half, width), jnp.float32),
            jax.ShapeDtypeStruct((half, width), jnp.bfloat16),
            jax.ShapeDtypeStruct((TOKENS, 8 * HALF), jnp.bfloat16),
        ],
        compiler_params=pltpu.CompilerParams(vmem_limit_bytes=60 << 20),
        cost_estimate=pl.CostEstimate(
            flops=2 * TOKENS * 4096 * columns, bytes_accessed=12 << 20, transcendentals=0
        ),
    )(place, *blocks, weights)


def hold_kernel(keys, values, keys_out, values_out, sems):
    copies = []
    for index in range(5):
        rows = pl.ds(index * 32, 32)
        copies.append(pltpu.make_async_copy(keys.at[rows], keys_out.at[rows], sems.at[index]))
        copies.append(
            pltpu.make_async_copy(values.at[rows], values_out.at[rows], sems.at[5 + index])
        )
    for copy in copies:
        copy.start()
    for copy in copies:
        copy.wait()


def hold(k_cache, v_cache):
    far = pl.BlockSpec(memory_space=pltpu.HBM)
    near = pl.BlockSpec(memory_space=pltpu.VMEM)
    return pl.pallas_call(
        hold_kernel,
        in_specs=[far, far],
        out_specs=[near, near],
        out_shape=[jax.ShapeDtypeStruct(k_cache.shape, k_cache.dtype)] * 2,
        scratch_shapes=[pltpu.SemaphoreType.DMA((10,))],
        compiler_params=pltpu.CompilerParams(vmem_limit_bytes=12 << 20),
        cost_estimate=pl.CostEstimate(flops=0, bytes_accessed=20 << 20, transcendentals=0),
    )(k_cache, v_cache)


BLOCK = 32


def spread(scratch, array):
    for index in range(8):
        scratch[pl.ds(index, BLOCK, stride=8), :] = array
    return scratch[...].reshape(BLOCK, 8, HEAD)


def attend_kernel(first, *refs):
    if first:
        mine, came, bias, cosine, sine, mask, k_ref, v_ref = refs[:8]
        out, keys_out, values_out, scale_out = refs[8:12]
        work = refs[12]
        spare = refs[13:]
    else:
        mine, came, bias, cosine, sine, mask, k_ref, v_ref = refs[:8]
        keys_in, values_in, scale_in = refs[8:11]
        out = refs[12]
        work = refs[13]
        spare = refs[14:]

    def rotated(field, step):
        return field * cosine[step] + pltpu.roll(field, HEAD // 2, 1) * sine[step]

    def raw(step, start, scale):
        features = slice(start, start + HEAD)
        total = mine[step, :, features] + came[step, :, features].astype(jnp.float32)
        return total * scale + bias[:, features]

    new_keys, new_values = [], []
    for step in range(2):
        if first:
            part = came[step, :, FIRST : FIRST + 128].astype(jnp.float32)
            sums = mine[step, :, FIRST : FIRST + 128] + part + pltpu.roll(part, 64, 1)
            scale = lax.rsqrt(sums / D + 1e-06) / math.sqrt(D)
            scale_out[step] = scale
            key = rotated(raw(step, PART, scale), step).astype(jnp.bfloat16)
            value = raw(step, PART + HEAD, scale).astype(jnp.bfloat16)
            keys_out[step] = key
            values_out[step] = value
        else:
            scale = scale_in[step]
            key, value = keys_in[step], values_in[step]
        new_keys.append(key.astype(jnp.float32))
        new_values.append(value.astype(jnp.float32))
        for head in range(4):
            query = rotated(raw(step, head * HEAD, scale), step)
            work[pl.ds(step * 4 + head, BLOCK, stride=8), :] = query
    queries = work[...].reshape(BLOCK, 8, HEAD).astype(jnp.bfloat16)
    wide = queries.astype(jnp.float32)
    root = 1.0 / math.sqrt(HEAD)
    near = pl.ds(pl.multiple_of(pl.program_id(0) * BLOCK, BLOCK), BLOCK)
    scores = (
        lax.dot_general(
            queries, k_ref[near], (((2,), (2,)), ((0,), (0,))), preferred_element_type=jnp.float32
        )
        * root
        + mask[...]
    )
    second = lax.broadcasted_iota(jnp.int32, (BLOCK, 8, 1), 1) >= 4
    own = [
        jnp.sum(wide * spread(spare[u], new_keys[u]), axis=2, keepdims=True) * root
        for u in range(2)
    ]
    own[1] = jnp.where(second, own[1], -1e30)
    peak = jnp.maximum(
        jnp.max(scores, axis=2, keepdims=True), jnp.maximum(own[0], own[1])
    )
    shares = jnp.exp(scores - peak)
    own = [jnp.exp(score - peak) for score in own]
    total = jnp.sum(shares, axis=2, keepdims=True) + own[0] + own[1]
    inverse = 1.0 / total
    weights = (shares * inverse).astype(jnp.bfloat16)
    context = lax.dot_general(
        weights, v_ref[near], (((2,), (1,)), ((0,), (0,))), preferred_element_type=jnp.float32
    )
    for u in range(2):
        weight = (own[u] * inverse).astype(jnp.bfloat16).astype(jnp.float32)
        context += weight * spread(spare[2 + u], new_values[u])
    work[...] = context.reshape(BLOCK * 8, HEAD)
    for step in range(2):
        for head in range(4):
            result = work[pl.ds(step * 4 + head, BLOCK, stride=8), :]
            out[step, :, head * HEAD : (head + 1) * HEAD] = result.astype(jnp.bfloat16)


def attend(first, mine, came, bias, cosine, sine, mask, k_cache, v_cache, *more):
    width = mine.shape[-1]

    def steps(columns):
        return pl.BlockSpec((2, BLOCK, columns), lambda i: (0, i, 0))

    def rows(a, b):
        return pl.BlockSpec((BLOCK, a, b), lambda i: (i, 0, 0))

    in_specs = [
        steps(width),
        steps(width),
        pl.BlockSpec((1, bias.shape[-1]), lambda i: (0, 0)),
        steps(HEAD),
        steps(HEAD),
        rows(8, HEAD),
        pl.BlockSpec(memory_space=pltpu.VMEM),
        pl.BlockSpec(memory_space=pltpu.VMEM),
    ]
    context = jax.ShapeDtypeStruct((2, ROWS, 2 * PART), jnp.bfloat16)
    if first:
        out_specs = [steps(PART), steps(HEAD), steps(HEAD), steps(HEAD)]
        out_shape = [
            context,
            jax.ShapeDtypeStruct((2, ROWS, HEAD), jnp.bfloat16),
            jax.ShapeDtypeStruct((2, ROWS, HEAD), jnp.bfloat16),
            jax.ShapeDtypeStruct((2, ROWS, HEAD), jnp.float32),
        ]
        aliases = {}
    else:
        in_specs += [steps(HEAD), steps(HEAD), steps(HEAD), pl.BlockSpec(memory_space=pl.ANY)]
        out_specs = pl.BlockSpec((2, BLOCK, PART), lambda i: (0, i, 1))
        out_shape = context
        aliases = {11: 0}
    return pl.pallas_call(
        functools.partial(attend_kernel, first),
        grid=(ROWS // BLOCK,),
        in_specs=in_specs,
        out_specs=out_specs,
        out_shape=out_shape,
        scratch_shapes=[pltpu.VMEM((BLOCK * 8, HEAD), jnp.float32)] * 5,
        input_output_aliases=aliases,
        compiler_params=pltpu.CompilerParams(vmem_limit_bytes=24 << 20),
        cost_estimate=pl.CostEstimate(
            flops=4 * ROWS * 8 * 128 * 128, bytes_accessed=12 << 20, transcendentals=ROWS * 1024
        ),
    )(mine, came, bias, cosine, sine, mask, k_cache, v_cache, *more)


def per_device(
    token_ids,
    embedding,
    cache_lengths,
    q_weight,
    q_bias,
    kv_bias,
    kv_master,
    kv_moment1,
    kv_moment2,
    kv_grad,
    k_cache,
    v_cache,
):
    xh, z, c = (lax.axis_index(name) for name in FSDP)
    y, xl = (lax.axis_index(name) for name in TP)
    fsdp_index = (xh * 4 + z) * 2 + c
    pair = z * 2 + c
    vocab_rows = embedding.shape[0]

    queries = send(q_weight, swap_xh_core)
    master_new, moment1_new, moment2_new = adamw_update(kv_master, kv_moment1, kv_moment2, kv_grad)
    rollout = master_new.astype(jnp.bfloat16)
    rollout = jnp.concatenate([rollout[:, 0, :], rollout[:, 1, :]], axis=1)
    rollout = send(rollout, swap_xh_core)

    paired = token_ids.reshape(2, 2, PAIRS, ROWS).transpose(2, 1, 0, 3).reshape(PAIRS, TOKENS)
    owners = paired // vocab_rows
    order = jnp.arange(TOKENS, dtype=jnp.int32)
    earlier = order[:, None] < order[None, :]
    same_id = paired[:, :, None] == paired[:, None, :]
    first = ~jnp.any(same_id & earlier[None], axis=1)
    first_owner = jnp.where(first, owners, -1)
    ranks = jnp.sum(
        ((first_owner[:, :, None] == owners[:, None, :]) & earlier[None]).astype(jnp.int32), axis=1
    )
    rounds = (jnp.max(jnp.where(first, ranks, 0)) + SLOTS) // SLOTS

    local = paired - fsdp_index * vocab_rows
    sent_rank = jnp.where(first_owner == fsdp_index, ranks, -1)
    own_ids = lax.dynamic_index_in_dim(paired, pair, 0, keepdims=False)
    own_first = lax.dynamic_index_in_dim(first, pair, 0, keepdims=False)
    own_ranks = lax.dynamic_index_in_dim(ranks, pair, 0, keepdims=False)
    own_owners = lax.dynamic_index_in_dim(owners, pair, 0, keepdims=False)
    got_rank = jnp.sum(
        jnp.where(
            (own_ids[:, None] == own_ids[None, :]) & own_first[:, None], own_ranks[:, None], 0
        ),
        axis=0,
    )

    def wanted_rows(turn):
        slots = turn * SLOTS + jnp.arange(SLOTS, dtype=jnp.int32)
        wanted = jnp.sum(
            jnp.where(sent_rank[:, :, None] == slots[None, None, :], local[:, :, None], 0), axis=1
        )
        wanted = lax.optimization_barrier(wanted)
        rows = embedding.at[wanted.reshape(-1)].get(mode="promise_in_bounds")
        rows = rows.reshape(PAIRS, SLOTS, 2, HALF).transpose(2, 0, 1, 3)
        return rows.reshape(OWNERS, SLOTS, HALF)

    def exchanged(rows):
        return lax.all_to_all(rows, FSDP, split_axis=0, concat_axis=0)

    def placed_rows(turn, rows):
        slot = got_rank - turn * SLOTS
        inside = (slot >= 0) & (slot < SLOTS)
        spot = jnp.where(inside, own_owners * SLOTS + slot, -1)
        pick = spot[:, None] == jnp.arange(OWNERS * SLOTS, dtype=jnp.int32)[None, :]
        return jnp.dot(
            pick.astype(jnp.bfloat16),
            rows.reshape(OWNERS * SLOTS, HALF),
            preferred_element_type=jnp.float32,
        ).astype(jnp.bfloat16)

    rows = exchanged(wanted_rows(0))
    queries, rollout, rows = lax.optimization_barrier((queries, rollout, rows))
    packed = pack_columns(queries, rollout[:, :1024], rollout[:, 1024:])
    own = placed_rows(0, rows)
    weights = []
    for part in packed:
        part = lax.all_to_all(part, TP, split_axis=0, concat_axis=0)
        part = lax.all_gather(part.reshape(HALF, part.shape[-1]), ("z", "c"))
        weights.append(part.reshape(8 * HALF, part.shape[-1]))
    _, own = lax.while_loop(
        lambda state: state[0] < rounds,
        lambda state: (state[0] + 1, state[1] + placed_rows(state[0], exchanged(wanted_rows(state[0])))),
        (jnp.int32(1), own),
    )

    half = TOKENS // 2
    across = send(own, other_xl)
    below = send(own, along_y(1))
    above = send(own, along_y(-1))
    far_low = send(below[:half], along_y(1))
    far_high = send(above[half:], along_y(-1))
    below_across = send(across, along_y(1))
    above_across = send(across, along_y(-1))
    far_low_across = send(far_low, other_xl)
    far_high_across = send(far_high, other_xl)
    members = [
        y * 2 + xl,
        y * 2 + 1 - xl,
        (y + 3) % 4 * 2 + xl,
        (y + 1) % 4 * 2 + xl,
        (y + 3) % 4 * 2 + 1 - xl,
        (y + 1) % 4 * 2 + 1 - xl,
        (y + 2) % 4 * 2 + xl,
        (y + 2) % 4 * 2 + 1 - xl,
    ]
    place = jnp.stack([member % 4 * 2 + member // 4 for member in members] + [xh]).astype(jnp.int32)
    blocks = (
        own,
        across,
        below,
        above,
        below_across,
        above_across,
        far_low,
        far_high,
        far_low_across,
        far_high_across,
    )
    mine_first, other_first, tokens = project(place, blocks, weights[0])
    came_first = send(other_first, other_xh)
    k_cache, v_cache, _ = lax.optimization_barrier((k_cache, v_cache, other_first))
    k_cache, v_cache = hold(k_cache, v_cache)
    total_second = jnp.dot(tokens, weights[1], preferred_element_type=jnp.float32)
    mine_second = lax.dynamic_slice_in_dim(total_second, xh * half, half, 0)
    other_second = lax.dynamic_slice_in_dim(total_second, (1 - xh) * half, half, 0)
    came_second = send(other_second.astype(jnp.bfloat16), other_xh)

    cosine, sine = rotation(cache_lengths[None, :] + jnp.arange(2, dtype=jnp.int32)[:, None])
    inside = jnp.arange(HEAD, dtype=jnp.int32)[None, :] < cache_lengths[:, None]
    mask = jnp.where(inside, 0.0, -1e30).astype(jnp.float32)
    mask = jnp.broadcast_to(mask[:, None, :], (ROWS, 8, HEAD))
    wide = q_bias.astype(jnp.float32)
    bias_first = jnp.concatenate([wide[:PART], kv_bias.reshape(256).astype(jnp.float32)])

    def stepwise(array):
        return array.reshape(2, ROWS, array.shape[-1])

    context, keys, values, scale = attend(
        True,
        stepwise(mine_first),
        stepwise(came_first),
        bias_first[None],
        cosine,
        sine,
        mask,
        k_cache,
        v_cache,
    )
    context = attend(
        False,
        stepwise(mine_second),
        stepwise(came_second),
        wide[None, PART:],
        cosine,
        sine,
        mask,
        k_cache,
        v_cache,
        keys,
        values,
        scale,
        context,
    )
    return (context, master_new, moment1_new, moment2_new)


def solution(mesh):
    parts = Mesh(mesh.devices.reshape(SIZES), NAMES)
    placed = (
        P(),
        P(FSDP, TP),
        P(FSDP),
        P(NAMES, None),
        P(TP),
        P(None, TP),
        P(NAMES, None, None),
        P(NAMES, None, None),
        P(NAMES, None, None),
        P(NAMES, None, None),
        P(FSDP, None, TP),
        P(FSDP, None, TP),
    )
    return jax.shard_map(
        per_device,
        mesh=parts,
        in_specs=placed,
        out_specs=(
            P(None, FSDP, TP),
            P(NAMES, None, None),
            P(NAMES, None, None),
            P(NAMES, None, None),
        ),
        check_vma=False,
    )
```

time: 223 us -> 181 us (0.81)
  waiting for transfers between devices: 62.1 us -> 42.4 us
  starting transfers between devices: 38.7 us -> 26.3 us
  other arithmetic: 20.2 us -> 10.7 us
  blocking collectives: 24.1 us -> 29.6 us
  matrix products: 12.2 us -> 7.91 us
    all_to_all x1, starting transfers between devices: 27.8 us -> 7.77 us  [exchanged(): return lax.all_to_all(rows, FSDP, split_axis=0, concat_axis=0)]
    ppermute x11 -> x13, waiting for transfers between devices: 44.2 us -> 30.9 us  [send(): return lax.ppermute(array, NAMES, pairs_of(move))]
    pallas_call x1 -> x4, Pallas kernels: 5.32 us -> 14.2 us  [the longest x2 13.2 us: attend(): pl.pallas_call(functools.partial(attend_kernel, first), grid=(ROWS // BLO...]
    pallas_call x1, Pallas kernels: 20.1 us -> 12.1 us  [project(): pl.pallas_call(project_kernel, grid_spec=pltpu.PrefetchScalarGridSpec(num...]
    all_to_all x1, waiting for transfers between devices: 17.8 us -> 10.2 us  [exchanged(): return lax.all_to_all(rows, FSDP, split_axis=0, concat_axis=0)]
    ppermute x11 -> x13, starting transfers between devices: 10.9 us -> 18.5 us  [send(): return lax.ppermute(array, NAMES, pairs_of(move))]
    all_to_all x1 -> x2, blocking collectives: 24.1 us -> 29.6 us  [per_device(): part = lax.all_to_all(part, TP, split_axis=0, concat_axis=0)]
    dot_general x5 -> x2, matrix products: 12.2 us -> 7.91 us  [the longest x1 6.18 us: per_device(): jnp.dot(tokens, weights[1], preferred_element_type=jnp.float32)]
  transfers between devices with their start and end apart: 13 -> 16, of which waited for: 7 -> 6; matrix products, arithmetic and copies ran while one was open for 14% -> 20% of each run, Pallas kernels for 0% -> 11%
where the time goes in v2:
time: 181 us; the launch traced here: 178 us
  waiting for transfers between devices  42.4 us (23%)
  blocking collectives  29.6 us (16%)
  starting transfers between devices  26.3 us (15%)
  Pallas kernels  26.3 us (15%)
  local copies, waits for them, and re-layouts  19.7 us (11%)
  between operations  15.1 us (8%)
  other arithmetic  10.7 us (6%)
  matrix products  7.91 us (4%)
    ppermute x13, waiting for transfers between devices, send(): return lax.ppermute(array, NAMES, pairs_of(move))  30.9 us
    all_to_all x2, blocking collectives, per_device(): part = lax.all_to_all(part, TP, split_axis=0, concat_axis=0)  29.6 us
    ppermute x13, starting transfers between devices, send(): return lax.ppermute(array, NAMES, pairs_of(move))  18.5 us
    pallas_call x2, Pallas kernels, attend(): pl.pallas_call(functools.partial(attend_kernel, first), grid=(ROWS // BLO...  13.2 us
    pallas_call x1, Pallas kernels, project(): pl.pallas_call(project_kernel, grid_spec=pltpu.PrefetchScalarGridSpec(num...  12.1 us
    all_to_all x1, waiting for transfers between devices, exchanged(): return lax.all_to_all(rows, FSDP, split_axis=0, concat_axis=0)  10.2 us
    unnamed x41, local copies, waits for them, and re-layouts  8.06 us
    all_to_all x1, starting transfers between devices, exchanged(): return lax.all_to_all(rows, FSDP, split_axis=0, concat_axis=0)  7.77 us
  transfers between devices with their start and end apart: 16, of which 6 were waited for; matrix products, arithmetic and copies ran while one was open for 20% of the time, Pallas kernels for 11%

profile of v2, /device:TPU:64, one launch (start us, length us, event | category | flops | bytes accessed | tf_op | source)
XLA Modules:
  0.0 178.1 jit_solution(8548973262674795759)
XLA Ops:
  7.2 1.9 %collective-permute-start = (bf16[64,8192]{1,0:T(8,128)(2,1)}, bf16[64,8192]{1,0:T(8,128)(2,1)S(1)}, u32[]{:S(2)}, u32[]{:S(2)}) collective-permute-start(bf16[64,8192]{1,0:T(8,128)(2,1)} %param.17), channel_id=1, source_target_pairs={{0,0},{1,1},{2,2},{3,3},{4,4},{5,5},{6,6},{7,7},{8,64},{9,65},{10,... | collective-permute-start | bytes 3145736 | tf_op jit(solution)/shard_map/ppermute | solution.py:47
  9.0 0.1 iota_compare_fusion.8
  9.2 0.8 reshape.264
  10.0 0.1 reshape.265
  10.1 2.7 %and_reduce_fusion = pred[8,640]{1,0:T(8,128)(4,1)S(1)} fusion(s32[8,640]{1,0:T(8,128)S(1)} %reshape.265, pred[640,640]{1,0:T(8,128)(4,1)S(1)} %iota_compare_fusion.8), kind=kLoop, calls=%fused_computation.13 | loop fusion | flops 9825280 | bytes 435200 | tf_op jit(solution)/shard_map/reduce_or | solution.py:395
  12.8 2.7 %convert_reduce_fusion = s32[8,640]{1,0:T(8,128)S(1)} fusion(s32[8,640]{1,0:T(8,128)S(1)} %get-tuple-element.123, s32[8,640]{1,0:T(8,128)S(1)} %get-tuple-element.122, pred[640,640]{1,0:T(8,128)(4,1)S(1)} %iota_compare_fusion.8), kind=kLoop, calls=%fused_computation.12 | loop fusion | flops 13102080 | bytes 471040 | tf_op jit(solution)/shard_map/reduce_sum | solution.py:397
  15.5 0.6 select_reduce_fusion.3
  16.2 0.2 select_reduce_fusion.2
  16.4 0.1 reshape.266
  16.5 7.7 %gather_fusion.1 = bf16[512,1024]{1,0:T(8,128)(2,1)S(1)} fusion(bf16[4752,1024]{1,0:T(8,128)(2,1)} %param.15, s32[1024]{0:T(1024)S(1)} %pad_clamp_fusion.1), kind=kCustom, calls=%fused_computation.1 | custom fusion | bytes 2099200 | tf_op jit(solution)/shard_map/gather | solution.py:421
  24.2 0.8 reshape.267
  25.0 0.0 copy-start.3
  25.1 1.2 copy.55
  26.2 7.8 %all-to-all-start.1 = ((bf16[16,64,512]{2,1,0:T(8,128)(2,1)}), bf16[16,64,512]{2,1,0:T(8,128)(2,1)S(1)}, u32[]{:S(2)}, u32[]{:S(2)}) async-start(bf16[16,64,512]{2,1,0:T(8,128)(2,1)} %bitcast.18), calls=%async_computation.1 | async-start | bytes 2097152 | tf_op jit(solution)/shard_map/all_to_all | solution.py:426
  34.0 0.0 all-gather.3.cloned.1.call-start
  34.1 2.9 %fusion.13 = (bf16[64,2,1024]{2,0,1:T(8,128)(2,1)S(1)}, f32[64,2,1024]{2,0,1:T(8,128)}, f32[64,2,1024]{2,0,1:T(8,128)S(1)}, f32[64,2,1024]{2,0,1:T(8,128)S(1)}) fusion(f32[64,2,1024]{2,1,0:T(2,128)} %param.20, bf16[64,2,1024]{2,1,0:T(2,128)(2,1)S(1)} %copy-done.3, f32[64,2,1024]{2,1,0:T(2,128)} %param.21, f32[64,2,1024]{2,1,0:T(2,128)} %param.22), kind=kLoop, calls=%fused_computation.62 | loop fusion | flops 2228224 | bytes 3670016 | tf_op jit(solution)/shard_map/convert_element_type | solution.py:386
  37.1 0.7 collective-permute-start.1
  37.7 0.0 collective-permute-done.1
  37.8 10.2 %all-to-all-done.1 = bf16[16,64,512]{2,1,0:T(8,128)(2,1)S(1)} async-done(((bf16[16,64,512]{2,1,0:T(8,128)(2,1)}), bf16[16,64,512]{2,1,0:T(8,128)(2,1)S(1)}, u32[]{:S(2)}, u32[]{:S(2)}) %all-to-all-start.1) | async-done | bytes 1048608 | tf_op jit(solution)/shard_map/all_to_all | solution.py:426
  48.0 0.9 copy-done.1
  49.0 0.1 shard_map.147
  49.1 16.7 %all_to_all.21 = bf16[8,64,768]{2,1,0:T(8,128)(2,1)} all-to-all(bf16[8,64,768]{2,1,0:T(8,128)(2,1)S(1)} %get-tuple-element.67), channel_id=1, replica_groups=mesh['xh'=2,'z'=4,'c'=2,'y'=4,'xl'=2] {'y','xl'}, dimensions={0} | all-to-all | bytes 1572864 | tf_op jit(solution)/shard_map/all_to_all | solution.py:445
  65.8 0.0 all-gather.3.cloned.1.call-update
  65.8 0.0 all-gather.5.cloned.1.call-start
  65.8 12.9 %all_to_all.22 = bf16[8,64,512]{2,1,0:T(8,128)(2,1)} all-to-all(bf16[8,64,512]{2,1,0:T(8,128)(2,1)S(1)} %get-tuple-element.69), channel_id=1, replica_groups=mesh['xh'=2,'z'=4,'c'=2,'y'=4,'xl'=2] {'y','xl'}, dimensions={0} | all-to-all | bytes 1048576 | tf_op jit(solution)/shard_map/all_to_all | solution.py:445
  78.8 0.0 all-gather.5.cloned.1.call-update
  79.6 0.4 select_reduce_fusion.1
  80.0 1.7 fusion.5
  81.8 0.1 collective-permute-start.3
  81.8 3.2 %collective-permute-start.4 = (bf16[640,512]{1,0:T(8,128)(2,1)}, bf16[640,512]{1,0:T(8,128)(2,1)S(1)}, u32[]{:S(2)}, u32[]{:S(2)}) collective-permute-start(bf16[640,512]{1,0:T(8,128)(2,1)} %get-tuple-element.64.refs_0_), channel_id=1, source_target_pairs={{0,6},{1,7},{2,0},{3,1},{4,2},{5,3},{6,4},{7,5},{8,14},{9,15},{10,... | collective-permute-start | bytes 1966088 | tf_op jit(solution)/shard_map/ppermute | solution.py:47
  85.1 0.8 collective-permute-start.2
  85.9 2.2 %copy.56 = f32[64,2,1024]{2,1,0:T(2,128)} copy(f32[64,2,1024]{2,0,1:T(8,128)} %get-tuple-element.113) | data formatting | bytes 1048576
  88.1 1.2 copy.57
  89.3 1.2 copy.58
  90.5 0.6 stack.39.place_ref
  91.1 9.3 %collective-permute-done.3.refs_2_ = bf16[640,512]{1,0:T(8,128)(2,1)S(1)} collective-permute-done((bf16[640,512]{1,0:T(8,128)(2,1)}, bf16[640,512]{1,0:T(8,128)(2,1)S(1)}, u32[]{:S(2)}, u32[]{:S(2)}) %collective-permute-start.3) | collective-permute-done | bytes 655392 | tf_op jit(solution)/shard_map/ppermute | solution.py:47
  100.5 0.1 collective-permute-start.7
  100.5 0.0 collective-permute-done.4.refs_3_
  100.6 3.4 %collective-permute-start.8 = (bf16[320,512]{1,0:T(8,128)(2,1)S(1)}, bf16[320,512]{1,0:T(8,128)(2,1)S(1)}, u32[]{:S(2)}, u32[]{:S(2)}) collective-permute-start(bf16[320,512]{1,0:T(8,128)(2,1)S(1)} %slice.39), channel_id=1, source_target_pairs={{0,6},{1,7},{2,0},{3,1},{4,2},{5,3},{6,4},{7,5},{8,14},{9,15},{10,... | collective-permute-start | bytes 983048 | tf_op jit(solution)/shard_map/ppermute | solution.py:47
  104.0 0.0 collective-permute-start.5
  104.0 3.2 %collective-permute-start.6 = (bf16[640,512]{1,0:T(8,128)(2,1)S(1)}, bf16[640,512]{1,0:T(8,128)(2,1)S(1)}, u32[]{:S(2)}, u32[]{:S(2)}) collective-permute-start(bf16[640,512]{1,0:T(8,128)(2,1)S(1)} %collective-permute-done.2.refs_1_), channel_id=1, source_target_pairs={{0,6},{1,7},{2,0},{3,1},{4,2},{5,3},{6,4},{7,5},{8,14},{9,15},{10,... | collective-permute-start | bytes 1966088 | tf_op jit(solution)/shard_map/ppermute | solution.py:47
  107.2 5.0 %collective-permute-done.7.refs_6_ = bf16[320,512]{1,0:T(8,128)(2,1)S(1)} collective-permute-done((bf16[320,512]{1,0:T(8,128)(2,1)S(1)}, bf16[320,512]{1,0:T(8,128)(2,1)S(1)}, u32[]{:S(2)}, u32[]{:S(2)}) %collective-permute-start.7) | collective-permute-done | bytes 327712 | tf_op jit(solution)/shard_map/ppermute | solution.py:47
  112.3 0.7 collective-permute-start.9
  113.0 0.0 collective-permute-done.8.refs_7_
  113.0 1.4 collective-permute-start.10
  114.3 0.6 fusion.10
  115.0 0.2 pad_maximum_fusion.1
  115.1 10.5 %collective-permute-done.5.refs_4_ = bf16[640,512]{1,0:T(8,128)(2,1)S(1)} collective-permute-done((bf16[640,512]{1,0:T(8,128)(2,1)S(1)}, bf16[640,512]{1,0:T(8,128)(2,1)S(1)}, u32[]{:S(2)}, u32[]{:S(2)}) %collective-permute-start.5) | collective-permute-done | bytes 655392 | tf_op jit(solution)/shard_map/ppermute | solution.py:47
  125.6 0.8 copy-done.9
  126.5 0.0 collective-permute-done.9.refs_8_
  126.5 0.8 copy-done.10
  127.3 0.7 copy-done.13
  128.1 12.1 %shard_map.148 = (f32[320,896]{1,0:T(8,128)}, bf16[320,896]{1,0:T(8,128)(2,1)}, bf16[640,4096]{1,0:T(8,128)(2,1)}) custom-call(s32[9]{0:T(128)} %stack.39.place_ref, bf16[640,512]{1,0:T(8,128)(2,1)} %get-tuple-element.64.refs_0_, bf16[640,512]{1,0:T(8,128)(2,1)} %copy-done.8, bf16[640,512]{1,0:T(8,128)(2,1)} %copy-done.4, bf16[640,512]{1,0:T(8,128)(2,1)} %copy-done.5, ...), custom_call_target="tpu_custom_call" | custom-call | flops 4026531840 | bytes 12582912 | tf_op jit(solution)/shard_map/pallas_call | solution.py:171
  140.2 0.1 collective-permute-start.12
  140.3 1.2 all-gather.5.cloned.1.call-done
  141.6 6.2 %fusion.18 = f32[640,512]{1,0:T(8,128)S(1)} fusion(bf16[640,4096]{1,0:T(8,128)(2,1)} %get-tuple-element.68, bf16[4096,512]{1,0:T(8,128)(2,1)} %bitcast.67), kind=kOutput, calls=%fused_computation.65 | convolution fusion | flops 2684354560 | bytes 10747904 | tf_op jit(solution)/shard_map/dot_general | solution.py:491
  147.7 0.1 dynamic-slice_convert_fusion
  147.8 3.1 %collective-permute-start.11 = (bf16[320,512]{1,0:T(8,128)(2,1)S(1)}, bf16[320,512]{1,0:T(8,128)(2,1)S(1)}, u32[]{:S(2)}, u32[]{:S(2)}) collective-permute-start(bf16[320,512]{1,0:T(8,128)(2,1)S(1)} %dynamic-slice_convert_fusion), channel_id=1, source_target_pairs={{0,64},{1,65},{2,66},{3,67},{4,68},{5,69},{6,70},{7,71},{8,72},{9,... | collective-permute-start | bytes 983048 | tf_op jit(solution)/shard_map/ppermute | solution.py:47
  150.9 0.1 fusion.9
  151.0 0.8 shard_map.149
  151.8 0.1 constant_dynamic-slice_fusion
  151.9 6.1 %collective-permute-done.12 = bf16[320,896]{1,0:T(8,128)(2,1)S(1)} collective-permute-done((bf16[320,896]{1,0:T(8,128)(2,1)}, bf16[320,896]{1,0:T(8,128)(2,1)S(1)}, u32[]{:S(2)}, u32[]{:S(2)}) %collective-permute-start.12) | collective-permute-done | bytes 573472 | tf_op jit(solution)/shard_map/ppermute | solution.py:47
  158.0 7.1 %shard_map.150 = (bf16[2,160,1024]{2,1,0:T(8,128)(2,1)}, bf16[2,160,128]{2,1,0:T(8,128)(2,1)S(1)}, bf16[2,160,128]{2,1,0:T(8,128)(2,1)S(1)}, f32[2,160,128]{2,1,0:T(8,128)S(1)}) custom-call(f32[2,160,896]{2,1,0:T(8,128)S(1)} %bitcast.55, bf16[2,160,896]{2,1,0:T(8,128)(2,1)S(1)} %bitcast.56, f32[1,768]{1,0:T(1,128)S(1)} %broadcast_in_dim.111.refs_2_, ...), custom_call_target="tpu_custom_call" | custom-call | flops 83886080 | bytes 12582912 | tf_op jit(solution)/shard_map/pallas_call | solution.py:349
  165.1 6.1 %shard_map.151 = bf16[2,160,1024]{2,1,0:T(8,128)(2,1)} custom-call(f32[2,160,512]{2,1,0:T(8,128)S(1)} %bitcast.54, bf16[2,160,512]{2,1,0:T(8,128)(2,1)S(1)} %bitcast.57, f32[1,512]{1,0:T(1,128)S(1)} %bitcast.58, f32[2,160,128]{2,1,0:T(8,128)S(1)} %get-tuple-element.132.refs_3_, ...), custom_call_target="tpu_custom_call", output_to_operand_aliasing={{}: (11, {})} | custom-call | flops 83886080 | bytes 12582912 | tf_op jit(solution)/shard_map/pallas_call | solution.py:349
  (62 shorter events, 0.4 us)
Async XLA Ops:
  7.2 40.8 %collective-permute-start = (bf16[64,8192]{1,0:T(8,128)(2,1)}, bf16[64,8192]{1,0:T(8,128)(2,1)S(1)}, u32[]{:S(2)}, u32[]{:S(2)}) collective-permute-start(bf16[64,8192]{1,0:T(8,128)(2,1)} %param.17), channel_id=1, source_target_pairs={{0,0},{1,1},{2,2},{3,3},{4,4},{5,5},{6,6},{7,7},{8,64},{9,65},{10,... | collective-permute-start | bytes 3145736 | tf_op jit(solution)/shard_map/ppermute | solution.py:47
  25.0 9.0 %copy-start.3 = (bf16[64,2,1024]{2,1,0:T(2,128)(2,1)S(1)}, bf16[64,2,1024]{2,1,0:T(2,128)(2,1)}, u32[]{:S(2)}) copy-start(bf16[64,2,1024]{2,1,0:T(2,128)(2,1)} %param.23) | copy-start | bytes 786436
  26.2 21.7 %all-to-all-start.1 = ((bf16[16,64,512]{2,1,0:T(8,128)(2,1)}), bf16[16,64,512]{2,1,0:T(8,128)(2,1)S(1)}, u32[]{:S(2)}, u32[]{:S(2)}) async-start(bf16[16,64,512]{2,1,0:T(8,128)(2,1)} %bitcast.18), calls=%async_computation.1 | async-start | bytes 2097152 | tf_op jit(solution)/shard_map/all_to_all | solution.py:426
  34.0 94.1 %all-gather.3.cloned.1.call-start = ((), (), s32[]{:S(2)}) async-start(), calls=%async_computation.4 | async-start | bytes 7077888 | tf_op jit(solution)/shard_map/all_gather | solution.py:446
  37.1 0.7 collective-permute-start.1
  48.0 1.0 copy-start.1
  49.1 30.9 %copy-start.2 = (bf16[16,64,512]{2,1,0:T(8,128)(2,1)S(1)}, bf16[16,64,512]{2,1,0:T(8,128)(2,1)}, u32[]{:S(2)}) copy-start(bf16[16,64,512]{2,1,0:T(8,128)(2,1)} %copy-done.1) | copy-start | bytes 3145732
  65.8 75.7 %all-gather.5.cloned.1.call-start = ((), (), s32[]{:S(2)}) async-start(), calls=%async_computation.5 | async-start | bytes 4718592 | tf_op jit(solution)/shard_map/all_gather | solution.py:446
  81.7 4.1 %copy-start.14 = (bf16[2,128]{1,0:T(2,128)(2,1)S(1)}, bf16[2,128]{1,0:T(2,128)(2,1)}, u32[]{:S(2)}) copy-start(bf16[2,128]{1,0:T(2,128)(2,1)} %param.19) | copy-start | bytes 1540
  81.7 4.1 %copy-start.6 = (bf16[1024]{0:T(1024)(128)(2,1)S(1)}, bf16[1024]{0:T(1024)(128)(2,1)}, u32[]{:S(2)}) copy-start(bf16[1024]{0:T(1024)(128)(2,1)} %param.18) | copy-start | bytes 6148
  81.7 25.5 %copy-start.7 = (s32[160]{0:T(256)S(1)}, s32[160]{0:T(256)}, u32[]{:S(2)}) copy-start(s32[160]{0:T(256)} %param.16) | copy-start | bytes 1924
  81.8 18.7 %collective-permute-start.3 = (bf16[640,512]{1,0:T(8,128)(2,1)}, bf16[640,512]{1,0:T(8,128)(2,1)S(1)}, u32[]{:S(2)}, u32[]{:S(2)}) collective-permute-start(bf16[640,512]{1,0:T(8,128)(2,1)} %get-tuple-element.64.refs_0_), channel_id=1, source_target_pairs={{0,2},{1,3},{2,4},{3,5},{4,6},{5,7},{6,0},{7,1},{8,10},{9,11},{10,... | collective-permute-start | bytes 1966088 | tf_op jit(solution)/shard_map/ppermute | solution.py:47
  81.8 18.7 %collective-permute-start.4 = (bf16[640,512]{1,0:T(8,128)(2,1)}, bf16[640,512]{1,0:T(8,128)(2,1)S(1)}, u32[]{:S(2)}, u32[]{:S(2)}) collective-permute-start(bf16[640,512]{1,0:T(8,128)(2,1)} %get-tuple-element.64.refs_0_), channel_id=1, source_target_pairs={{0,6},{1,7},{2,0},{3,1},{4,2},{5,3},{6,4},{7,5},{8,14},{9,15},{10,... | collective-permute-start | bytes 1966088 | tf_op jit(solution)/shard_map/ppermute | solution.py:47
  85.1 18.9 %collective-permute-start.2 = (bf16[640,512]{1,0:T(8,128)(2,1)}, bf16[640,512]{1,0:T(8,128)(2,1)S(1)}, u32[]{:S(2)}, u32[]{:S(2)}) collective-permute-start(bf16[640,512]{1,0:T(8,128)(2,1)} %get-tuple-element.64.refs_0_), channel_id=1, source_target_pairs={{0,1},{1,0},{2,3},{3,2},{4,5},{5,4},{6,7},{7,6},{8,9},{9,8},{10,11... | collective-permute-start | bytes 1966088 | tf_op jit(solution)/shard_map/ppermute | solution.py:47
  100.4 27.6 %copy-start.4 = (bf16[640,512]{1,0:T(8,128)(2,1)}, bf16[640,512]{1,0:T(8,128)(2,1)S(1)}, u32[]{:S(2)}) copy-start(bf16[640,512]{1,0:T(8,128)(2,1)S(1)} %collective-permute-done.3.refs_2_) | copy-start | bytes 1966084
  100.5 11.8 %collective-permute-start.7 = (bf16[320,512]{1,0:T(8,128)(2,1)S(1)}, bf16[320,512]{1,0:T(8,128)(2,1)S(1)}, u32[]{:S(2)}, u32[]{:S(2)}) collective-permute-start(bf16[320,512]{1,0:T(8,128)(2,1)S(1)} %slice.38), channel_id=1, source_target_pairs={{0,2},{1,3},{2,4},{3,5},{4,6},{5,7},{6,0},{7,1},{8,10},{9,11},{10,... | collective-permute-start | bytes 983048 | tf_op jit(solution)/shard_map/ppermute | solution.py:47
  100.6 27.5 %copy-start.5 = (bf16[640,512]{1,0:T(8,128)(2,1)}, bf16[640,512]{1,0:T(8,128)(2,1)S(1)}, u32[]{:S(2)}) copy-start(bf16[640,512]{1,0:T(8,128)(2,1)S(1)} %collective-permute-done.4.refs_3_) | copy-start | bytes 1966084
  100.6 12.4 %collective-permute-start.8 = (bf16[320,512]{1,0:T(8,128)(2,1)S(1)}, bf16[320,512]{1,0:T(8,128)(2,1)S(1)}, u32[]{:S(2)}, u32[]{:S(2)}) collective-permute-start(bf16[320,512]{1,0:T(8,128)(2,1)S(1)} %slice.39), channel_id=1, source_target_pairs={{0,6},{1,7},{2,0},{3,1},{4,2},{5,3},{6,4},{7,5},{8,14},{9,15},{10,... | collective-permute-start | bytes 983048 | tf_op jit(solution)/shard_map/ppermute | solution.py:47
  104.0 24.1 %copy-start.8 = (bf16[640,512]{1,0:T(8,128)(2,1)}, bf16[640,512]{1,0:T(8,128)(2,1)S(1)}, u32[]{:S(2)}) copy-start(bf16[640,512]{1,0:T(8,128)(2,1)S(1)} %collective-permute-done.2.refs_1_) | copy-start | bytes 1966084
  104.0 21.7 %collective-permute-start.5 = (bf16[640,512]{1,0:T(8,128)(2,1)S(1)}, bf16[640,512]{1,0:T(8,128)(2,1)S(1)}, u32[]{:S(2)}, u32[]{:S(2)}) collective-permute-start(bf16[640,512]{1,0:T(8,128)(2,1)S(1)} %collective-permute-done.2.refs_1_), channel_id=1, source_target_pairs={{0,2},{1,3},{2,4},{3,5},{4,6},{5,7},{6,0},{7,1},{8,10},{9,11},{10,... | collective-permute-start | bytes 1966088 | tf_op jit(solution)/shard_map/ppermute | solution.py:47
  104.0 21.7 %collective-permute-start.6 = (bf16[640,512]{1,0:T(8,128)(2,1)S(1)}, bf16[640,512]{1,0:T(8,128)(2,1)S(1)}, u32[]{:S(2)}, u32[]{:S(2)}) collective-permute-start(bf16[640,512]{1,0:T(8,128)(2,1)S(1)} %collective-permute-done.2.refs_1_), channel_id=1, source_target_pairs={{0,6},{1,7},{2,0},{3,1},{4,2},{5,3},{6,4},{7,5},{8,14},{9,15},{10,... | collective-permute-start | bytes 1966088 | tf_op jit(solution)/shard_map/ppermute | solution.py:47
  112.3 15.8 %copy-start.11 = (bf16[320,512]{1,0:T(8,128)(2,1)}, bf16[320,512]{1,0:T(8,128)(2,1)S(1)}, u32[]{:S(2)}) copy-start(bf16[320,512]{1,0:T(8,128)(2,1)S(1)} %collective-permute-done.7.refs_6_) | copy-start | bytes 983044
  112.3 14.2 %collective-permute-start.9 = (bf16[320,512]{1,0:T(8,128)(2,1)S(1)}, bf16[320,512]{1,0:T(8,128)(2,1)S(1)}, u32[]{:S(2)}, u32[]{:S(2)}) collective-permute-start(bf16[320,512]{1,0:T(8,128)(2,1)S(1)} %collective-permute-done.7.refs_6_), channel_id=1, source_target_pairs={{0,1},{1,0},{2,3},{3,2},{4,5},{5,4},{6,7},{7,6},{8,9},{9,8},{10,11... | collective-permute-start | bytes 983048 | tf_op jit(solution)/shard_map/ppermute | solution.py:47
  113.0 13.5 %copy-start.12 = (bf16[320,512]{1,0:T(8,128)(2,1)}, bf16[320,512]{1,0:T(8,128)(2,1)S(1)}, u32[]{:S(2)}) copy-start(bf16[320,512]{1,0:T(8,128)(2,1)S(1)} %collective-permute-done.8.refs_7_) | copy-start | bytes 983044
  113.0 15.1 %collective-permute-start.10 = (bf16[320,512]{1,0:T(8,128)(2,1)S(1)}, bf16[320,512]{1,0:T(8,128)(2,1)}, u32[]{:S(2)}, u32[]{:S(2)}) collective-permute-start(bf16[320,512]{1,0:T(8,128)(2,1)S(1)} %collective-permute-done.8.refs_7_), channel_id=1, source_target_pairs={{0,1},{1,0},{2,3},{3,2},{4,5},{5,4},{6,7},{7,6},{8,9},{9,8},{10,11... | collective-permute-start | bytes 983048 | tf_op jit(solution)/shard_map/ppermute | solution.py:47
  125.6 0.9 copy-start.9
  126.5 0.9 copy-start.10
  127.3 0.7 copy-start.13
  140.2 17.7 %collective-permute-start.12 = (bf16[320,896]{1,0:T(8,128)(2,1)}, bf16[320,896]{1,0:T(8,128)(2,1)S(1)}, u32[]{:S(2)}, u32[]{:S(2)}) collective-permute-start(bf16[320,896]{1,0:T(8,128)(2,1)} %get-tuple-element.70), channel_id=1, source_target_pairs={{0,64},{1,65},{2,66},{3,67},{4,68},{5,69},{6,70},{7,71},{8,72},{9,... | collective-permute-start | bytes 1720328 | tf_op jit(solution)/shard_map/ppermute | solution.py:47
  141.5 9.4 %slice-start = ((s8[5242880]{0:T(1024)(128)(4,1)}), s8[4194304]{0:T(1024)(128)(4,1)S(1)}, s32[]{:S(2)}) async-start(s8[5242880]{0:T(1024)(128)(4,1)} %bitcast.50), calls=%async_computation.6 | async-start | bytes 8388608
  141.5 9.4 %slice-start.2 = ((s8[5242880]{0:T(1024)(128)(4,1)}), s8[4194304]{0:T(1024)(128)(4,1)S(1)}, s32[]{:S(2)}) async-start(s8[5242880]{0:T(1024)(128)(4,1)} %bitcast.52), calls=%async_computation.8 | async-start | bytes 8388608
  141.5 9.4 %slice-start.1 = ((s8[5242880]{0:T(1024)(128)(4,1)}), s8[1048576]{0:T(1024)(128)(4,1)S(1)}, s32[]{:S(2)}) async-start(s8[5242880]{0:T(1024)(128)(4,1)} %bitcast.50), calls=%async_computation.7 | async-start | bytes 2097152
  141.6 9.4 %slice-start.3 = ((s8[5242880]{0:T(1024)(128)(4,1)}), s8[1048576]{0:T(1024)(128)(4,1)S(1)}, s32[]{:S(2)}) async-start(s8[5242880]{0:T(1024)(128)(4,1)} %bitcast.52), calls=%async_computation.9 | async-start | bytes 2097152
  147.8 17.3 %collective-permute-start.11 = (bf16[320,512]{1,0:T(8,128)(2,1)S(1)}, bf16[320,512]{1,0:T(8,128)(2,1)S(1)}, u32[]{:S(2)}, u32[]{:S(2)}) collective-permute-start(bf16[320,512]{1,0:T(8,128)(2,1)S(1)} %dynamic-slice_convert_fusion), channel_id=1, source_target_pairs={{0,64},{1,65},{2,66},{3,67},{4,68},{5,69},{6,70},{7,71},{8,72},{9,... | collective-permute-start | bytes 983048 | tf_op jit(solution)/shard_map/ppermute | solution.py:47
  151.8 6.2 %copy-start = (f32[320,896]{1,0:T(8,128)S(1)}, f32[320,896]{1,0:T(8,128)}, u32[]{:S(2)}) copy-start(f32[320,896]{1,0:T(8,128)} %get-tuple-element.75) | copy-start | bytes 3440644
Sparse Core Ops, SparseCore 0:
  65.9 41.6 all-gather.2
  109.4 32.1 all-gather.4

commit v3 on v2

--- a/solution.py
+++ b/solution.py
@@ -23,7 +23,7 @@
 ROWS = 160
 TOKENS = 4 * ROWS
 HALF = 512
-SLOTS = 64
+SLOTS = 56
 PART = 512
 FIRST = 768
 
@@ -109,7 +109,10 @@
 
 
 def project_kernel(place_ref, *refs):
-    blocks, w_ref, mine_ref, other_ref, tokens_ref, held, total, sems = refs[:10], *refs[10:17]
+    blocks, w_ref, mine_ref, other_ref, sums_ref, tokens_ref, held, total, sems = (
+        refs[:10],
+        *refs[10:18],
+    )
     half = TOKENS // 2
     width = w_ref.shape[1]
     columns = mine_ref.shape[1] - 128
@@ -151,12 +154,7 @@
             return jnp.sum(parts, axis=1, keepdims=True)
 
         mine_ref[:, columns:] = jnp.broadcast_to(sums(own), (half, 128))
-        partner_sums = sums(partner)
-        high = partner_sums.astype(jnp.bfloat16).astype(jnp.float32)
-        lanes = lax.broadcasted_iota(jnp.int32, (half, 128), 1)
-        other_ref[:, columns:] = jnp.where(lanes < 64, high, partner_sums - high).astype(
-            jnp.bfloat16
-        )
+        sums_ref[...] = jnp.broadcast_to(sums(partner), (half, 128))
 
     @pl.when(step == pl.num_programs(0) - 1)
     def _():
@@ -176,7 +174,8 @@
             in_specs=[anywhere] * 10 + [pl.BlockSpec((8 * HALF, 256), lambda n, place: (0, n))],
             out_specs=[
                 pl.BlockSpec((half, width), lambda n, place: (0, 0)),
-                pl.BlockSpec((half, width), lambda n, place: (0, 0)),
+                pl.BlockSpec((half, columns), lambda n, place: (0, 0)),
+                pl.BlockSpec((half, 128), lambda n, place: (0, 0)),
                 anywhere,
             ],
             scratch_shapes=[
@@ -187,7 +186,8 @@
         ),
         out_shape=[
             jax.ShapeDtypeStruct((half, width), jnp.float32),
-            jax.ShapeDtypeStruct((half, width), jnp.bfloat16),
+            jax.ShapeDtypeStruct((half, columns), jnp.bfloat16),
+            jax.ShapeDtypeStruct((half, 128), jnp.float32),
             jax.ShapeDtypeStruct((TOKENS, 8 * HALF), jnp.bfloat16),
         ],
         compiler_params=pltpu.CompilerParams(vmem_limit_bytes=60 << 20),
@@ -236,10 +236,10 @@
 
 def attend_kernel(first, *refs):
     if first:
-        mine, came, bias, cosine, sine, mask, k_ref, v_ref = refs[:8]
-        out, keys_out, values_out, scale_out = refs[8:12]
-        work = refs[12]
-        spare = refs[13:]
+        mine, came, bias, cosine, sine, mask, k_ref, v_ref, came_sums = refs[:9]
+        out, keys_out, values_out, scale_out = refs[9:13]
+        work = refs[13]
+        spare = refs[14:]
     else:
         mine, came, bias, cosine, sine, mask, k_ref, v_ref = refs[:8]
         keys_in, values_in, scale_in = refs[8:11]
@@ -258,8 +258,7 @@
     new_keys, new_values = [], []
     for step in range(2):
         if first:
-            part = came[step, :, FIRST : FIRST + 128].astype(jnp.float32)
-            sums = mine[step, :, FIRST : FIRST + 128] + part + pltpu.roll(part, 64, 1)
+            sums = mine[step, :, FIRST : FIRST + 128] + came_sums[step]
             scale = lax.rsqrt(sums / D + 1e-06) / math.sqrt(D)
             scale_out[step] = scale
             key = rotated(raw(step, PART, scale), step).astype(jnp.bfloat16)
@@ -323,7 +322,7 @@
 
     in_specs = [
         steps(width),
-        steps(width),
+        steps(came.shape[-1]),
         pl.BlockSpec((1, bias.shape[-1]), lambda i: (0, 0)),
         steps(HEAD),
         steps(HEAD),
@@ -333,6 +332,7 @@
     ]
     context = jax.ShapeDtypeStruct((2, ROWS, 2 * PART), jnp.bfloat16)
     if first:
+        in_specs += [steps(HEAD)]
         out_specs = [steps(PART), steps(HEAD), steps(HEAD), steps(HEAD)]
         out_shape = [
             context,
@@ -393,18 +393,29 @@
     earlier = order[:, None] < order[None, :]
     same_id = paired[:, :, None] == paired[:, None, :]
     first = ~jnp.any(same_id & earlier[None], axis=1)
-    first_owner = jnp.where(first, owners, -1)
-    ranks = jnp.sum(
-        ((first_owner[:, :, None] == owners[:, None, :]) & earlier[None]).astype(jnp.int32), axis=1
-    )
-    rounds = (jnp.max(jnp.where(first, ranks, 0)) + SLOTS) // SLOTS
+    counts = jnp.sum(
+        (first[:, None, :] & (owners[:, None, :] == jnp.arange(OWNERS)[None, :, None])).astype(
+            jnp.int32
+        ),
+        axis=2,
+    )
+    rounds = (jnp.max(counts) + SLOTS - 1) // SLOTS
+
+    def ranks_in(chosen):
+        return jnp.dot(
+            chosen.astype(jnp.bfloat16),
+            earlier.astype(jnp.bfloat16),
+            preferred_element_type=jnp.float32,
+        ).astype(jnp.int32)
 
     local = paired - fsdp_index * vocab_rows
-    sent_rank = jnp.where(first_owner == fsdp_index, ranks, -1)
+    sent = first & (owners == fsdp_index)
+    sent_rank = jnp.where(sent, ranks_in(sent), -1)
     own_ids = lax.dynamic_index_in_dim(paired, pair, 0, keepdims=False)
     own_first = lax.dynamic_index_in_dim(first, pair, 0, keepdims=False)
-    own_ranks = lax.dynamic_index_in_dim(ranks, pair, 0, keepdims=False)
     own_owners = lax.dynamic_index_in_dim(owners, pair, 0, keepdims=False)
+    by_owner = own_first[None, :] & (own_owners[None, :] == jnp.arange(OWNERS)[:, None])
+    own_ranks = jnp.sum(jnp.where(by_owner, ranks_in(by_owner), 0), axis=0)
     got_rank = jnp.sum(
         jnp.where(
             (own_ids[:, None] == own_ids[None, :]) & own_first[:, None], own_ranks[:, None], 0
@@ -438,13 +449,15 @@
 
     rows = exchanged(wanted_rows(0))
     queries, rollout, rows = lax.optimization_barrier((queries, rollout, rows))
-    packed = pack_columns(queries, rollout[:, :1024], rollout[:, 1024:])
-    own = placed_rows(0, rows)
-    weights = []
-    for part in packed:
+    first_part, second_part = pack_columns(queries, rollout[:, :1024], rollout[:, 1024:])
+
+    def gathered(part):
         part = lax.all_to_all(part, TP, split_axis=0, concat_axis=0)
         part = lax.all_gather(part.reshape(HALF, part.shape[-1]), ("z", "c"))
-        weights.append(part.reshape(8 * HALF, part.shape[-1]))
+        return part.reshape(8 * HALF, part.shape[-1])
+
+    weights = [gathered(first_part), gathered(second_part)]
+    own = placed_rows(0, rows)
     _, own = lax.while_loop(
         lambda state: state[0] < rounds,
         lambda state: (state[0] + 1, state[1] + placed_rows(state[0], exchanged(wanted_rows(state[0])))),
@@ -484,8 +497,10 @@
         far_low_across,
         far_high_across,
     )
-    mine_first, other_first, tokens = project(place, blocks, weights[0])
+    mine_first, other_first, other_sums, tokens = project(place, blocks, weights[0])
     came_first = send(other_first, other_xh)
+    came_sums = send(other_sums[:, 0], other_xh)
+    came_sums = jnp.broadcast_to(came_sums[:, None], (half, HEAD))
     k_cache, v_cache, _ = lax.optimization_barrier((k_cache, v_cache, other_first))
     k_cache, v_cache = hold(k_cache, v_cache)
     total_second = jnp.dot(tokens, weights[1], preferred_element_type=jnp.float32)
@@ -513,6 +528,7 @@
         mask,
         k_cache,
         v_cache,
+        stepwise(came_sums),
     )
     context = attend(
         False,

time: 181 us -> 184 us (1.017); the launches traced: 178 us -> 183 us
  local copies, waits for them, and re-layouts: 19.7 us -> 26.6 us
  other arithmetic: 10.7 us -> 7.35 us
    unnamed x41 -> x45, local copies, waits for them, and re-layouts: 8.06 us -> 14.8 us
    reduce_sum x1, other arithmetic: 2.67 us -> 0.22 us  [per_device(): jnp.sum((first[:, None, :] & (owners[:, None, :] == jnp.arange(OWNERS)[No...]
    ppermute x13 -> x14, waiting for transfers between devices: 30.9 us -> 32.7 us  [send(): return lax.ppermute(array, NAMES, pairs_of(move))]
    ppermute x13 -> x14, starting transfers between devices: 18.5 us -> 18.3 us  [send(): return lax.ppermute(array, NAMES, pairs_of(move))]
  transfers between devices with their start and end apart: 16 -> 17, of which waited for: 6 -> 6; matrix products, arithmetic and copies ran while one was open for 20% -> 18% of each run, Pallas kernels for 11% -> 10%
where the time goes in v3:
time: 184 us; the launch traced here: 183 us
  waiting for transfers between devices  42.6 us (23%)
  blocking collectives  29.8 us (16%)
  local copies, waits for them, and re-layouts  26.6 us (14%)
  starting transfers between devices  26.2 us (14%)
  Pallas kernels  25.3 us (14%)
  between operations  15.5 us (8%)
  matrix products  9.56 us (5%)
  other arithmetic  7.35 us (4%)
    ppermute x14, waiting for transfers between devices, send(): return lax.ppermute(array, NAMES, pairs_of(move))  32.7 us
    all_to_all x2, blocking collectives, gathered(): part = lax.all_to_all(part, TP, split_axis=0, concat_axis=0)  29.8 us
    ppermute x14, starting transfers between devices, send(): return lax.ppermute(array, NAMES, pairs_of(move))  18.3 us
    unnamed x45, local copies, waits for them, and re-layouts  14.8 us
    pallas_call x2, Pallas kernels, attend(): pl.pallas_call(functools.partial(attend_kernel, first), grid=(ROWS // BLO...  12.3 us
    pallas_call x1, Pallas kernels, project(): pl.pallas_call(project_kernel, grid_spec=pltpu.PrefetchScalarGridSpec(num...  12.1 us
    all_to_all x1, waiting for transfers between devices, exchanged(): return lax.all_to_all(rows, FSDP, split_axis=0, concat_axis=0)  9.8 us
    gather x1, local copies, waits for them, and re-layouts, wanted_rows(): rows = embedding.at[wanted.reshape(-1)].get(mode='promise_in_bounds')  7.82 us
  transfers between devices with their start and end apart: 17, of which 6 were waited for; matrix products, arithmetic and copies ran while one was open for 18% of the time, Pallas kernels for 10%

profile of v3, /device:TPU:64, one launch (start us, length us, event | category | flops | bytes accessed | tf_op | source)
XLA Modules:
  0.0 182.9 jit_solution(11646537369548782578)
XLA Ops:
  7.2 1.9 %collective-permute-start = (bf16[64,8192]{1,0:T(8,128)(2,1)}, bf16[64,8192]{1,0:T(8,128)(2,1)S(1)}, u32[]{:S(2)}, u32[]{:S(2)}) collective-permute-start(bf16[64,8192]{1,0:T(8,128)(2,1)} %param.17), channel_id=1, source_target_pairs={{0,0},{1,1},{2,2},{3,3},{4,4},{5,5},{6,6},{7,7},{8,64},{9,65},{10,... | collective-permute-start | bytes 3145736 | tf_op jit(solution)/shard_map/ppermute | solution.py:47
  9.0 0.1 iota_compare_fusion.8
  9.2 0.8 reshape.240
  10.0 0.1 reshape.241
  10.2 2.7 %and_reduce_fusion = pred[8,640]{1,0:T(8,128)(4,1)S(1)} fusion(s32[8,640]{1,0:T(8,128)S(1)} %reshape.241, pred[640,640]{1,0:T(8,128)(4,1)S(1)} %iota_compare_fusion.8), kind=kLoop, calls=%fused_computation.12 | loop fusion | flops 9825280 | bytes 435200 | tf_op jit(solution)/shard_map/reduce_or | solution.py:395
  12.8 0.2 fusion.9
  13.0 0.2 select_reduce_fusion.2
  13.3 0.1 reshape.242
  13.4 7.8 %gather_fusion.1 = bf16[448,1024]{1,0:T(8,128)(2,1)S(1)} fusion(bf16[4752,1024]{1,0:T(8,128)(2,1)} %param.15, s32[1024]{0:T(1024)S(1)} %pad_clamp_fusion.1), kind=kCustom, calls=%fused_computation.1 | custom fusion | bytes 1836800 | tf_op jit(solution)/shard_map/gather | solution.py:432
  21.2 0.7 reshape.243
  21.9 1.1 copy.55
  23.0 7.8 %all-to-all-start.1 = ((bf16[16,56,512]{2,1,0:T(8,128)(2,1)}), bf16[16,56,512]{2,1,0:T(8,128)(2,1)}, u32[]{:S(2)}, u32[]{:S(2)}) async-start(bf16[16,56,512]{2,1,0:T(8,128)(2,1)} %bitcast.18), calls=%async_computation.1 | async-start | bytes 1835008 | tf_op jit(solution)/shard_map/all_to_all | solution.py:437
  30.8 0.0 all-gather.3.cloned.1.call-start
  30.8 2.1 %fusion.24 = (bf16[64,2,1024]{2,0,1:T(8,128)(2,1)S(1)}, f32[64,2,1024]{2,0,1:T(8,128)S(1)}, f32[64,2,1024]{2,0,1:T(8,128)S(1)}, f32[64,2,1024]{2,0,1:T(8,128)S(1)}) fusion(f32[64,2,1024]{2,1,0:T(2,128)S(1)} %copy-done.7, bf16[64,2,1024]{2,1,0:T(2,128)(2,1)} %param.23, f32[64,2,1024]{2,1,0:T(2,128)} %param.21, f32[64,2,1024]{2,1,0:T(2,128)} %param.22), kind=kLoop, calls=%fused_computation.73 | loop fusion | flops 2228224 | bytes 3670016 | tf_op jit(solution)/shard_map/convert_element_type | solution.py:386
  32.9 0.7 collective-permute-start.1
  33.6 9.8 %all-to-all-done.1 = bf16[16,56,512]{2,1,0:T(8,128)(2,1)} async-done(((bf16[16,56,512]{2,1,0:T(8,128)(2,1)}), bf16[16,56,512]{2,1,0:T(8,128)(2,1)}, u32[]{:S(2)}, u32[]{:S(2)}) %all-to-all-start.1) | async-done | bytes 917536 | tf_op jit(solution)/shard_map/all_to_all | solution.py:437
  43.5 0.1 shard_map.147
  43.6 16.6 %all_to_all.21 = bf16[8,64,768]{2,1,0:T(8,128)(2,1)} all-to-all(bf16[8,64,768]{2,1,0:T(8,128)(2,1)S(1)} %get-tuple-element.68), channel_id=1, replica_groups=mesh['xh'=2,'z'=4,'c'=2,'y'=4,'xl'=2] {'y','xl'}, dimensions={0} | all-to-all | bytes 1572864 | tf_op jit(solution)/shard_map/all_to_all | solution.py:455
  60.2 0.0 all-gather.5.cloned.1.call-start
  60.3 13.2 %all_to_all.22 = bf16[8,64,512]{2,1,0:T(8,128)(2,1)} all-to-all(bf16[8,64,512]{2,1,0:T(8,128)(2,1)S(1)} %get-tuple-element.70), channel_id=1, replica_groups=mesh['xh'=2,'z'=4,'c'=2,'y'=4,'xl'=2] {'y','xl'}, dimensions={0} | all-to-all | bytes 1048576 | tf_op jit(solution)/shard_map/all_to_all | solution.py:455
  73.7 0.2 convert_reduce_fusion
  73.9 0.6 reduce_max.9
  75.5 0.2 fusion.8
  75.7 0.4 select_reduce_fusion.1
  76.1 2.9 %fusion.5 = bf16[640,512]{1,0:T(8,128)(2,1)} fusion(bf16[896,512]{1,0:T(8,128)(2,1)} %bitcast.19, s32[640]{0:T(1024)S(1)} %add_select_fusion.2), kind=kOutput, calls=%fused_computation.17 | convolution fusion | flops 588103680 | bytes 1575424 | tf_op jit(solution)/shard_map/dot_general | solution.py:444
  79.0 0.9 collective-permute-start.2
  79.9 1.0 collective-permute-start.3
  80.9 2.3 %collective-permute-start.4 = (bf16[640,512]{1,0:T(8,128)(2,1)}, bf16[640,512]{1,0:T(8,128)(2,1)S(1)}, u32[]{:S(2)}, u32[]{:S(2)}) collective-permute-start(bf16[640,512]{1,0:T(8,128)(2,1)} %get-tuple-element.65.refs_0_), channel_id=1, source_target_pairs={{0,6},{1,7},{2,0},{3,1},{4,2},{5,3},{6,4},{7,5},{8,14},{9,15},{10,... | collective-permute-start | bytes 1966088 | tf_op jit(solution)/shard_map/ppermute | solution.py:47
  83.2 15.7 %collective-permute-done.3.refs_2_ = bf16[640,512]{1,0:T(8,128)(2,1)S(1)} collective-permute-done((bf16[640,512]{1,0:T(8,128)(2,1)}, bf16[640,512]{1,0:T(8,128)(2,1)S(1)}, u32[]{:S(2)}, u32[]{:S(2)}) %collective-permute-start.3) | collective-permute-done | bytes 655392 | tf_op jit(solution)/shard_map/ppermute | solution.py:47
  98.9 0.1 collective-permute-start.7
  99.0 0.8 copy-done.8
  99.8 2.5 %collective-permute-start.8 = (bf16[320,512]{1,0:T(8,128)(2,1)S(1)}, bf16[320,512]{1,0:T(8,128)(2,1)S(1)}, u32[]{:S(2)}, u32[]{:S(2)}) collective-permute-start(bf16[320,512]{1,0:T(8,128)(2,1)S(1)} %slice.43), channel_id=1, source_target_pairs={{0,6},{1,7},{2,0},{3,1},{4,2},{5,3},{6,4},{7,5},{8,14},{9,15},{10,... | collective-permute-start | bytes 983048 | tf_op jit(solution)/shard_map/ppermute | solution.py:47
  102.3 3.2 %collective-permute-start.6 = (bf16[640,512]{1,0:T(8,128)(2,1)}, bf16[640,512]{1,0:T(8,128)(2,1)}, u32[]{:S(2)}, u32[]{:S(2)}) collective-permute-start(bf16[640,512]{1,0:T(8,128)(2,1)} %collective-permute-done.2.refs_1_), channel_id=1, source_target_pairs={{0,6},{1,7},{2,0},{3,1},{4,2},{5,3},{6,4},{7,5},{8,14},{9,15},{10,... | collective-permute-start | bytes 1966088 | tf_op jit(solution)/shard_map/ppermute | solution.py:47
  105.6 1.2 copy.56
  106.8 1.2 copy.57
  107.9 1.2 copy.58
  109.2 0.6 stack.39.place_ref
  109.8 0.1 fusion.13
  109.9 1.0 collective-permute-done.7.refs_6_
  110.8 1.2 collective-permute-start.9
  112.1 0.8 collective-permute-start.10
  112.9 0.7 fusion.14
  113.5 10.5 %collective-permute-done.5.refs_4_ = bf16[640,512]{1,0:T(8,128)(2,1)} collective-permute-done((bf16[640,512]{1,0:T(8,128)(2,1)}, bf16[640,512]{1,0:T(8,128)(2,1)}, u32[]{:S(2)}, u32[]{:S(2)}) %collective-permute-start.5) | collective-permute-done | bytes 655392 | tf_op jit(solution)/shard_map/ppermute | solution.py:47
  124.1 2.1 %collective-permute-done.10.refs_9_ = bf16[320,512]{1,0:T(8,128)(2,1)S(1)} collective-permute-done((bf16[320,512]{1,0:T(8,128)(2,1)S(1)}, bf16[320,512]{1,0:T(8,128)(2,1)S(1)}, u32[]{:S(2)}, u32[]{:S(2)}) %collective-permute-start.10) | collective-permute-done | bytes 327712 | tf_op jit(solution)/shard_map/ppermute | solution.py:47
  126.1 0.7 copy-done.17
  126.9 12.1 %shard_map.148 = (f32[320,896]{1,0:T(8,128)}, bf16[320,768]{1,0:T(8,128)(2,1)}, f32[320,128]{1,0:T(8,128)}, bf16[640,4096]{1,0:T(8,128)(2,1)}) custom-call(s32[9]{0:T(128)} %stack.39.place_ref, bf16[640,512]{1,0:T(8,128)(2,1)} %get-tuple-element.65.refs_0_, bf16[640,512]{1,0:T(8,128)(2,1)} %collective-permute-done.2.refs_1_, bf16[640,512]{1,0:T(8,128)(2,1)} %copy-done.8, ...), custom_call_target="tpu_custom_call" | custom-call | flops 4026531840 | bytes 12582912 | tf_op jit(solution)/shard_map/pallas_call | solution.py:169
  139.0 0.1 collective-permute-start.12
  139.1 0.0 all-gather.5.cloned.1.call-done
  139.2 6.2 %fusion.29 = f32[640,512]{1,0:T(8,128)S(1)} fusion(bf16[640,4096]{1,0:T(8,128)(2,1)} %get-tuple-element.69, bf16[4096,512]{1,0:T(8,128)(2,1)} %bitcast.66), kind=kOutput, calls=%fused_computation.76 | convolution fusion | flops 2684354560 | bytes 10747904 | tf_op jit(solution)/shard_map/dot_general | solution.py:506
  145.4 0.1 dynamic-slice_convert_fusion
  145.4 3.5 %collective-permute-start.11 = (bf16[320,512]{1,0:T(8,128)(2,1)S(1)}, bf16[320,512]{1,0:T(8,128)(2,1)S(1)}, u32[]{:S(2)}, u32[]{:S(2)}) collective-permute-start(bf16[320,512]{1,0:T(8,128)(2,1)S(1)} %dynamic-slice_convert_fusion), channel_id=1, source_target_pairs={{0,64},{1,65},{2,66},{3,67},{4,68},{5,69},{6,70},{7,71},{8,72},{9,... | collective-permute-start | bytes 983048 | tf_op jit(solution)/shard_map/ppermute | solution.py:47
  149.0 0.2 pad_maximum_fusion.1
  149.2 0.1 slice_reduce_fusion
  149.3 0.1 collective-permute-start.13
  149.5 0.8 shard_map.149
  150.4 2.3 %copy-done = bf16[160,128,128]{2,1,0:T(8,128)(2,1)} copy-done((bf16[160,128,128]{2,1,0:T(8,128)(2,1)}, bf16[160,128,128]{2,1,0:T(8,128)(2,1)S(1)}, u32[]{:S(2)}) %copy-start) | copy-done | bytes 5242904
  152.7 2.4 %copy-done.3 = bf16[160,128,128]{2,1,0:T(8,128)(2,1)} copy-done((bf16[160,128,128]{2,1,0:T(8,128)(2,1)}, bf16[160,128,128]{2,1,0:T(8,128)(2,1)S(1)}, u32[]{:S(2)}) %copy-start.3) | copy-done | bytes 5242904
  155.1 3.5 %collective-permute-done.13 = f32[320]{0:T(512)S(1)} collective-permute-done((f32[320]{0:T(512)S(1)}, f32[320]{0:T(512)S(1)}, u32[]{:S(2)}, u32[]{:S(2)}) %collective-permute-start.13) | collective-permute-done | bytes 1312 | tf_op jit(solution)/shard_map/ppermute | solution.py:47
  158.6 0.1 broadcast_in_dim.120
  158.7 0.1 broadcast_in_dim.121.refs_8_
  158.8 2.5 %copy-done.1 = bf16[160,128,128]{2,1,0:T(8,128)(2,1)S(1)} copy-done((bf16[160,128,128]{2,1,0:T(8,128)(2,1)S(1)}, bf16[160,128,128]{2,1,0:T(8,128)(2,1)}, u32[]{:S(2)}) %copy-start.1) | copy-done | bytes 5242904
  161.3 2.5 %copy-done.4 = bf16[160,128,128]{2,1,0:T(8,128)(2,1)S(1)} copy-done((bf16[160,128,128]{2,1,0:T(8,128)(2,1)S(1)}, bf16[160,128,128]{2,1,0:T(8,128)(2,1)}, u32[]{:S(2)}) %copy-start.4) | copy-done | bytes 5242904
  163.8 6.2 %shard_map.150 = (bf16[2,160,1024]{2,1,0:T(8,128)(2,1)}, bf16[2,160,128]{2,1,0:T(8,128)(2,1)S(1)}, bf16[2,160,128]{2,1,0:T(8,128)(2,1)S(1)}, f32[2,160,128]{2,1,0:T(8,128)S(1)}) custom-call(f32[2,160,896]{2,1,0:T(8,128)S(1)} %bitcast.55, bf16[2,160,768]{2,1,0:T(8,128)(2,1)S(1)} %bitcast.56, f32[1,768]{1,0:T(1,128)S(1)} %broadcast_in_dim.119.refs_2_, ...), custom_call_target="tpu_custom_call" | custom-call | flops 83886080 | bytes 12582912 | tf_op jit(solution)/shard_map/pallas_call | solution.py:349
  170.0 6.1 %shard_map.151 = bf16[2,160,1024]{2,1,0:T(8,128)(2,1)} custom-call(f32[2,160,512]{2,1,0:T(8,128)S(1)} %bitcast.54, bf16[2,160,512]{2,1,0:T(8,128)(2,1)S(1)} %bitcast.57, f32[1,512]{1,0:T(1,128)S(1)} %bitcast.58, f32[2,160,128]{2,1,0:T(8,128)S(1)} %get-tuple-element.131.refs_3_, ...), custom_call_target="tpu_custom_call", output_to_operand_aliasing={{}: (11, {})} | custom-call | flops 83886080 | bytes 12582912 | tf_op jit(solution)/shard_map/pallas_call | solution.py:349
  (73 shorter events, 0.5 us)
Async XLA Ops:
  7.2 36.3 %collective-permute-start = (bf16[64,8192]{1,0:T(8,128)(2,1)}, bf16[64,8192]{1,0:T(8,128)(2,1)S(1)}, u32[]{:S(2)}, u32[]{:S(2)}) collective-permute-start(bf16[64,8192]{1,0:T(8,128)(2,1)} %param.17), channel_id=1, source_target_pairs={{0,0},{1,1},{2,2},{3,3},{4,4},{5,5},{6,6},{7,7},{8,64},{9,65},{10,... | collective-permute-start | bytes 3145736 | tf_op jit(solution)/shard_map/ppermute | solution.py:47
  21.9 8.9 %copy-start.7 = (f32[64,2,1024]{2,1,0:T(2,128)S(1)}, f32[64,2,1024]{2,1,0:T(2,128)}, u32[]{:S(2)}) copy-start(f32[64,2,1024]{2,1,0:T(2,128)} %param.20) | copy-start | bytes 1572868
  23.0 20.4 %all-to-all-start.1 = ((bf16[16,56,512]{2,1,0:T(8,128)(2,1)}), bf16[16,56,512]{2,1,0:T(8,128)(2,1)}, u32[]{:S(2)}, u32[]{:S(2)}) async-start(bf16[16,56,512]{2,1,0:T(8,128)(2,1)} %bitcast.18), calls=%async_computation.1 | async-start | bytes 1835008 | tf_op jit(solution)/shard_map/all_to_all | solution.py:437
  30.8 95.4 %all-gather.3.cloned.1.call-start = ((), (), s32[]{:S(2)}) async-start(), calls=%async_computation.4 | async-start | bytes 7077888 | tf_op jit(solution)/shard_map/all_gather | solution.py:456
  32.9 0.7 collective-permute-start.1
  60.2 78.8 %all-gather.5.cloned.1.call-start = ((), (), s32[]{:S(2)}) async-start(), calls=%async_computation.5 | async-start | bytes 4718592 | tf_op jit(solution)/shard_map/all_gather | solution.py:456
  79.0 4.1 %copy-start.18 = (bf16[2,128]{1,0:T(2,128)(2,1)S(1)}, bf16[2,128]{1,0:T(2,128)(2,1)}, u32[]{:S(2)}) copy-start(bf16[2,128]{1,0:T(2,128)(2,1)} %param.19) | copy-start | bytes 1540
  79.0 4.1 %copy-start.12 = (s32[160]{0:T(256)S(1)}, s32[160]{0:T(256)}, u32[]{:S(2)}) copy-start(s32[160]{0:T(256)} %param.16) | copy-start | bytes 1924
  79.0 4.1 %copy-start.11 = (bf16[1024]{0:T(1024)(128)(2,1)S(1)}, bf16[1024]{0:T(1024)(128)(2,1)}, u32[]{:S(2)}) copy-start(bf16[1024]{0:T(1024)(128)(2,1)} %param.18) | copy-start | bytes 6148
  79.0 23.3 %collective-permute-start.2 = (bf16[640,512]{1,0:T(8,128)(2,1)}, bf16[640,512]{1,0:T(8,128)(2,1)}, u32[]{:S(2)}, u32[]{:S(2)}) collective-permute-start(bf16[640,512]{1,0:T(8,128)(2,1)} %get-tuple-element.65.refs_0_), channel_id=1, source_target_pairs={{0,1},{1,0},{2,3},{3,2},{4,5},{5,4},{6,7},{7,6},{8,9},{9,8},{10,11... | collective-permute-start | bytes 1966088 | tf_op jit(solution)/shard_map/ppermute | solution.py:47
  79.9 18.9 %collective-permute-start.3 = (bf16[640,512]{1,0:T(8,128)(2,1)}, bf16[640,512]{1,0:T(8,128)(2,1)S(1)}, u32[]{:S(2)}, u32[]{:S(2)}) collective-permute-start(bf16[640,512]{1,0:T(8,128)(2,1)} %get-tuple-element.65.refs_0_), channel_id=1, source_target_pairs={{0,2},{1,3},{2,4},{3,5},{4,6},{5,7},{6,0},{7,1},{8,10},{9,11},{10,... | collective-permute-start | bytes 1966088 | tf_op jit(solution)/shard_map/ppermute | solution.py:47
  80.9 18.8 %collective-permute-start.4 = (bf16[640,512]{1,0:T(8,128)(2,1)}, bf16[640,512]{1,0:T(8,128)(2,1)S(1)}, u32[]{:S(2)}, u32[]{:S(2)}) collective-permute-start(bf16[640,512]{1,0:T(8,128)(2,1)} %get-tuple-element.65.refs_0_), channel_id=1, source_target_pairs={{0,6},{1,7},{2,0},{3,1},{4,2},{5,3},{6,4},{7,5},{8,14},{9,15},{10,... | collective-permute-start | bytes 1966088 | tf_op jit(solution)/shard_map/ppermute | solution.py:47
  98.9 0.9 copy-start.8
  98.9 11.9 %collective-permute-start.7 = (bf16[320,512]{1,0:T(8,128)(2,1)S(1)}, bf16[320,512]{1,0:T(8,128)(2,1)}, u32[]{:S(2)}, u32[]{:S(2)}) collective-permute-start(bf16[320,512]{1,0:T(8,128)(2,1)S(1)} %slice.42), channel_id=1, source_target_pairs={{0,2},{1,3},{2,4},{3,5},{4,6},{5,7},{6,0},{7,1},{8,10},{9,11},{10,... | collective-permute-start | bytes 983048 | tf_op jit(solution)/shard_map/ppermute | solution.py:47
  99.7 9.4 %copy-start.9 = (bf16[640,512]{1,0:T(8,128)(2,1)}, bf16[640,512]{1,0:T(8,128)(2,1)S(1)}, u32[]{:S(2)}) copy-start(bf16[640,512]{1,0:T(8,128)(2,1)S(1)} %collective-permute-done.4.refs_3_) | copy-start | bytes 1966084
  99.8 12.3 %collective-permute-start.8 = (bf16[320,512]{1,0:T(8,128)(2,1)S(1)}, bf16[320,512]{1,0:T(8,128)(2,1)S(1)}, u32[]{:S(2)}, u32[]{:S(2)}) collective-permute-start(bf16[320,512]{1,0:T(8,128)(2,1)S(1)} %slice.43), channel_id=1, source_target_pairs={{0,6},{1,7},{2,0},{3,1},{4,2},{5,3},{6,4},{7,5},{8,14},{9,15},{10,... | collective-permute-start | bytes 983048 | tf_op jit(solution)/shard_map/ppermute | solution.py:47
  102.3 21.7 %collective-permute-start.5 = (bf16[640,512]{1,0:T(8,128)(2,1)}, bf16[640,512]{1,0:T(8,128)(2,1)}, u32[]{:S(2)}, u32[]{:S(2)}) collective-permute-start(bf16[640,512]{1,0:T(8,128)(2,1)} %collective-permute-done.2.refs_1_), channel_id=1, source_target_pairs={{0,2},{1,3},{2,4},{3,5},{4,6},{5,7},{6,0},{7,1},{8,10},{9,11},{10,... | collective-permute-start | bytes 1966088 | tf_op jit(solution)/shard_map/ppermute | solution.py:47
  102.3 21.7 %collective-permute-start.6 = (bf16[640,512]{1,0:T(8,128)(2,1)}, bf16[640,512]{1,0:T(8,128)(2,1)}, u32[]{:S(2)}, u32[]{:S(2)}) collective-permute-start(bf16[640,512]{1,0:T(8,128)(2,1)} %collective-permute-done.2.refs_1_), channel_id=1, source_target_pairs={{0,6},{1,7},{2,0},{3,1},{4,2},{5,3},{6,4},{7,5},{8,14},{9,15},{10,... | collective-permute-start | bytes 1966088 | tf_op jit(solution)/shard_map/ppermute | solution.py:47
  110.8 13.2 %collective-permute-start.9 = (bf16[320,512]{1,0:T(8,128)(2,1)}, bf16[320,512]{1,0:T(8,128)(2,1)S(1)}, u32[]{:S(2)}, u32[]{:S(2)}) collective-permute-start(bf16[320,512]{1,0:T(8,128)(2,1)} %collective-permute-done.7.refs_6_), channel_id=1, source_target_pairs={{0,1},{1,0},{2,3},{3,2},{4,5},{5,4},{6,7},{7,6},{8,9},{9,8},{10,11... | collective-permute-start | bytes 983048 | tf_op jit(solution)/shard_map/ppermute | solution.py:47
  112.1 14.1 %copy-start.15 = (bf16[320,512]{1,0:T(8,128)(2,1)}, bf16[320,512]{1,0:T(8,128)(2,1)S(1)}, u32[]{:S(2)}) copy-start(bf16[320,512]{1,0:T(8,128)(2,1)S(1)} %collective-permute-done.8.refs_7_) | copy-start | bytes 983044
  112.1 14.1 %collective-permute-start.10 = (bf16[320,512]{1,0:T(8,128)(2,1)S(1)}, bf16[320,512]{1,0:T(8,128)(2,1)S(1)}, u32[]{:S(2)}, u32[]{:S(2)}) collective-permute-start(bf16[320,512]{1,0:T(8,128)(2,1)S(1)} %collective-permute-done.8.refs_7_), channel_id=1, source_target_pairs={{0,1},{1,0},{2,3},{3,2},{4,5},{5,4},{6,7},{7,6},{8,9},{9,8},{10,11... | collective-permute-start | bytes 983048 | tf_op jit(solution)/shard_map/ppermute | solution.py:47
  124.1 2.1 %copy-start.16 = (bf16[320,512]{1,0:T(8,128)(2,1)}, bf16[320,512]{1,0:T(8,128)(2,1)S(1)}, u32[]{:S(2)}) copy-start(bf16[320,512]{1,0:T(8,128)(2,1)S(1)} %collective-permute-done.9.refs_8_) | copy-start | bytes 983044
  126.1 0.7 copy-start.17
  139.0 19.7 %collective-permute-start.12 = (bf16[320,768]{1,0:T(8,128)(2,1)}, bf16[320,768]{1,0:T(8,128)(2,1)S(1)}, u32[]{:S(2)}, u32[]{:S(2)}) collective-permute-start(bf16[320,768]{1,0:T(8,128)(2,1)} %get-tuple-element.71), channel_id=1, source_target_pairs={{0,64},{1,65},{2,66},{3,67},{4,68},{5,69},{6,70},{7,71},{8,72},{9,... | collective-permute-start | bytes 1474568 | tf_op jit(solution)/shard_map/ppermute | solution.py:47
  139.1 10.4 %slice-start = ((s8[5242880]{0:T(1024)(128)(4,1)}), s8[4194304]{0:T(1024)(128)(4,1)S(1)}, s32[]{:S(2)}) async-start(s8[5242880]{0:T(1024)(128)(4,1)} %bitcast.50), calls=%async_computation.6 | async-start | bytes 8388608
  139.1 10.4 %slice-start.2 = ((s8[5242880]{0:T(1024)(128)(4,1)}), s8[4194304]{0:T(1024)(128)(4,1)S(1)}, s32[]{:S(2)}) async-start(s8[5242880]{0:T(1024)(128)(4,1)} %bitcast.52), calls=%async_computation.8 | async-start | bytes 8388608
  139.1 10.0 %copy-start.10 = (f32[320,128]{1,0:T(8,128)S(1)}, f32[320,128]{1,0:T(8,128)}, u32[]{:S(2)}) copy-start(f32[320,128]{1,0:T(8,128)} %get-tuple-element.77) | copy-start | bytes 491524
  139.1 10.4 %slice-start.1 = ((s8[5242880]{0:T(1024)(128)(4,1)}), s8[1048576]{0:T(1024)(128)(4,1)S(1)}, s32[]{:S(2)}) async-start(s8[5242880]{0:T(1024)(128)(4,1)} %bitcast.50), calls=%async_computation.7 | async-start | bytes 2097152
  139.1 10.4 %slice-start.3 = ((s8[5242880]{0:T(1024)(128)(4,1)}), s8[1048576]{0:T(1024)(128)(4,1)S(1)}, s32[]{:S(2)}) async-start(s8[5242880]{0:T(1024)(128)(4,1)} %bitcast.52), calls=%async_computation.9 | async-start | bytes 2097152
  145.4 24.5 %collective-permute-start.11 = (bf16[320,512]{1,0:T(8,128)(2,1)S(1)}, bf16[320,512]{1,0:T(8,128)(2,1)S(1)}, u32[]{:S(2)}, u32[]{:S(2)}) collective-permute-start(bf16[320,512]{1,0:T(8,128)(2,1)S(1)} %dynamic-slice_convert_fusion), channel_id=1, source_target_pairs={{0,64},{1,65},{2,66},{3,67},{4,68},{5,69},{6,70},{7,71},{8,72},{9,... | collective-permute-start | bytes 983048 | tf_op jit(solution)/shard_map/ppermute | solution.py:47
  149.3 9.3 %collective-permute-start.13 = (f32[320]{0:T(512)S(1)}, f32[320]{0:T(512)S(1)}, u32[]{:S(2)}, u32[]{:S(2)}) collective-permute-start(f32[320]{0:T(512)S(1)} %slice_reduce_fusion), channel_id=1, source_target_pairs={{0,64},{1,65},{2,66},{3,67},{4,68},{5,69},{6,70},{7,71},{8,72},{9,... | collective-permute-start | bytes 3848 | tf_op jit(solution)/shard_map/ppermute | solution.py:47
  149.5 9.3 %copy-start.6 = (f32[320,896]{1,0:T(8,128)S(1)}, f32[320,896]{1,0:T(8,128)}, u32[]{:S(2)}) copy-start(f32[320,896]{1,0:T(8,128)} %get-tuple-element.76) | copy-start | bytes 3440644
  150.4 2.3 %copy-start = (bf16[160,128,128]{2,1,0:T(8,128)(2,1)}, bf16[160,128,128]{2,1,0:T(8,128)(2,1)S(1)}, u32[]{:S(2)}) copy-start(bf16[160,128,128]{2,1,0:T(8,128)(2,1)S(1)} %get-tuple-element.74.refs_6_) | copy-start | bytes 15728644
  152.7 2.4 %copy-start.3 = (bf16[160,128,128]{2,1,0:T(8,128)(2,1)}, bf16[160,128,128]{2,1,0:T(8,128)(2,1)S(1)}, u32[]{:S(2)}) copy-start(bf16[160,128,128]{2,1,0:T(8,128)(2,1)S(1)} %get-tuple-element.75.refs_7_) | copy-start | bytes 15728644
  158.8 2.5 %copy-start.1 = (bf16[160,128,128]{2,1,0:T(8,128)(2,1)S(1)}, bf16[160,128,128]{2,1,0:T(8,128)(2,1)}, u32[]{:S(2)}) copy-start(bf16[160,128,128]{2,1,0:T(8,128)(2,1)} %copy-done) | copy-start | bytes 15728644
  161.3 2.5 %copy-start.4 = (bf16[160,128,128]{2,1,0:T(8,128)(2,1)S(1)}, bf16[160,128,128]{2,1,0:T(8,128)(2,1)}, u32[]{:S(2)}) copy-start(bf16[160,128,128]{2,1,0:T(8,128)(2,1)} %copy-done.3) | copy-start | bytes 15728644
  163.8 6.2 %copy-start.2 = (bf16[160,128,128]{2,1,0:T(8,128)(2,1)S(1)}, bf16[160,128,128]{2,1,0:T(8,128)(2,1)}, u32[]{:S(2)}) copy-start(bf16[160,128,128]{2,1,0:T(8,128)(2,1)} %copy-done) | copy-start | bytes 15728644
  163.8 6.2 %copy-start.5 = (bf16[160,128,128]{2,1,0:T(8,128)(2,1)S(1)}, bf16[160,128,128]{2,1,0:T(8,128)(2,1)}, u32[]{:S(2)}) copy-start(bf16[160,128,128]{2,1,0:T(8,128)(2,1)} %copy-done.3) | copy-start | bytes 15728644
Sparse Core Ops, SparseCore 0:
  60.4 41.3 all-gather.2
  103.5 32.1 all-gather.4

commit v4 on v2

--- a/solution.py
+++ b/solution.py
@@ -23,7 +23,7 @@
 ROWS = 160
 TOKENS = 4 * ROWS
 HALF = 512
-SLOTS = 64
+SLOTS = 56
 PART = 512
 FIRST = 768
 
@@ -393,18 +393,29 @@
     earlier = order[:, None] < order[None, :]
     same_id = paired[:, :, None] == paired[:, None, :]
     first = ~jnp.any(same_id & earlier[None], axis=1)
-    first_owner = jnp.where(first, owners, -1)
-    ranks = jnp.sum(
-        ((first_owner[:, :, None] == owners[:, None, :]) & earlier[None]).astype(jnp.int32), axis=1
-    )
-    rounds = (jnp.max(jnp.where(first, ranks, 0)) + SLOTS) // SLOTS
+    counts = jnp.sum(
+        (first[:, None, :] & (owners[:, None, :] == jnp.arange(OWNERS)[None, :, None])).astype(
+            jnp.int32
+        ),
+        axis=2,
+    )
+    rounds = (jnp.max(counts) + SLOTS - 1) // SLOTS
+
+    def ranks_in(chosen):
+        return jnp.dot(
+            chosen.astype(jnp.bfloat16),
+            earlier.astype(jnp.bfloat16),
+            preferred_element_type=jnp.float32,
+        ).astype(jnp.int32)
 
     local = paired - fsdp_index * vocab_rows
-    sent_rank = jnp.where(first_owner == fsdp_index, ranks, -1)
+    sent = first & (owners == fsdp_index)
+    sent_rank = jnp.where(sent, ranks_in(sent), -1)
     own_ids = lax.dynamic_index_in_dim(paired, pair, 0, keepdims=False)
     own_first = lax.dynamic_index_in_dim(first, pair, 0, keepdims=False)
-    own_ranks = lax.dynamic_index_in_dim(ranks, pair, 0, keepdims=False)
     own_owners = lax.dynamic_index_in_dim(owners, pair, 0, keepdims=False)
+    by_owner = own_first[None, :] & (own_owners[None, :] == jnp.arange(OWNERS)[:, None])
+    own_ranks = jnp.sum(jnp.where(by_owner, ranks_in(by_owner), 0), axis=0)
     got_rank = jnp.sum(
         jnp.where(
             (own_ids[:, None] == own_ids[None, :]) & own_first[:, None], own_ranks[:, None], 0
@@ -438,13 +449,15 @@
 
     rows = exchanged(wanted_rows(0))
     queries, rollout, rows = lax.optimization_barrier((queries, rollout, rows))
-    packed = pack_columns(queries, rollout[:, :1024], rollout[:, 1024:])
-    own = placed_rows(0, rows)
-    weights = []
-    for part in packed:
+    first_part, second_part = pack_columns(queries, rollout[:, :1024], rollout[:, 1024:])
+
+    def gathered(part):
         part = lax.all_to_all(part, TP, split_axis=0, concat_axis=0)
         part = lax.all_gather(part.reshape(HALF, part.shape[-1]), ("z", "c"))
-        weights.append(part.reshape(8 * HALF, part.shape[-1]))
+        return part.reshape(8 * HALF, part.shape[-1])
+
+    weights = [gathered(first_part), gathered(second_part)]
+    own = placed_rows(0, rows)
     _, own = lax.while_loop(
         lambda state: state[0] < rounds,
         lambda state: (state[0] + 1, state[1] + placed_rows(state[0], exchanged(wanted_rows(state[0])))),

time: 181 us -> 176 us (0.972)
  local copies, waits for them, and re-layouts: 19.7 us -> 16 us
  other arithmetic: 10.7 us -> 7.35 us
    unnamed x41 -> x35, local copies, waits for them, and re-layouts: 8.06 us -> 4.44 us
    ppermute x13, waiting for transfers between devices: 30.9 us -> 33.8 us  [send(): return lax.ppermute(array, NAMES, pairs_of(move))]
    reduce_sum x1, other arithmetic: 2.67 us -> 0.22 us  [per_device(): jnp.sum((first[:, None, :] & (owners[:, None, :] == jnp.arange(OWNERS)[No...]
  transfers between devices with their start and end apart: 16 -> 16, of which waited for: 6 -> 6; matrix products, arithmetic and copies ran while one was open for 20% -> 18% of each run, Pallas kernels for 11% -> 12%
where the time goes in v4:
time: 176 us; the launch traced here: 175 us
  waiting for transfers between devices  43.6 us (25%)
  blocking collectives  29.8 us (17%)
  starting transfers between devices  26.8 us (15%)
  Pallas kernels  26.3 us (15%)
  local copies, waits for them, and re-layouts  16 us (9%)
  between operations  15.2 us (9%)
  matrix products  9.5 us (5%)
  other arithmetic  7.35 us (4%)
    ppermute x13, waiting for transfers between devices, send(): return lax.ppermute(array, NAMES, pairs_of(move))  33.8 us
    all_to_all x2, blocking collectives, gathered(): part = lax.all_to_all(part, TP, split_axis=0, concat_axis=0)  29.8 us
    ppermute x13, starting transfers between devices, send(): return lax.ppermute(array, NAMES, pairs_of(move))  18.9 us
    pallas_call x2, Pallas kernels, attend(): pl.pallas_call(functools.partial(attend_kernel, first), grid=(ROWS // BLO...  13.2 us
    pallas_call x1, Pallas kernels, project(): pl.pallas_call(project_kernel, grid_spec=pltpu.PrefetchScalarGridSpec(num...  12.2 us
    all_to_all x1, waiting for transfers between devices, exchanged(): return lax.all_to_all(rows, FSDP, split_axis=0, concat_axis=0)  9.8 us
    gather x1, local copies, waits for them, and re-layouts, wanted_rows(): rows = embedding.at[wanted.reshape(-1)].get(mode='promise_in_bounds')  7.82 us
    all_to_all x1, starting transfers between devices, exchanged(): return lax.all_to_all(rows, FSDP, split_axis=0, concat_axis=0)  7.77 us
  transfers between devices with their start and end apart: 16, of which 6 were waited for; matrix products, arithmetic and copies ran while one was open for 18% of the time, Pallas kernels for 12%

profile of v4, /device:TPU:64, one launch (start us, length us, event | category | flops | bytes accessed | tf_op | source)
XLA Modules:
  0.0 174.5 jit_solution(8296077283691042874)
XLA Ops:
  7.2 1.9 %collective-permute-start = (bf16[64,8192]{1,0:T(8,128)(2,1)}, bf16[64,8192]{1,0:T(8,128)(2,1)S(1)}, u32[]{:S(2)}, u32[]{:S(2)}) collective-permute-start(bf16[64,8192]{1,0:T(8,128)(2,1)} %param.17), channel_id=1, source_target_pairs={{0,0},{1,1},{2,2},{3,3},{4,4},{5,5},{6,6},{7,7},{8,64},{9,65},{10,... | collective-permute-start | bytes 3145736 | tf_op jit(solution)/shard_map/ppermute | solution.py:47
  9.0 0.1 iota_compare_fusion.8
  9.2 0.8 reshape.233
  10.0 0.1 reshape.234
  10.2 2.7 %and_reduce_fusion = pred[8,640]{1,0:T(8,128)(4,1)S(1)} fusion(s32[8,640]{1,0:T(8,128)S(1)} %reshape.234, pred[640,640]{1,0:T(8,128)(4,1)S(1)} %iota_compare_fusion.8), kind=kLoop, calls=%fused_computation.12 | loop fusion | flops 9825280 | bytes 435200 | tf_op jit(solution)/shard_map/reduce_or | solution.py:395
  12.8 0.2 fusion.9
  13.0 0.2 select_reduce_fusion.2
  13.3 0.1 reshape.235
  13.4 7.8 %gather_fusion.1 = bf16[448,1024]{1,0:T(8,128)(2,1)S(1)} fusion(bf16[4752,1024]{1,0:T(8,128)(2,1)} %param.15, s32[1024]{0:T(1024)S(1)} %pad_clamp_fusion.1), kind=kCustom, calls=%fused_computation.1 | custom fusion | bytes 1836800 | tf_op jit(solution)/shard_map/gather | solution.py:432
  21.2 0.7 reshape.236
  21.9 0.0 copy-start.1
  21.9 1.1 copy.55
  23.0 7.8 %all-to-all-start.1 = ((bf16[16,56,512]{2,1,0:T(8,128)(2,1)}), bf16[16,56,512]{2,1,0:T(8,128)(2,1)}, u32[]{:S(2)}, u32[]{:S(2)}) async-start(bf16[16,56,512]{2,1,0:T(8,128)(2,1)} %bitcast.18), calls=%async_computation.1 | async-start | bytes 1835008 | tf_op jit(solution)/shard_map/all_to_all | solution.py:437
  30.8 0.0 all-gather.3.cloned.1.call-start
  30.8 2.1 %fusion.24 = (bf16[64,2,1024]{2,0,1:T(8,128)(2,1)S(1)}, f32[64,2,1024]{2,0,1:T(8,128)S(1)}, f32[64,2,1024]{2,0,1:T(8,128)S(1)}, f32[64,2,1024]{2,0,1:T(8,128)S(1)}) fusion(f32[64,2,1024]{2,1,0:T(2,128)S(1)} %copy-done.1, bf16[64,2,1024]{2,1,0:T(2,128)(2,1)} %param.23, f32[64,2,1024]{2,1,0:T(2,128)} %param.21, f32[64,2,1024]{2,1,0:T(2,128)} %param.22), kind=kLoop, calls=%fused_computation.72 | loop fusion | flops 2228224 | bytes 3670016 | tf_op jit(solution)/shard_map/convert_element_type | solution.py:386
  33.0 0.7 collective-permute-start.1
  33.6 0.0 collective-permute-done.1
  33.7 9.8 %all-to-all-done.1 = bf16[16,56,512]{2,1,0:T(8,128)(2,1)} async-done(((bf16[16,56,512]{2,1,0:T(8,128)(2,1)}), bf16[16,56,512]{2,1,0:T(8,128)(2,1)}, u32[]{:S(2)}, u32[]{:S(2)}) %all-to-all-start.1) | async-done | bytes 917536 | tf_op jit(solution)/shard_map/all_to_all | solution.py:437
  43.5 0.0 collective-permute-done.query_ref
  43.5 0.1 shard_map.147
  43.6 16.6 %all_to_all.21 = bf16[8,64,768]{2,1,0:T(8,128)(2,1)} all-to-all(bf16[8,64,768]{2,1,0:T(8,128)(2,1)S(1)} %get-tuple-element.67), channel_id=1, replica_groups=mesh['xh'=2,'z'=4,'c'=2,'y'=4,'xl'=2] {'y','xl'}, dimensions={0} | all-to-all | bytes 1572864 | tf_op jit(solution)/shard_map/all_to_all | solution.py:455
  60.2 0.0 all-gather.3.cloned.1.call-update
  60.3 0.0 all-gather.5.cloned.1.call-start
  60.3 13.2 %all_to_all.22 = bf16[8,64,512]{2,1,0:T(8,128)(2,1)} all-to-all(bf16[8,64,512]{2,1,0:T(8,128)(2,1)S(1)} %get-tuple-element.69), channel_id=1, replica_groups=mesh['xh'=2,'z'=4,'c'=2,'y'=4,'xl'=2] {'y','xl'}, dimensions={0} | all-to-all | bytes 1048576 | tf_op jit(solution)/shard_map/all_to_all | solution.py:455
  73.5 0.0 all-gather.5.cloned.1.call-update
  73.5 0.2 convert_reduce_fusion
  73.7 0.6 reduce_max.9
  75.1 0.2 fusion.8
  75.3 0.4 select_reduce_fusion.1
  75.8 2.9 %fusion.5 = bf16[640,512]{1,0:T(8,128)(2,1)} fusion(bf16[896,512]{1,0:T(8,128)(2,1)} %bitcast.19, s32[640]{0:T(1024)S(1)} %add_select_fusion.2), kind=kOutput, calls=%fused_computation.17 | convolution fusion | flops 588103680 | bytes 1575424 | tf_op jit(solution)/shard_map/dot_general | solution.py:444
  78.7 3.2 %collective-permute-start.4 = (bf16[640,512]{1,0:T(8,128)(2,1)}, bf16[640,512]{1,0:T(8,128)(2,1)S(1)}, u32[]{:S(2)}, u32[]{:S(2)}) collective-permute-start(bf16[640,512]{1,0:T(8,128)(2,1)} %get-tuple-element.64.refs_0_), channel_id=1, source_target_pairs={{0,6},{1,7},{2,0},{3,1},{4,2},{5,3},{6,4},{7,5},{8,14},{9,15},{10,... | collective-permute-start | bytes 1966088 | tf_op jit(solution)/shard_map/ppermute | solution.py:47
  81.9 0.8 collective-permute-start.2
  82.8 1.2 copy.56
  84.0 1.2 copy.57
  85.2 1.2 copy.58
  86.4 0.7 stack.39.place_ref
  87.0 10.3 %collective-permute-done.3.refs_2_ = bf16[640,512]{1,0:T(8,128)(2,1)S(1)} collective-permute-done((bf16[640,512]{1,0:T(8,128)(2,1)}, bf16[640,512]{1,0:T(8,128)(2,1)S(1)}, u32[]{:S(2)}, u32[]{:S(2)}) %collective-permute-start.3) | collective-permute-done | bytes 655392 | tf_op jit(solution)/shard_map/ppermute | solution.py:47
  97.4 0.1 collective-permute-start.7
  97.5 3.4 %collective-permute-start.8 = (bf16[320,512]{1,0:T(8,128)(2,1)S(1)}, bf16[320,512]{1,0:T(8,128)(2,1)S(1)}, u32[]{:S(2)}, u32[]{:S(2)}) collective-permute-start(bf16[320,512]{1,0:T(8,128)(2,1)S(1)} %slice.39), channel_id=1, source_target_pairs={{0,6},{1,7},{2,0},{3,1},{4,2},{5,3},{6,4},{7,5},{8,14},{9,15},{10,... | collective-permute-start | bytes 983048 | tf_op jit(solution)/shard_map/ppermute | solution.py:47
  100.9 3.2 %collective-permute-start.6 = (bf16[640,512]{1,0:T(8,128)(2,1)}, bf16[640,512]{1,0:T(8,128)(2,1)S(1)}, u32[]{:S(2)}, u32[]{:S(2)}) collective-permute-start(bf16[640,512]{1,0:T(8,128)(2,1)} %collective-permute-done.2.refs_1_), channel_id=1, source_target_pairs={{0,6},{1,7},{2,0},{3,1},{4,2},{5,3},{6,4},{7,5},{8,14},{9,15},{10,... | collective-permute-start | bytes 1966088 | tf_op jit(solution)/shard_map/ppermute | solution.py:47
  104.2 5.1 %collective-permute-done.7.refs_6_ = bf16[320,512]{1,0:T(8,128)(2,1)S(1)} collective-permute-done((bf16[320,512]{1,0:T(8,128)(2,1)S(1)}, bf16[320,512]{1,0:T(8,128)(2,1)S(1)}, u32[]{:S(2)}, u32[]{:S(2)}) %collective-permute-start.7) | collective-permute-done | bytes 327712 | tf_op jit(solution)/shard_map/ppermute | solution.py:47
  109.2 0.9 collective-permute-start.9
  110.1 0.0 collective-permute-done.8.refs_7_
  110.1 1.2 collective-permute-start.10
  111.3 0.6 fusion.14
  111.9 0.2 pad_maximum_fusion.1
  112.1 10.4 %collective-permute-done.5.refs_4_ = bf16[640,512]{1,0:T(8,128)(2,1)S(1)} collective-permute-done((bf16[640,512]{1,0:T(8,128)(2,1)}, bf16[640,512]{1,0:T(8,128)(2,1)S(1)}, u32[]{:S(2)}, u32[]{:S(2)}) %collective-permute-start.5) | collective-permute-done | bytes 655392 | tf_op jit(solution)/shard_map/ppermute | solution.py:47
  122.5 0.0 collective-permute-done.6.refs_5_
  122.5 0.8 copy-done.12
  123.3 1.2 collective-permute-done.10.refs_9_
  124.5 12.2 %shard_map.148 = (f32[320,896]{1,0:T(8,128)}, bf16[320,896]{1,0:T(8,128)(2,1)}, bf16[640,4096]{1,0:T(8,128)(2,1)}) custom-call(s32[9]{0:T(128)} %stack.39.place_ref, bf16[640,512]{1,0:T(8,128)(2,1)} %get-tuple-element.64.refs_0_, bf16[640,512]{1,0:T(8,128)(2,1)} %collective-permute-done.2.refs_1_, bf16[640,512]{1,0:T(8,128)(2,1)} %copy-done.2, ...), custom_call_target="tpu_custom_call" | custom-call | flops 4026531840 | bytes 12582912 | tf_op jit(solution)/shard_map/pallas_call | solution.py:171
  136.7 0.1 collective-permute-start.12
  136.8 0.0 all-gather.5.cloned.1.call-done
  136.8 0.0 slice-start
  136.8 0.0 slice-start.2
  136.9 6.2 %fusion.29 = f32[640,512]{1,0:T(8,128)S(1)} fusion(bf16[640,4096]{1,0:T(8,128)(2,1)} %get-tuple-element.68, bf16[4096,512]{1,0:T(8,128)(2,1)} %bitcast.66), kind=kOutput, calls=%fused_computation.75 | convolution fusion | flops 2684354560 | bytes 10747904 | tf_op jit(solution)/shard_map/dot_general | solution.py:504
  143.1 0.1 dynamic-slice_convert_fusion
  143.1 3.5 %collective-permute-start.11 = (bf16[320,512]{1,0:T(8,128)(2,1)S(1)}, bf16[320,512]{1,0:T(8,128)(2,1)S(1)}, u32[]{:S(2)}, u32[]{:S(2)}) collective-permute-start(bf16[320,512]{1,0:T(8,128)(2,1)S(1)} %dynamic-slice_convert_fusion), channel_id=1, source_target_pairs={{0,64},{1,65},{2,66},{3,67},{4,68},{5,69},{6,70},{7,71},{8,72},{9,... | collective-permute-start | bytes 983048 | tf_op jit(solution)/shard_map/ppermute | solution.py:47
  146.7 0.1 fusion.13
  146.8 0.8 shard_map.149
  147.6 0.1 constant_dynamic-slice_fusion
  147.7 6.7 %collective-permute-done.12 = bf16[320,896]{1,0:T(8,128)(2,1)S(1)} collective-permute-done((bf16[320,896]{1,0:T(8,128)(2,1)}, bf16[320,896]{1,0:T(8,128)(2,1)S(1)}, u32[]{:S(2)}, u32[]{:S(2)}) %collective-permute-start.12) | collective-permute-done | bytes 573472 | tf_op jit(solution)/shard_map/ppermute | solution.py:47
  154.5 7.1 %shard_map.150 = (bf16[2,160,1024]{2,1,0:T(8,128)(2,1)}, bf16[2,160,128]{2,1,0:T(8,128)(2,1)S(1)}, bf16[2,160,128]{2,1,0:T(8,128)(2,1)S(1)}, f32[2,160,128]{2,1,0:T(8,128)S(1)}) custom-call(f32[2,160,896]{2,1,0:T(8,128)S(1)} %bitcast.55, bf16[2,160,896]{2,1,0:T(8,128)(2,1)S(1)} %bitcast.56, f32[1,768]{1,0:T(1,128)S(1)} %broadcast_in_dim.111.refs_2_, ...), custom_call_target="tpu_custom_call" | custom-call | flops 83886080 | bytes 12582912 | tf_op jit(solution)/shard_map/pallas_call | solution.py:349
  161.6 6.1 %shard_map.151 = bf16[2,160,1024]{2,1,0:T(8,128)(2,1)} custom-call(f32[2,160,512]{2,1,0:T(8,128)S(1)} %bitcast.54, bf16[2,160,512]{2,1,0:T(8,128)(2,1)S(1)} %bitcast.57, f32[1,512]{1,0:T(1,128)S(1)} %bitcast.58, f32[2,160,128]{2,1,0:T(8,128)S(1)} %get-tuple-element.129.refs_3_, ...), custom_call_target="tpu_custom_call", output_to_operand_aliasing={{}: (11, {})} | custom-call | flops 83886080 | bytes 12582912 | tf_op jit(solution)/shard_map/pallas_call | solution.py:349
  (58 shorter events, 0.4 us)
Async XLA Ops:
  7.2 36.3 %collective-permute-start = (bf16[64,8192]{1,0:T(8,128)(2,1)}, bf16[64,8192]{1,0:T(8,128)(2,1)S(1)}, u32[]{:S(2)}, u32[]{:S(2)}) collective-permute-start(bf16[64,8192]{1,0:T(8,128)(2,1)} %param.17), channel_id=1, source_target_pairs={{0,0},{1,1},{2,2},{3,3},{4,4},{5,5},{6,6},{7,7},{8,64},{9,65},{10,... | collective-permute-start | bytes 3145736 | tf_op jit(solution)/shard_map/ppermute | solution.py:47
  21.9 8.9 %copy-start.1 = (f32[64,2,1024]{2,1,0:T(2,128)S(1)}, f32[64,2,1024]{2,1,0:T(2,128)}, u32[]{:S(2)}) copy-start(f32[64,2,1024]{2,1,0:T(2,128)} %param.20) | copy-start | bytes 1572868
  23.0 20.4 %all-to-all-start.1 = ((bf16[16,56,512]{2,1,0:T(8,128)(2,1)}), bf16[16,56,512]{2,1,0:T(8,128)(2,1)}, u32[]{:S(2)}, u32[]{:S(2)}) async-start(bf16[16,56,512]{2,1,0:T(8,128)(2,1)} %bitcast.18), calls=%async_computation.1 | async-start | bytes 1835008 | tf_op jit(solution)/shard_map/all_to_all | solution.py:437
  30.8 93.7 %all-gather.3.cloned.1.call-start = ((), (), s32[]{:S(2)}) async-start(), calls=%async_computation.4 | async-start | bytes 7077888 | tf_op jit(solution)/shard_map/all_gather | solution.py:456
  33.0 0.7 collective-permute-start.1
  60.3 76.6 %all-gather.5.cloned.1.call-start = ((), (), s32[]{:S(2)}) async-start(), calls=%async_computation.5 | async-start | bytes 4718592 | tf_op jit(solution)/shard_map/all_gather | solution.py:456
  78.7 4.1 %copy-start.13 = (bf16[2,128]{1,0:T(2,128)(2,1)S(1)}, bf16[2,128]{1,0:T(2,128)(2,1)}, u32[]{:S(2)}) copy-start(bf16[2,128]{1,0:T(2,128)(2,1)} %param.19) | copy-start | bytes 1540
  78.7 4.1 %copy-start.4 = (bf16[1024]{0:T(1024)(128)(2,1)S(1)}, bf16[1024]{0:T(1024)(128)(2,1)}, u32[]{:S(2)}) copy-start(bf16[1024]{0:T(1024)(128)(2,1)} %param.18) | copy-start | bytes 6148
  78.7 18.7 %collective-permute-start.3 = (bf16[640,512]{1,0:T(8,128)(2,1)}, bf16[640,512]{1,0:T(8,128)(2,1)S(1)}, u32[]{:S(2)}, u32[]{:S(2)}) collective-permute-start(bf16[640,512]{1,0:T(8,128)(2,1)} %get-tuple-element.64.refs_0_), channel_id=1, source_target_pairs={{0,2},{1,3},{2,4},{3,5},{4,6},{5,7},{6,0},{7,1},{8,10},{9,11},{10,... | collective-permute-start | bytes 1966088 | tf_op jit(solution)/shard_map/ppermute | solution.py:47
  78.7 18.8 %collective-permute-start.4 = (bf16[640,512]{1,0:T(8,128)(2,1)}, bf16[640,512]{1,0:T(8,128)(2,1)S(1)}, u32[]{:S(2)}, u32[]{:S(2)}) collective-permute-start(bf16[640,512]{1,0:T(8,128)(2,1)} %get-tuple-element.64.refs_0_), channel_id=1, source_target_pairs={{0,6},{1,7},{2,0},{3,1},{4,2},{5,3},{6,4},{7,5},{8,14},{9,15},{10,... | collective-permute-start | bytes 1966088 | tf_op jit(solution)/shard_map/ppermute | solution.py:47
  81.9 19.0 %collective-permute-start.2 = (bf16[640,512]{1,0:T(8,128)(2,1)}, bf16[640,512]{1,0:T(8,128)(2,1)}, u32[]{:S(2)}, u32[]{:S(2)}) collective-permute-start(bf16[640,512]{1,0:T(8,128)(2,1)} %get-tuple-element.64.refs_0_), channel_id=1, source_target_pairs={{0,1},{1,0},{2,3},{3,2},{4,5},{5,4},{6,7},{7,6},{8,9},{9,8},{10,11... | collective-permute-start | bytes 1966088 | tf_op jit(solution)/shard_map/ppermute | solution.py:47
  84.0 20.2 %copy-start.5 = (s32[160]{0:T(256)S(1)}, s32[160]{0:T(256)}, u32[]{:S(2)}) copy-start(s32[160]{0:T(256)} %param.16) | copy-start | bytes 1924
  97.4 27.1 %copy-start.2 = (bf16[640,512]{1,0:T(8,128)(2,1)}, bf16[640,512]{1,0:T(8,128)(2,1)S(1)}, u32[]{:S(2)}) copy-start(bf16[640,512]{1,0:T(8,128)(2,1)S(1)} %collective-permute-done.3.refs_2_) | copy-start | bytes 1966084
  97.4 11.8 %collective-permute-start.7 = (bf16[320,512]{1,0:T(8,128)(2,1)S(1)}, bf16[320,512]{1,0:T(8,128)(2,1)S(1)}, u32[]{:S(2)}, u32[]{:S(2)}) collective-permute-start(bf16[320,512]{1,0:T(8,128)(2,1)S(1)} %slice.38), channel_id=1, source_target_pairs={{0,2},{1,3},{2,4},{3,5},{4,6},{5,7},{6,0},{7,1},{8,10},{9,11},{10,... | collective-permute-start | bytes 983048 | tf_op jit(solution)/shard_map/ppermute | solution.py:47
  97.5 27.0 %copy-start.3 = (bf16[640,512]{1,0:T(8,128)(2,1)}, bf16[640,512]{1,0:T(8,128)(2,1)S(1)}, u32[]{:S(2)}) copy-start(bf16[640,512]{1,0:T(8,128)(2,1)S(1)} %collective-permute-done.4.refs_3_) | copy-start | bytes 1966084
  97.5 12.6 %collective-permute-start.8 = (bf16[320,512]{1,0:T(8,128)(2,1)S(1)}, bf16[320,512]{1,0:T(8,128)(2,1)S(1)}, u32[]{:S(2)}, u32[]{:S(2)}) collective-permute-start(bf16[320,512]{1,0:T(8,128)(2,1)S(1)} %slice.39), channel_id=1, source_target_pairs={{0,6},{1,7},{2,0},{3,1},{4,2},{5,3},{6,4},{7,5},{8,14},{9,15},{10,... | collective-permute-start | bytes 983048 | tf_op jit(solution)/shard_map/ppermute | solution.py:47
  100.9 21.6 %collective-permute-start.5 = (bf16[640,512]{1,0:T(8,128)(2,1)}, bf16[640,512]{1,0:T(8,128)(2,1)S(1)}, u32[]{:S(2)}, u32[]{:S(2)}) collective-permute-start(bf16[640,512]{1,0:T(8,128)(2,1)} %collective-permute-done.2.refs_1_), channel_id=1, source_target_pairs={{0,2},{1,3},{2,4},{3,5},{4,6},{5,7},{6,0},{7,1},{8,10},{9,11},{10,... | collective-permute-start | bytes 1966088 | tf_op jit(solution)/shard_map/ppermute | solution.py:47
  100.9 21.6 %collective-permute-start.6 = (bf16[640,512]{1,0:T(8,128)(2,1)}, bf16[640,512]{1,0:T(8,128)(2,1)S(1)}, u32[]{:S(2)}, u32[]{:S(2)}) collective-permute-start(bf16[640,512]{1,0:T(8,128)(2,1)} %collective-permute-done.2.refs_1_), channel_id=1, source_target_pairs={{0,6},{1,7},{2,0},{3,1},{4,2},{5,3},{6,4},{7,5},{8,14},{9,15},{10,... | collective-permute-start | bytes 1966088 | tf_op jit(solution)/shard_map/ppermute | solution.py:47
  109.2 15.3 %copy-start.10 = (bf16[320,512]{1,0:T(8,128)(2,1)}, bf16[320,512]{1,0:T(8,128)(2,1)S(1)}, u32[]{:S(2)}) copy-start(bf16[320,512]{1,0:T(8,128)(2,1)S(1)} %collective-permute-done.7.refs_6_) | copy-start | bytes 983044
  109.2 13.3 %collective-permute-start.9 = (bf16[320,512]{1,0:T(8,128)(2,1)S(1)}, bf16[320,512]{1,0:T(8,128)(2,1)S(1)}, u32[]{:S(2)}, u32[]{:S(2)}) collective-permute-start(bf16[320,512]{1,0:T(8,128)(2,1)S(1)} %collective-permute-done.7.refs_6_), channel_id=1, source_target_pairs={{0,1},{1,0},{2,3},{3,2},{4,5},{5,4},{6,7},{7,6},{8,9},{9,8},{10,11... | collective-permute-start | bytes 983048 | tf_op jit(solution)/shard_map/ppermute | solution.py:47
  110.1 12.4 %copy-start.11 = (bf16[320,512]{1,0:T(8,128)(2,1)}, bf16[320,512]{1,0:T(8,128)(2,1)S(1)}, u32[]{:S(2)}) copy-start(bf16[320,512]{1,0:T(8,128)(2,1)S(1)} %collective-permute-done.8.refs_7_) | copy-start | bytes 983044
  110.1 14.4 %collective-permute-start.10 = (bf16[320,512]{1,0:T(8,128)(2,1)S(1)}, bf16[320,512]{1,0:T(8,128)(2,1)}, u32[]{:S(2)}, u32[]{:S(2)}) collective-permute-start(bf16[320,512]{1,0:T(8,128)(2,1)S(1)} %collective-permute-done.8.refs_7_), channel_id=1, source_target_pairs={{0,1},{1,0},{2,3},{3,2},{4,5},{5,4},{6,7},{7,6},{8,9},{9,8},{10,11... | collective-permute-start | bytes 983048 | tf_op jit(solution)/shard_map/ppermute | solution.py:47
  122.5 2.0 %copy-start.6 = (bf16[640,512]{1,0:T(8,128)(2,1)}, bf16[640,512]{1,0:T(8,128)(2,1)S(1)}, u32[]{:S(2)}) copy-start(bf16[640,512]{1,0:T(8,128)(2,1)S(1)} %collective-permute-done.5.refs_4_) | copy-start | bytes 1966084
  122.5 2.0 %copy-start.7 = (bf16[640,512]{1,0:T(8,128)(2,1)}, bf16[640,512]{1,0:T(8,128)(2,1)S(1)}, u32[]{:S(2)}) copy-start(bf16[640,512]{1,0:T(8,128)(2,1)S(1)} %collective-permute-done.6.refs_5_) | copy-start | bytes 1966084
  122.5 0.8 copy-start.12
  136.7 17.7 %collective-permute-start.12 = (bf16[320,896]{1,0:T(8,128)(2,1)}, bf16[320,896]{1,0:T(8,128)(2,1)S(1)}, u32[]{:S(2)}, u32[]{:S(2)}) collective-permute-start(bf16[320,896]{1,0:T(8,128)(2,1)} %get-tuple-element.70), channel_id=1, source_target_pairs={{0,64},{1,65},{2,66},{3,67},{4,68},{5,69},{6,70},{7,71},{8,72},{9,... | collective-permute-start | bytes 1720328 | tf_op jit(solution)/shard_map/ppermute | solution.py:47
  136.8 9.9 %slice-start = ((s8[5242880]{0:T(1024)(128)(4,1)}), s8[4194304]{0:T(1024)(128)(4,1)S(1)}, s32[]{:S(2)}) async-start(s8[5242880]{0:T(1024)(128)(4,1)} %bitcast.50), calls=%async_computation.6 | async-start | bytes 8388608
  136.8 9.9 %slice-start.2 = ((s8[5242880]{0:T(1024)(128)(4,1)}), s8[4194304]{0:T(1024)(128)(4,1)S(1)}, s32[]{:S(2)}) async-start(s8[5242880]{0:T(1024)(128)(4,1)} %bitcast.52), calls=%async_computation.8 | async-start | bytes 8388608
  136.9 9.9 %slice-start.1 = ((s8[5242880]{0:T(1024)(128)(4,1)}), s8[1048576]{0:T(1024)(128)(4,1)S(1)}, s32[]{:S(2)}) async-start(s8[5242880]{0:T(1024)(128)(4,1)} %bitcast.50), calls=%async_computation.7 | async-start | bytes 2097152
  136.9 9.9 %slice-start.3 = ((s8[5242880]{0:T(1024)(128)(4,1)}), s8[1048576]{0:T(1024)(128)(4,1)S(1)}, s32[]{:S(2)}) async-start(s8[5242880]{0:T(1024)(128)(4,1)} %bitcast.52), calls=%async_computation.9 | async-start | bytes 2097152
  143.1 18.5 %collective-permute-start.11 = (bf16[320,512]{1,0:T(8,128)(2,1)S(1)}, bf16[320,512]{1,0:T(8,128)(2,1)S(1)}, u32[]{:S(2)}, u32[]{:S(2)}) collective-permute-start(bf16[320,512]{1,0:T(8,128)(2,1)S(1)} %dynamic-slice_convert_fusion), channel_id=1, source_target_pairs={{0,64},{1,65},{2,66},{3,67},{4,68},{5,69},{6,70},{7,71},{8,72},{9,... | collective-permute-start | bytes 983048 | tf_op jit(solution)/shard_map/ppermute | solution.py:47
  147.6 6.8 %copy-start = (f32[320,896]{1,0:T(8,128)S(1)}, f32[320,896]{1,0:T(8,128)}, u32[]{:S(2)}) copy-start(f32[320,896]{1,0:T(8,128)} %get-tuple-element.75) | copy-start | bytes 3440644
Sparse Core Ops, SparseCore 0:
  60.4 41.3 all-gather.2
  103.5 32.1 all-gather.4

commit v5 on v4

--- a/solution.py
+++ b/solution.py
@@ -225,7 +225,7 @@
     )(k_cache, v_cache)
 
 
-BLOCK = 32
+BLOCK = 80
 
 
 def spread(scratch, array):

time: 176 us -> 174 us (0.989)
  Pallas kernels: 26.3 us -> 24.4 us
    pallas_call x2, Pallas kernels: 13.2 us -> 11.4 us  [attend(): pl.pallas_call(functools.partial(attend_kernel, first), grid=(ROWS // BLO...]
  transfers between devices with their start and end apart: 16 -> 16, of which waited for: 6 -> 6; matrix products, arithmetic and copies ran while one was open for 18% -> 19% of each run, Pallas kernels for 12% -> 11%
where the time goes in v5:
time: 174 us; the launch traced here: 173 us
  waiting for transfers between devices  43.6 us (25%)
  blocking collectives  29.8 us (17%)
  starting transfers between devices  26.8 us (15%)
  Pallas kernels  24.4 us (14%)
  local copies, waits for them, and re-layouts  16 us (9%)
  between operations  15.2 us (9%)
  matrix products  9.5 us (5%)
  other arithmetic  7.35 us (4%)
    ppermute x13, waiting for transfers between devices, send(): return lax.ppermute(array, NAMES, pairs_of(move))  33.8 us
    all_to_all x2, blocking collectives, gathered(): part = lax.all_to_all(part, TP, split_axis=0, concat_axis=0)  29.8 us
    ppermute x13, starting transfers between devices, send(): return lax.ppermute(array, NAMES, pairs_of(move))  18.9 us
    pallas_call x1, Pallas kernels, project(): pl.pallas_call(project_kernel, grid_spec=pltpu.PrefetchScalarGridSpec(num...  12.2 us
    pallas_call x2, Pallas kernels, attend(): pl.pallas_call(functools.partial(attend_kernel, first), grid=(ROWS // BLO...  11.4 us
    all_to_all x1, waiting for transfers between devices, exchanged(): return lax.all_to_all(rows, FSDP, split_axis=0, concat_axis=0)  9.8 us
    gather x1, local copies, waits for them, and re-layouts, wanted_rows(): rows = embedding.at[wanted.reshape(-1)].get(mode='promise_in_bounds')  7.82 us
    all_to_all x1, starting transfers between devices, exchanged(): return lax.all_to_all(rows, FSDP, split_axis=0, concat_axis=0)  7.77 us
  transfers between devices with their start and end apart: 16, of which 6 were waited for; matrix products, arithmetic and copies ran while one was open for 19% of the time, Pallas kernels for 11%

profile of v5, /device:TPU:64, one launch (start us, length us, event | category | flops | bytes accessed | tf_op | source)
XLA Modules:
  0.0 172.7 jit_solution(5386332798194338847)
XLA Ops:
  7.2 1.9 %collective-permute-start = (bf16[64,8192]{1,0:T(8,128)(2,1)}, bf16[64,8192]{1,0:T(8,128)(2,1)S(1)}, u32[]{:S(2)}, u32[]{:S(2)}) collective-permute-start(bf16[64,8192]{1,0:T(8,128)(2,1)} %param.17), channel_id=1, source_target_pairs={{0,0},{1,1},{2,2},{3,3},{4,4},{5,5},{6,6},{7,7},{8,64},{9,65},{10,... | collective-permute-start | bytes 3145736 | tf_op jit(solution)/shard_map/ppermute | solution.py:47
  9.0 0.1 iota_compare_fusion.8
  9.2 0.8 reshape.233
  10.0 0.1 reshape.234
  10.2 2.7 %and_reduce_fusion = pred[8,640]{1,0:T(8,128)(4,1)S(1)} fusion(s32[8,640]{1,0:T(8,128)S(1)} %reshape.234, pred[640,640]{1,0:T(8,128)(4,1)S(1)} %iota_compare_fusion.8), kind=kLoop, calls=%fused_computation.12 | loop fusion | flops 9825280 | bytes 435200 | tf_op jit(solution)/shard_map/reduce_or | solution.py:395
  12.8 0.2 fusion.9
  13.0 0.2 select_reduce_fusion.2
  13.3 0.1 reshape.235
  13.4 7.8 %gather_fusion.1 = bf16[448,1024]{1,0:T(8,128)(2,1)S(1)} fusion(bf16[4752,1024]{1,0:T(8,128)(2,1)} %param.15, s32[1024]{0:T(1024)S(1)} %pad_clamp_fusion.1), kind=kCustom, calls=%fused_computation.1 | custom fusion | bytes 1836800 | tf_op jit(solution)/shard_map/gather | solution.py:432
  21.2 0.7 reshape.236
  21.9 0.0 copy-start.1
  21.9 1.1 copy.55
  23.0 7.8 %all-to-all-start.1 = ((bf16[16,56,512]{2,1,0:T(8,128)(2,1)}), bf16[16,56,512]{2,1,0:T(8,128)(2,1)}, u32[]{:S(2)}, u32[]{:S(2)}) async-start(bf16[16,56,512]{2,1,0:T(8,128)(2,1)} %bitcast.18), calls=%async_computation.1 | async-start | bytes 1835008 | tf_op jit(solution)/shard_map/all_to_all | solution.py:437
  30.8 0.0 all-gather.3.cloned.1.call-start
  30.8 2.1 %fusion.24 = (bf16[64,2,1024]{2,0,1:T(8,128)(2,1)S(1)}, f32[64,2,1024]{2,0,1:T(8,128)S(1)}, f32[64,2,1024]{2,0,1:T(8,128)S(1)}, f32[64,2,1024]{2,0,1:T(8,128)S(1)}) fusion(f32[64,2,1024]{2,1,0:T(2,128)S(1)} %copy-done.1, bf16[64,2,1024]{2,1,0:T(2,128)(2,1)} %param.23, f32[64,2,1024]{2,1,0:T(2,128)} %param.21, f32[64,2,1024]{2,1,0:T(2,128)} %param.22), kind=kLoop, calls=%fused_computation.72 | loop fusion | flops 2228224 | bytes 3670016 | tf_op jit(solution)/shard_map/convert_element_type | solution.py:386
  33.0 0.7 collective-permute-start.1
  33.6 0.0 collective-permute-done.1
  33.7 9.8 %all-to-all-done.1 = bf16[16,56,512]{2,1,0:T(8,128)(2,1)} async-done(((bf16[16,56,512]{2,1,0:T(8,128)(2,1)}), bf16[16,56,512]{2,1,0:T(8,128)(2,1)}, u32[]{:S(2)}, u32[]{:S(2)}) %all-to-all-start.1) | async-done | bytes 917536 | tf_op jit(solution)/shard_map/all_to_all | solution.py:437
  43.5 0.0 collective-permute-done.query_ref
  43.5 0.1 shard_map.147
  43.6 16.6 %all_to_all.21 = bf16[8,64,768]{2,1,0:T(8,128)(2,1)} all-to-all(bf16[8,64,768]{2,1,0:T(8,128)(2,1)S(1)} %get-tuple-element.67), channel_id=1, replica_groups=mesh['xh'=2,'z'=4,'c'=2,'y'=4,'xl'=2] {'y','xl'}, dimensions={0} | all-to-all | bytes 1572864 | tf_op jit(solution)/shard_map/all_to_all | solution.py:455
  60.2 0.0 all-gather.3.cloned.1.call-update
  60.3 0.0 all-gather.5.cloned.1.call-start
  60.3 13.2 %all_to_all.22 = bf16[8,64,512]{2,1,0:T(8,128)(2,1)} all-to-all(bf16[8,64,512]{2,1,0:T(8,128)(2,1)S(1)} %get-tuple-element.69), channel_id=1, replica_groups=mesh['xh'=2,'z'=4,'c'=2,'y'=4,'xl'=2] {'y','xl'}, dimensions={0} | all-to-all | bytes 1048576 | tf_op jit(solution)/shard_map/all_to_all | solution.py:455
  73.5 0.0 all-gather.5.cloned.1.call-update
  73.5 0.2 convert_reduce_fusion
  73.7 0.6 reduce_max.9
  75.1 0.2 fusion.8
  75.3 0.4 select_reduce_fusion.1
  75.8 2.9 %fusion.5 = bf16[640,512]{1,0:T(8,128)(2,1)} fusion(bf16[896,512]{1,0:T(8,128)(2,1)} %bitcast.19, s32[640]{0:T(1024)S(1)} %add_select_fusion.2), kind=kOutput, calls=%fused_computation.17 | convolution fusion | flops 588103680 | bytes 1575424 | tf_op jit(solution)/shard_map/dot_general | solution.py:444
  78.7 3.2 %collective-permute-start.4 = (bf16[640,512]{1,0:T(8,128)(2,1)}, bf16[640,512]{1,0:T(8,128)(2,1)S(1)}, u32[]{:S(2)}, u32[]{:S(2)}) collective-permute-start(bf16[640,512]{1,0:T(8,128)(2,1)} %get-tuple-element.64.refs_0_), channel_id=1, source_target_pairs={{0,6},{1,7},{2,0},{3,1},{4,2},{5,3},{6,4},{7,5},{8,14},{9,15},{10,... | collective-permute-start | bytes 1966088 | tf_op jit(solution)/shard_map/ppermute | solution.py:47
  81.9 0.8 collective-permute-start.2
  82.8 1.2 copy.56
  84.0 1.2 copy.57
  85.2 1.2 copy.58
  86.4 0.7 stack.39.place_ref
  87.0 10.3 %collective-permute-done.3.refs_2_ = bf16[640,512]{1,0:T(8,128)(2,1)S(1)} collective-permute-done((bf16[640,512]{1,0:T(8,128)(2,1)}, bf16[640,512]{1,0:T(8,128)(2,1)S(1)}, u32[]{:S(2)}, u32[]{:S(2)}) %collective-permute-start.3) | collective-permute-done | bytes 655392 | tf_op jit(solution)/shard_map/ppermute | solution.py:47
  97.4 0.1 collective-permute-start.7
  97.5 3.4 %collective-permute-start.8 = (bf16[320,512]{1,0:T(8,128)(2,1)S(1)}, bf16[320,512]{1,0:T(8,128)(2,1)S(1)}, u32[]{:S(2)}, u32[]{:S(2)}) collective-permute-start(bf16[320,512]{1,0:T(8,128)(2,1)S(1)} %slice.39), channel_id=1, source_target_pairs={{0,6},{1,7},{2,0},{3,1},{4,2},{5,3},{6,4},{7,5},{8,14},{9,15},{10,... | collective-permute-start | bytes 983048 | tf_op jit(solution)/shard_map/ppermute | solution.py:47
  100.9 3.2 %collective-permute-start.6 = (bf16[640,512]{1,0:T(8,128)(2,1)}, bf16[640,512]{1,0:T(8,128)(2,1)S(1)}, u32[]{:S(2)}, u32[]{:S(2)}) collective-permute-start(bf16[640,512]{1,0:T(8,128)(2,1)} %collective-permute-done.2.refs_1_), channel_id=1, source_target_pairs={{0,6},{1,7},{2,0},{3,1},{4,2},{5,3},{6,4},{7,5},{8,14},{9,15},{10,... | collective-permute-start | bytes 1966088 | tf_op jit(solution)/shard_map/ppermute | solution.py:47
  104.2 5.1 %collective-permute-done.7.refs_6_ = bf16[320,512]{1,0:T(8,128)(2,1)S(1)} collective-permute-done((bf16[320,512]{1,0:T(8,128)(2,1)S(1)}, bf16[320,512]{1,0:T(8,128)(2,1)S(1)}, u32[]{:S(2)}, u32[]{:S(2)}) %collective-permute-start.7) | collective-permute-done | bytes 327712 | tf_op jit(solution)/shard_map/ppermute | solution.py:47
  109.2 0.9 collective-permute-start.9
  110.1 0.0 collective-permute-done.8.refs_7_
  110.1 1.2 collective-permute-start.10
  111.3 0.6 fusion.14
  111.9 0.2 pad_maximum_fusion.1
  112.1 10.4 %collective-permute-done.5.refs_4_ = bf16[640,512]{1,0:T(8,128)(2,1)S(1)} collective-permute-done((bf16[640,512]{1,0:T(8,128)(2,1)}, bf16[640,512]{1,0:T(8,128)(2,1)S(1)}, u32[]{:S(2)}, u32[]{:S(2)}) %collective-permute-start.5) | collective-permute-done | bytes 655392 | tf_op jit(solution)/shard_map/ppermute | solution.py:47
  122.5 0.0 collective-permute-done.6.refs_5_
  122.5 0.8 copy-done.12
  123.3 1.2 collective-permute-done.10.refs_9_
  124.5 12.2 %shard_map.148 = (f32[320,896]{1,0:T(8,128)}, bf16[320,896]{1,0:T(8,128)(2,1)}, bf16[640,4096]{1,0:T(8,128)(2,1)}) custom-call(s32[9]{0:T(128)} %stack.39.place_ref, bf16[640,512]{1,0:T(8,128)(2,1)} %get-tuple-element.64.refs_0_, bf16[640,512]{1,0:T(8,128)(2,1)} %collective-permute-done.2.refs_1_, bf16[640,512]{1,0:T(8,128)(2,1)} %copy-done.2, ...), custom_call_target="tpu_custom_call" | custom-call | flops 4026531840 | bytes 12582912 | tf_op jit(solution)/shard_map/pallas_call | solution.py:171
  136.7 0.1 collective-permute-start.12
  136.8 0.0 all-gather.5.cloned.1.call-done
  136.8 0.0 slice-start
  136.8 0.0 slice-start.2
  136.9 6.2 %fusion.29 = f32[640,512]{1,0:T(8,128)S(1)} fusion(bf16[640,4096]{1,0:T(8,128)(2,1)} %get-tuple-element.68, bf16[4096,512]{1,0:T(8,128)(2,1)} %bitcast.66), kind=kOutput, calls=%fused_computation.75 | convolution fusion | flops 2684354560 | bytes 10747904 | tf_op jit(solution)/shard_map/dot_general | solution.py:504
  143.1 0.1 dynamic-slice_convert_fusion
  143.1 3.5 %collective-permute-start.11 = (bf16[320,512]{1,0:T(8,128)(2,1)S(1)}, bf16[320,512]{1,0:T(8,128)(2,1)S(1)}, u32[]{:S(2)}, u32[]{:S(2)}) collective-permute-start(bf16[320,512]{1,0:T(8,128)(2,1)S(1)} %dynamic-slice_convert_fusion), channel_id=1, source_target_pairs={{0,64},{1,65},{2,66},{3,67},{4,68},{5,69},{6,70},{7,71},{8,72},{9,... | collective-permute-start | bytes 983048 | tf_op jit(solution)/shard_map/ppermute | solution.py:47
  146.7 0.1 fusion.13
  146.8 0.8 shard_map.149
  147.6 0.1 constant_dynamic-slice_fusion
  147.7 6.7 %collective-permute-done.12 = bf16[320,896]{1,0:T(8,128)(2,1)S(1)} collective-permute-done((bf16[320,896]{1,0:T(8,128)(2,1)}, bf16[320,896]{1,0:T(8,128)(2,1)S(1)}, u32[]{:S(2)}, u32[]{:S(2)}) %collective-permute-start.12) | collective-permute-done | bytes 573472 | tf_op jit(solution)/shard_map/ppermute | solution.py:47
  154.5 6.0 %shard_map.150 = (bf16[2,160,1024]{2,1,0:T(8,128)(2,1)}, bf16[2,160,128]{2,1,0:T(8,128)(2,1)S(1)}, bf16[2,160,128]{2,1,0:T(8,128)(2,1)S(1)}, f32[2,160,128]{2,1,0:T(8,128)S(1)}) custom-call(f32[2,160,896]{2,1,0:T(8,128)S(1)} %bitcast.55, bf16[2,160,896]{2,1,0:T(8,128)(2,1)S(1)} %bitcast.56, f32[1,768]{1,0:T(1,128)S(1)} %broadcast_in_dim.111.refs_2_, ...), custom_call_target="tpu_custom_call" | custom-call | flops 83886080 | bytes 12582912 | tf_op jit(solution)/shard_map/pallas_call | solution.py:349
  160.5 5.4 %shard_map.151 = bf16[2,160,1024]{2,1,0:T(8,128)(2,1)} custom-call(f32[2,160,512]{2,1,0:T(8,128)S(1)} %bitcast.54, bf16[2,160,512]{2,1,0:T(8,128)(2,1)S(1)} %bitcast.57, f32[1,512]{1,0:T(1,128)S(1)} %bitcast.58, f32[2,160,128]{2,1,0:T(8,128)S(1)} %get-tuple-element.129.refs_3_, ...), custom_call_target="tpu_custom_call", output_to_operand_aliasing={{}: (11, {})} | custom-call | flops 83886080 | bytes 12582912 | tf_op jit(solution)/shard_map/pallas_call | solution.py:349
  (58 shorter events, 0.4 us)
Async XLA Ops:
  7.2 36.3 %collective-permute-start = (bf16[64,8192]{1,0:T(8,128)(2,1)}, bf16[64,8192]{1,0:T(8,128)(2,1)S(1)}, u32[]{:S(2)}, u32[]{:S(2)}) collective-permute-start(bf16[64,8192]{1,0:T(8,128)(2,1)} %param.17), channel_id=1, source_target_pairs={{0,0},{1,1},{2,2},{3,3},{4,4},{5,5},{6,6},{7,7},{8,64},{9,65},{10,... | collective-permute-start | bytes 3145736 | tf_op jit(solution)/shard_map/ppermute | solution.py:47
  21.9 8.9 %copy-start.1 = (f32[64,2,1024]{2,1,0:T(2,128)S(1)}, f32[64,2,1024]{2,1,0:T(2,128)}, u32[]{:S(2)}) copy-start(f32[64,2,1024]{2,1,0:T(2,128)} %param.20) | copy-start | bytes 1572868
  23.0 20.4 %all-to-all-start.1 = ((bf16[16,56,512]{2,1,0:T(8,128)(2,1)}), bf16[16,56,512]{2,1,0:T(8,128)(2,1)}, u32[]{:S(2)}, u32[]{:S(2)}) async-start(bf16[16,56,512]{2,1,0:T(8,128)(2,1)} %bitcast.18), calls=%async_computation.1 | async-start | bytes 1835008 | tf_op jit(solution)/shard_map/all_to_all | solution.py:437
  30.8 93.7 %all-gather.3.cloned.1.call-start = ((), (), s32[]{:S(2)}) async-start(), calls=%async_computation.4 | async-start | bytes 7077888 | tf_op jit(solution)/shard_map/all_gather | solution.py:456
  33.0 0.7 collective-permute-start.1
  60.3 76.6 %all-gather.5.cloned.1.call-start = ((), (), s32[]{:S(2)}) async-start(), calls=%async_computation.5 | async-start | bytes 4718592 | tf_op jit(solution)/shard_map/all_gather | solution.py:456
  78.7 4.1 %copy-start.13 = (bf16[2,128]{1,0:T(2,128)(2,1)S(1)}, bf16[2,128]{1,0:T(2,128)(2,1)}, u32[]{:S(2)}) copy-start(bf16[2,128]{1,0:T(2,128)(2,1)} %param.19) | copy-start | bytes 1540
  78.7 4.1 %copy-start.4 = (bf16[1024]{0:T(1024)(128)(2,1)S(1)}, bf16[1024]{0:T(1024)(128)(2,1)}, u32[]{:S(2)}) copy-start(bf16[1024]{0:T(1024)(128)(2,1)} %param.18) | copy-start | bytes 6148
  78.7 18.7 %collective-permute-start.3 = (bf16[640,512]{1,0:T(8,128)(2,1)}, bf16[640,512]{1,0:T(8,128)(2,1)S(1)}, u32[]{:S(2)}, u32[]{:S(2)}) collective-permute-start(bf16[640,512]{1,0:T(8,128)(2,1)} %get-tuple-element.64.refs_0_), channel_id=1, source_target_pairs={{0,2},{1,3},{2,4},{3,5},{4,6},{5,7},{6,0},{7,1},{8,10},{9,11},{10,... | collective-permute-start | bytes 1966088 | tf_op jit(solution)/shard_map/ppermute | solution.py:47
  78.7 18.8 %collective-permute-start.4 = (bf16[640,512]{1,0:T(8,128)(2,1)}, bf16[640,512]{1,0:T(8,128)(2,1)S(1)}, u32[]{:S(2)}, u32[]{:S(2)}) collective-permute-start(bf16[640,512]{1,0:T(8,128)(2,1)} %get-tuple-element.64.refs_0_), channel_id=1, source_target_pairs={{0,6},{1,7},{2,0},{3,1},{4,2},{5,3},{6,4},{7,5},{8,14},{9,15},{10,... | collective-permute-start | bytes 1966088 | tf_op jit(solution)/shard_map/ppermute | solution.py:47
  81.9 19.0 %collective-permute-start.2 = (bf16[640,512]{1,0:T(8,128)(2,1)}, bf16[640,512]{1,0:T(8,128)(2,1)}, u32[]{:S(2)}, u32[]{:S(2)}) collective-permute-start(bf16[640,512]{1,0:T(8,128)(2,1)} %get-tuple-element.64.refs_0_), channel_id=1, source_target_pairs={{0,1},{1,0},{2,3},{3,2},{4,5},{5,4},{6,7},{7,6},{8,9},{9,8},{10,11... | collective-permute-start | bytes 1966088 | tf_op jit(solution)/shard_map/ppermute | solution.py:47
  84.0 20.2 %copy-start.5 = (s32[160]{0:T(256)S(1)}, s32[160]{0:T(256)}, u32[]{:S(2)}) copy-start(s32[160]{0:T(256)} %param.16) | copy-start | bytes 1924
  97.4 27.1 %copy-start.2 = (bf16[640,512]{1,0:T(8,128)(2,1)}, bf16[640,512]{1,0:T(8,128)(2,1)S(1)}, u32[]{:S(2)}) copy-start(bf16[640,512]{1,0:T(8,128)(2,1)S(1)} %collective-permute-done.3.refs_2_) | copy-start | bytes 1966084
  97.4 11.8 %collective-permute-start.7 = (bf16[320,512]{1,0:T(8,128)(2,1)S(1)}, bf16[320,512]{1,0:T(8,128)(2,1)S(1)}, u32[]{:S(2)}, u32[]{:S(2)}) collective-permute-start(bf16[320,512]{1,0:T(8,128)(2,1)S(1)} %slice.38), channel_id=1, source_target_pairs={{0,2},{1,3},{2,4},{3,5},{4,6},{5,7},{6,0},{7,1},{8,10},{9,11},{10,... | collective-permute-start | bytes 983048 | tf_op jit(solution)/shard_map/ppermute | solution.py:47
  97.5 27.0 %copy-start.3 = (bf16[640,512]{1,0:T(8,128)(2,1)}, bf16[640,512]{1,0:T(8,128)(2,1)S(1)}, u32[]{:S(2)}) copy-start(bf16[640,512]{1,0:T(8,128)(2,1)S(1)} %collective-permute-done.4.refs_3_) | copy-start | bytes 1966084
  97.5 12.6 %collective-permute-start.8 = (bf16[320,512]{1,0:T(8,128)(2,1)S(1)}, bf16[320,512]{1,0:T(8,128)(2,1)S(1)}, u32[]{:S(2)}, u32[]{:S(2)}) collective-permute-start(bf16[320,512]{1,0:T(8,128)(2,1)S(1)} %slice.39), channel_id=1, source_target_pairs={{0,6},{1,7},{2,0},{3,1},{4,2},{5,3},{6,4},{7,5},{8,14},{9,15},{10,... | collective-permute-start | bytes 983048 | tf_op jit(solution)/shard_map/ppermute | solution.py:47
  100.9 21.6 %collective-permute-start.5 = (bf16[640,512]{1,0:T(8,128)(2,1)}, bf16[640,512]{1,0:T(8,128)(2,1)S(1)}, u32[]{:S(2)}, u32[]{:S(2)}) collective-permute-start(bf16[640,512]{1,0:T(8,128)(2,1)} %collective-permute-done.2.refs_1_), channel_id=1, source_target_pairs={{0,2},{1,3},{2,4},{3,5},{4,6},{5,7},{6,0},{7,1},{8,10},{9,11},{10,... | collective-permute-start | bytes 1966088 | tf_op jit(solution)/shard_map/ppermute | solution.py:47
  100.9 21.6 %collective-permute-start.6 = (bf16[640,512]{1,0:T(8,128)(2,1)}, bf16[640,512]{1,0:T(8,128)(2,1)S(1)}, u32[]{:S(2)}, u32[]{:S(2)}) collective-permute-start(bf16[640,512]{1,0:T(8,128)(2,1)} %collective-permute-done.2.refs_1_), channel_id=1, source_target_pairs={{0,6},{1,7},{2,0},{3,1},{4,2},{5,3},{6,4},{7,5},{8,14},{9,15},{10,... | collective-permute-start | bytes 1966088 | tf_op jit(solution)/shard_map/ppermute | solution.py:47
  109.2 15.3 %copy-start.10 = (bf16[320,512]{1,0:T(8,128)(2,1)}, bf16[320,512]{1,0:T(8,128)(2,1)S(1)}, u32[]{:S(2)}) copy-start(bf16[320,512]{1,0:T(8,128)(2,1)S(1)} %collective-permute-done.7.refs_6_) | copy-start | bytes 983044
  109.2 13.3 %collective-permute-start.9 = (bf16[320,512]{1,0:T(8,128)(2,1)S(1)}, bf16[320,512]{1,0:T(8,128)(2,1)S(1)}, u32[]{:S(2)}, u32[]{:S(2)}) collective-permute-start(bf16[320,512]{1,0:T(8,128)(2,1)S(1)} %collective-permute-done.7.refs_6_), channel_id=1, source_target_pairs={{0,1},{1,0},{2,3},{3,2},{4,5},{5,4},{6,7},{7,6},{8,9},{9,8},{10,11... | collective-permute-start | bytes 983048 | tf_op jit(solution)/shard_map/ppermute | solution.py:47
  110.1 12.4 %copy-start.11 = (bf16[320,512]{1,0:T(8,128)(2,1)}, bf16[320,512]{1,0:T(8,128)(2,1)S(1)}, u32[]{:S(2)}) copy-start(bf16[320,512]{1,0:T(8,128)(2,1)S(1)} %collective-permute-done.8.refs_7_) | copy-start | bytes 983044
  110.1 14.4 %collective-permute-start.10 = (bf16[320,512]{1,0:T(8,128)(2,1)S(1)}, bf16[320,512]{1,0:T(8,128)(2,1)}, u32[]{:S(2)}, u32[]{:S(2)}) collective-permute-start(bf16[320,512]{1,0:T(8,128)(2,1)S(1)} %collective-permute-done.8.refs_7_), channel_id=1, source_target_pairs={{0,1},{1,0},{2,3},{3,2},{4,5},{5,4},{6,7},{7,6},{8,9},{9,8},{10,11... | collective-permute-start | bytes 983048 | tf_op jit(solution)/shard_map/ppermute | solution.py:47
  122.5 2.0 %copy-start.6 = (bf16[640,512]{1,0:T(8,128)(2,1)}, bf16[640,512]{1,0:T(8,128)(2,1)S(1)}, u32[]{:S(2)}) copy-start(bf16[640,512]{1,0:T(8,128)(2,1)S(1)} %collective-permute-done.5.refs_4_) | copy-start | bytes 1966084
  122.5 2.0 %copy-start.7 = (bf16[640,512]{1,0:T(8,128)(2,1)}, bf16[640,512]{1,0:T(8,128)(2,1)S(1)}, u32[]{:S(2)}) copy-start(bf16[640,512]{1,0:T(8,128)(2,1)S(1)} %collective-permute-done.6.refs_5_) | copy-start | bytes 1966084
  122.5 0.8 copy-start.12
  136.7 17.7 %collective-permute-start.12 = (bf16[320,896]{1,0:T(8,128)(2,1)}, bf16[320,896]{1,0:T(8,128)(2,1)S(1)}, u32[]{:S(2)}, u32[]{:S(2)}) collective-permute-start(bf16[320,896]{1,0:T(8,128)(2,1)} %get-tuple-element.70), channel_id=1, source_target_pairs={{0,64},{1,65},{2,66},{3,67},{4,68},{5,69},{6,70},{7,71},{8,72},{9,... | collective-permute-start | bytes 1720328 | tf_op jit(solution)/shard_map/ppermute | solution.py:47
  136.8 9.9 %slice-start = ((s8[5242880]{0:T(1024)(128)(4,1)}), s8[4194304]{0:T(1024)(128)(4,1)S(1)}, s32[]{:S(2)}) async-start(s8[5242880]{0:T(1024)(128)(4,1)} %bitcast.50), calls=%async_computation.6 | async-start | bytes 8388608
  136.8 9.9 %slice-start.2 = ((s8[5242880]{0:T(1024)(128)(4,1)}), s8[4194304]{0:T(1024)(128)(4,1)S(1)}, s32[]{:S(2)}) async-start(s8[5242880]{0:T(1024)(128)(4,1)} %bitcast.52), calls=%async_computation.8 | async-start | bytes 8388608
  136.9 9.9 %slice-start.1 = ((s8[5242880]{0:T(1024)(128)(4,1)}), s8[1048576]{0:T(1024)(128)(4,1)S(1)}, s32[]{:S(2)}) async-start(s8[5242880]{0:T(1024)(128)(4,1)} %bitcast.50), calls=%async_computation.7 | async-start | bytes 2097152
  136.9 9.9 %slice-start.3 = ((s8[5242880]{0:T(1024)(128)(4,1)}), s8[1048576]{0:T(1024)(128)(4,1)S(1)}, s32[]{:S(2)}) async-start(s8[5242880]{0:T(1024)(128)(4,1)} %bitcast.52), calls=%async_computation.9 | async-start | bytes 2097152
  143.1 17.4 %collective-permute-start.11 = (bf16[320,512]{1,0:T(8,128)(2,1)S(1)}, bf16[320,512]{1,0:T(8,128)(2,1)S(1)}, u32[]{:S(2)}, u32[]{:S(2)}) collective-permute-start(bf16[320,512]{1,0:T(8,128)(2,1)S(1)} %dynamic-slice_convert_fusion), channel_id=1, source_target_pairs={{0,64},{1,65},{2,66},{3,67},{4,68},{5,69},{6,70},{7,71},{8,72},{9,... | collective-permute-start | bytes 983048 | tf_op jit(solution)/shard_map/ppermute | solution.py:47
  147.6 6.8 %copy-start = (f32[320,896]{1,0:T(8,128)S(1)}, f32[320,896]{1,0:T(8,128)}, u32[]{:S(2)}) copy-start(f32[320,896]{1,0:T(8,128)} %get-tuple-element.75) | copy-start | bytes 3440644
Sparse Core Ops, SparseCore 0:
  60.4 41.3 all-gather.2
  103.5 32.1 all-gather.4

commit v6 on v5

--- a/solution.py
+++ b/solution.py
@@ -225,7 +225,7 @@
     )(k_cache, v_cache)
 
 
-BLOCK = 80
+BLOCK = 160
 
 
 def spread(scratch, array):

time: 174 us -> 174 us (level)
  no operation moved by 1% of the time
where the time goes in v6:
time: 174 us; the launch traced here: 172 us
  waiting for transfers between devices  43.6 us (25%)
  blocking collectives  29.8 us (17%)
  starting transfers between devices  26.8 us (15%)
  Pallas kernels  23.7 us (14%)
  local copies, waits for them, and re-layouts  16 us (9%)
  between operations  15.2 us (9%)
  matrix products  9.5 us (5%)
  other arithmetic  7.35 us (4%)
    ppermute x13, waiting for transfers between devices, send(): return lax.ppermute(array, NAMES, pairs_of(move))  33.8 us
    all_to_all x2, blocking collectives, gathered(): part = lax.all_to_all(part, TP, split_axis=0, concat_axis=0)  29.8 us
    ppermute x13, starting transfers between devices, send(): return lax.ppermute(array, NAMES, pairs_of(move))  18.9 us
    pallas_call x1, Pallas kernels, project(): pl.pallas_call(project_kernel, grid_spec=pltpu.PrefetchScalarGridSpec(num...  12.2 us
    pallas_call x2, Pallas kernels, attend(): pl.pallas_call(functools.partial(attend_kernel, first), grid=(ROWS // BLO...  10.6 us
    all_to_all x1, waiting for transfers between devices, exchanged(): return lax.all_to_all(rows, FSDP, split_axis=0, concat_axis=0)  9.8 us
    gather x1, local copies, waits for them, and re-layouts, wanted_rows(): rows = embedding.at[wanted.reshape(-1)].get(mode='promise_in_bounds')  7.82 us
    all_to_all x1, starting transfers between devices, exchanged(): return lax.all_to_all(rows, FSDP, split_axis=0, concat_axis=0)  7.77 us
  transfers between devices with their start and end apart: 16, of which 6 were waited for; matrix products, arithmetic and copies ran while one was open for 19% of the time, Pallas kernels for 11%

profile of v6, /device:TPU:64, one launch (start us, length us, event | category | flops | bytes accessed | tf_op | source)
XLA Modules:
  0.0 171.9 jit_solution(5572439878551620339)
XLA Ops:
  7.2 1.9 %collective-permute-start = (bf16[64,8192]{1,0:T(8,128)(2,1)}, bf16[64,8192]{1,0:T(8,128)(2,1)S(1)}, u32[]{:S(2)}, u32[]{:S(2)}) collective-permute-start(bf16[64,8192]{1,0:T(8,128)(2,1)} %param.17), channel_id=1, source_target_pairs={{0,0},{1,1},{2,2},{3,3},{4,4},{5,5},{6,6},{7,7},{8,64},{9,65},{10,... | collective-permute-start | bytes 3145736 | tf_op jit(solution)/shard_map/ppermute | solution.py:47
  9.0 0.1 iota_compare_fusion.8
  9.2 0.8 reshape.233
  10.0 0.1 reshape.234
  10.2 2.7 %and_reduce_fusion = pred[8,640]{1,0:T(8,128)(4,1)S(1)} fusion(s32[8,640]{1,0:T(8,128)S(1)} %reshape.234, pred[640,640]{1,0:T(8,128)(4,1)S(1)} %iota_compare_fusion.8), kind=kLoop, calls=%fused_computation.12 | loop fusion | flops 9825280 | bytes 435200 | tf_op jit(solution)/shard_map/reduce_or | solution.py:395
  12.8 0.2 fusion.9
  13.0 0.2 select_reduce_fusion.2
  13.3 0.1 reshape.235
  13.4 7.8 %gather_fusion.1 = bf16[448,1024]{1,0:T(8,128)(2,1)S(1)} fusion(bf16[4752,1024]{1,0:T(8,128)(2,1)} %param.15, s32[1024]{0:T(1024)S(1)} %pad_clamp_fusion.1), kind=kCustom, calls=%fused_computation.1 | custom fusion | bytes 1836800 | tf_op jit(solution)/shard_map/gather | solution.py:432
  21.2 0.7 reshape.236
  21.9 0.0 copy-start.1
  21.9 1.1 copy.55
  23.0 7.8 %all-to-all-start.1 = ((bf16[16,56,512]{2,1,0:T(8,128)(2,1)}), bf16[16,56,512]{2,1,0:T(8,128)(2,1)}, u32[]{:S(2)}, u32[]{:S(2)}) async-start(bf16[16,56,512]{2,1,0:T(8,128)(2,1)} %bitcast.18), calls=%async_computation.1 | async-start | bytes 1835008 | tf_op jit(solution)/shard_map/all_to_all | solution.py:437
  30.8 0.0 all-gather.3.cloned.1.call-start
  30.8 2.1 %fusion.24 = (bf16[64,2,1024]{2,0,1:T(8,128)(2,1)S(1)}, f32[64,2,1024]{2,0,1:T(8,128)S(1)}, f32[64,2,1024]{2,0,1:T(8,128)S(1)}, f32[64,2,1024]{2,0,1:T(8,128)S(1)}) fusion(f32[64,2,1024]{2,1,0:T(2,128)S(1)} %copy-done.1, bf16[64,2,1024]{2,1,0:T(2,128)(2,1)} %param.23, f32[64,2,1024]{2,1,0:T(2,128)} %param.21, f32[64,2,1024]{2,1,0:T(2,128)} %param.22), kind=kLoop, calls=%fused_computation.72 | loop fusion | flops 2228224 | bytes 3670016 | tf_op jit(solution)/shard_map/convert_element_type | solution.py:386
  33.0 0.7 collective-permute-start.1
  33.6 0.0 collective-permute-done.1
  33.7 9.8 %all-to-all-done.1 = bf16[16,56,512]{2,1,0:T(8,128)(2,1)} async-done(((bf16[16,56,512]{2,1,0:T(8,128)(2,1)}), bf16[16,56,512]{2,1,0:T(8,128)(2,1)}, u32[]{:S(2)}, u32[]{:S(2)}) %all-to-all-start.1) | async-done | bytes 917536 | tf_op jit(solution)/shard_map/all_to_all | solution.py:437
  43.5 0.0 collective-permute-done.query_ref
  43.5 0.1 shard_map.147
  43.6 16.6 %all_to_all.21 = bf16[8,64,768]{2,1,0:T(8,128)(2,1)} all-to-all(bf16[8,64,768]{2,1,0:T(8,128)(2,1)S(1)} %get-tuple-element.67), channel_id=1, replica_groups=mesh['xh'=2,'z'=4,'c'=2,'y'=4,'xl'=2] {'y','xl'}, dimensions={0} | all-to-all | bytes 1572864 | tf_op jit(solution)/shard_map/all_to_all | solution.py:455
  60.2 0.0 all-gather.3.cloned.1.call-update
  60.3 0.0 all-gather.5.cloned.1.call-start
  60.3 13.2 %all_to_all.22 = bf16[8,64,512]{2,1,0:T(8,128)(2,1)} all-to-all(bf16[8,64,512]{2,1,0:T(8,128)(2,1)S(1)} %get-tuple-element.69), channel_id=1, replica_groups=mesh['xh'=2,'z'=4,'c'=2,'y'=4,'xl'=2] {'y','xl'}, dimensions={0} | all-to-all | bytes 1048576 | tf_op jit(solution)/shard_map/all_to_all | solution.py:455
  73.5 0.0 all-gather.5.cloned.1.call-update
  73.5 0.2 convert_reduce_fusion
  73.7 0.6 reduce_max.9
  75.1 0.2 fusion.8
  75.3 0.4 select_reduce_fusion.1
  75.8 2.9 %fusion.5 = bf16[640,512]{1,0:T(8,128)(2,1)} fusion(bf16[896,512]{1,0:T(8,128)(2,1)} %bitcast.19, s32[640]{0:T(1024)S(1)} %add_select_fusion.2), kind=kOutput, calls=%fused_computation.17 | convolution fusion | flops 588103680 | bytes 1575424 | tf_op jit(solution)/shard_map/dot_general | solution.py:444
  78.7 3.2 %collective-permute-start.4 = (bf16[640,512]{1,0:T(8,128)(2,1)}, bf16[640,512]{1,0:T(8,128)(2,1)S(1)}, u32[]{:S(2)}, u32[]{:S(2)}) collective-permute-start(bf16[640,512]{1,0:T(8,128)(2,1)} %get-tuple-element.64.refs_0_), channel_id=1, source_target_pairs={{0,6},{1,7},{2,0},{3,1},{4,2},{5,3},{6,4},{7,5},{8,14},{9,15},{10,... | collective-permute-start | bytes 1966088 | tf_op jit(solution)/shard_map/ppermute | solution.py:47
  81.9 0.8 collective-permute-start.2
  82.8 1.2 copy.56
  84.0 1.2 copy.57
  85.2 1.2 copy.58
  86.4 0.7 stack.39.place_ref
  87.0 10.3 %collective-permute-done.3.refs_2_ = bf16[640,512]{1,0:T(8,128)(2,1)S(1)} collective-permute-done((bf16[640,512]{1,0:T(8,128)(2,1)}, bf16[640,512]{1,0:T(8,128)(2,1)S(1)}, u32[]{:S(2)}, u32[]{:S(2)}) %collective-permute-start.3) | collective-permute-done | bytes 655392 | tf_op jit(solution)/shard_map/ppermute | solution.py:47
  97.4 0.1 collective-permute-start.7
  97.5 3.4 %collective-permute-start.8 = (bf16[320,512]{1,0:T(8,128)(2,1)S(1)}, bf16[320,512]{1,0:T(8,128)(2,1)S(1)}, u32[]{:S(2)}, u32[]{:S(2)}) collective-permute-start(bf16[320,512]{1,0:T(8,128)(2,1)S(1)} %slice.39), channel_id=1, source_target_pairs={{0,6},{1,7},{2,0},{3,1},{4,2},{5,3},{6,4},{7,5},{8,14},{9,15},{10,... | collective-permute-start | bytes 983048 | tf_op jit(solution)/shard_map/ppermute | solution.py:47
  100.9 3.2 %collective-permute-start.6 = (bf16[640,512]{1,0:T(8,128)(2,1)}, bf16[640,512]{1,0:T(8,128)(2,1)S(1)}, u32[]{:S(2)}, u32[]{:S(2)}) collective-permute-start(bf16[640,512]{1,0:T(8,128)(2,1)} %collective-permute-done.2.refs_1_), channel_id=1, source_target_pairs={{0,6},{1,7},{2,0},{3,1},{4,2},{5,3},{6,4},{7,5},{8,14},{9,15},{10,... | collective-permute-start | bytes 1966088 | tf_op jit(solution)/shard_map/ppermute | solution.py:47
  104.2 5.1 %collective-permute-done.7.refs_6_ = bf16[320,512]{1,0:T(8,128)(2,1)S(1)} collective-permute-done((bf16[320,512]{1,0:T(8,128)(2,1)S(1)}, bf16[320,512]{1,0:T(8,128)(2,1)S(1)}, u32[]{:S(2)}, u32[]{:S(2)}) %collective-permute-start.7) | collective-permute-done | bytes 327712 | tf_op jit(solution)/shard_map/ppermute | solution.py:47
  109.2 0.9 collective-permute-start.9
  110.1 0.0 collective-permute-done.8.refs_7_
  110.1 1.2 collective-permute-start.10
  111.3 0.6 fusion.14
  111.9 0.2 pad_maximum_fusion.1
  112.1 10.4 %collective-permute-done.5.refs_4_ = bf16[640,512]{1,0:T(8,128)(2,1)S(1)} collective-permute-done((bf16[640,512]{1,0:T(8,128)(2,1)}, bf16[640,512]{1,0:T(8,128)(2,1)S(1)}, u32[]{:S(2)}, u32[]{:S(2)}) %collective-permute-start.5) | collective-permute-done | bytes 655392 | tf_op jit(solution)/shard_map/ppermute | solution.py:47
  122.5 0.0 collective-permute-done.6.refs_5_
  122.5 0.8 copy-done.12
  123.3 1.2 collective-permute-done.10.refs_9_
  124.5 12.2 %shard_map.148 = (f32[320,896]{1,0:T(8,128)}, bf16[320,896]{1,0:T(8,128)(2,1)}, bf16[640,4096]{1,0:T(8,128)(2,1)}) custom-call(s32[9]{0:T(128)} %stack.39.place_ref, bf16[640,512]{1,0:T(8,128)(2,1)} %get-tuple-element.64.refs_0_, bf16[640,512]{1,0:T(8,128)(2,1)} %collective-permute-done.2.refs_1_, bf16[640,512]{1,0:T(8,128)(2,1)} %copy-done.2, ...), custom_call_target="tpu_custom_call" | custom-call | flops 4026531840 | bytes 12582912 | tf_op jit(solution)/shard_map/pallas_call | solution.py:171
  136.7 0.1 collective-permute-start.12
  136.8 0.0 all-gather.5.cloned.1.call-done
  136.8 0.0 slice-start
  136.8 0.0 slice-start.2
  136.9 6.2 %fusion.29 = f32[640,512]{1,0:T(8,128)S(1)} fusion(bf16[640,4096]{1,0:T(8,128)(2,1)} %get-tuple-element.68, bf16[4096,512]{1,0:T(8,128)(2,1)} %bitcast.66), kind=kOutput, calls=%fused_computation.75 | convolution fusion | flops 2684354560 | bytes 10747904 | tf_op jit(solution)/shard_map/dot_general | solution.py:504
  143.1 0.1 dynamic-slice_convert_fusion
  143.1 3.5 %collective-permute-start.11 = (bf16[320,512]{1,0:T(8,128)(2,1)S(1)}, bf16[320,512]{1,0:T(8,128)(2,1)S(1)}, u32[]{:S(2)}, u32[]{:S(2)}) collective-permute-start(bf16[320,512]{1,0:T(8,128)(2,1)S(1)} %dynamic-slice_convert_fusion), channel_id=1, source_target_pairs={{0,64},{1,65},{2,66},{3,67},{4,68},{5,69},{6,70},{7,71},{8,72},{9,... | collective-permute-start | bytes 983048 | tf_op jit(solution)/shard_map/ppermute | solution.py:47
  146.7 0.1 fusion.13
  146.8 0.8 shard_map.149
  147.6 0.1 constant_dynamic-slice_fusion
  147.7 6.7 %collective-permute-done.12 = bf16[320,896]{1,0:T(8,128)(2,1)S(1)} collective-permute-done((bf16[320,896]{1,0:T(8,128)(2,1)}, bf16[320,896]{1,0:T(8,128)(2,1)S(1)}, u32[]{:S(2)}, u32[]{:S(2)}) %collective-permute-start.12) | collective-permute-done | bytes 573472 | tf_op jit(solution)/shard_map/ppermute | solution.py:47
  154.5 5.5 %shard_map.150 = (bf16[2,160,1024]{2,1,0:T(8,128)(2,1)}, bf16[2,160,128]{2,1,0:T(8,128)(2,1)S(1)}, bf16[2,160,128]{2,1,0:T(8,128)(2,1)S(1)}, f32[2,160,128]{2,1,0:T(8,128)S(1)}) custom-call(f32[2,160,896]{2,1,0:T(8,128)S(1)} %bitcast.55, bf16[2,160,896]{2,1,0:T(8,128)(2,1)S(1)} %bitcast.56, f32[1,768]{1,0:T(1,128)S(1)} %broadcast_in_dim.111.refs_2_, ...), custom_call_target="tpu_custom_call" | custom-call | flops 83886080 | bytes 12582912 | tf_op jit(solution)/shard_map/pallas_call | solution.py:349
  160.0 5.1 %shard_map.151 = bf16[2,160,1024]{2,1,0:T(8,128)(2,1)} custom-call(f32[2,160,512]{2,1,0:T(8,128)S(1)} %bitcast.54, bf16[2,160,512]{2,1,0:T(8,128)(2,1)S(1)} %bitcast.57, f32[1,512]{1,0:T(1,128)S(1)} %bitcast.58, f32[2,160,128]{2,1,0:T(8,128)S(1)} %get-tuple-element.129.refs_3_, ...), custom_call_target="tpu_custom_call", output_to_operand_aliasing={{}: (11, {})} | custom-call | flops 83886080 | bytes 12582912 | tf_op jit(solution)/shard_map/pallas_call | solution.py:349
  (58 shorter events, 0.4 us)
Async XLA Ops:
  7.2 36.3 %collective-permute-start = (bf16[64,8192]{1,0:T(8,128)(2,1)}, bf16[64,8192]{1,0:T(8,128)(2,1)S(1)}, u32[]{:S(2)}, u32[]{:S(2)}) collective-permute-start(bf16[64,8192]{1,0:T(8,128)(2,1)} %param.17), channel_id=1, source_target_pairs={{0,0},{1,1},{2,2},{3,3},{4,4},{5,5},{6,6},{7,7},{8,64},{9,65},{10,... | collective-permute-start | bytes 3145736 | tf_op jit(solution)/shard_map/ppermute | solution.py:47
  21.9 8.9 %copy-start.1 = (f32[64,2,1024]{2,1,0:T(2,128)S(1)}, f32[64,2,1024]{2,1,0:T(2,128)}, u32[]{:S(2)}) copy-start(f32[64,2,1024]{2,1,0:T(2,128)} %param.20) | copy-start | bytes 1572868
  23.0 20.4 %all-to-all-start.1 = ((bf16[16,56,512]{2,1,0:T(8,128)(2,1)}), bf16[16,56,512]{2,1,0:T(8,128)(2,1)}, u32[]{:S(2)}, u32[]{:S(2)}) async-start(bf16[16,56,512]{2,1,0:T(8,128)(2,1)} %bitcast.18), calls=%async_computation.1 | async-start | bytes 1835008 | tf_op jit(solution)/shard_map/all_to_all | solution.py:437
  30.8 93.7 %all-gather.3.cloned.1.call-start = ((), (), s32[]{:S(2)}) async-start(), calls=%async_computation.4 | async-start | bytes 7077888 | tf_op jit(solution)/shard_map/all_gather | solution.py:456
  33.0 0.7 collective-permute-start.1
  60.3 76.6 %all-gather.5.cloned.1.call-start = ((), (), s32[]{:S(2)}) async-start(), calls=%async_computation.5 | async-start | bytes 4718592 | tf_op jit(solution)/shard_map/all_gather | solution.py:456
  78.7 4.1 %copy-start.13 = (bf16[2,128]{1,0:T(2,128)(2,1)S(1)}, bf16[2,128]{1,0:T(2,128)(2,1)}, u32[]{:S(2)}) copy-start(bf16[2,128]{1,0:T(2,128)(2,1)} %param.19) | copy-start | bytes 1540
  78.7 4.1 %copy-start.4 = (bf16[1024]{0:T(1024)(128)(2,1)S(1)}, bf16[1024]{0:T(1024)(128)(2,1)}, u32[]{:S(2)}) copy-start(bf16[1024]{0:T(1024)(128)(2,1)} %param.18) | copy-start | bytes 6148
  78.7 18.7 %collective-permute-start.3 = (bf16[640,512]{1,0:T(8,128)(2,1)}, bf16[640,512]{1,0:T(8,128)(2,1)S(1)}, u32[]{:S(2)}, u32[]{:S(2)}) collective-permute-start(bf16[640,512]{1,0:T(8,128)(2,1)} %get-tuple-element.64.refs_0_), channel_id=1, source_target_pairs={{0,2},{1,3},{2,4},{3,5},{4,6},{5,7},{6,0},{7,1},{8,10},{9,11},{10,... | collective-permute-start | bytes 1966088 | tf_op jit(solution)/shard_map/ppermute | solution.py:47
  78.7 18.8 %collective-permute-start.4 = (bf16[640,512]{1,0:T(8,128)(2,1)}, bf16[640,512]{1,0:T(8,128)(2,1)S(1)}, u32[]{:S(2)}, u32[]{:S(2)}) collective-permute-start(bf16[640,512]{1,0:T(8,128)(2,1)} %get-tuple-element.64.refs_0_), channel_id=1, source_target_pairs={{0,6},{1,7},{2,0},{3,1},{4,2},{5,3},{6,4},{7,5},{8,14},{9,15},{10,... | collective-permute-start | bytes 1966088 | tf_op jit(solution)/shard_map/ppermute | solution.py:47
  81.9 19.0 %collective-permute-start.2 = (bf16[640,512]{1,0:T(8,128)(2,1)}, bf16[640,512]{1,0:T(8,128)(2,1)}, u32[]{:S(2)}, u32[]{:S(2)}) collective-permute-start(bf16[640,512]{1,0:T(8,128)(2,1)} %get-tuple-element.64.refs_0_), channel_id=1, source_target_pairs={{0,1},{1,0},{2,3},{3,2},{4,5},{5,4},{6,7},{7,6},{8,9},{9,8},{10,11... | collective-permute-start | bytes 1966088 | tf_op jit(solution)/shard_map/ppermute | solution.py:47
  84.0 20.2 %copy-start.5 = (s32[160]{0:T(256)S(1)}, s32[160]{0:T(256)}, u32[]{:S(2)}) copy-start(s32[160]{0:T(256)} %param.16) | copy-start | bytes 1924
  97.4 27.1 %copy-start.2 = (bf16[640,512]{1,0:T(8,128)(2,1)}, bf16[640,512]{1,0:T(8,128)(2,1)S(1)}, u32[]{:S(2)}) copy-start(bf16[640,512]{1,0:T(8,128)(2,1)S(1)} %collective-permute-done.3.refs_2_) | copy-start | bytes 1966084
  97.4 11.8 %collective-permute-start.7 = (bf16[320,512]{1,0:T(8,128)(2,1)S(1)}, bf16[320,512]{1,0:T(8,128)(2,1)S(1)}, u32[]{:S(2)}, u32[]{:S(2)}) collective-permute-start(bf16[320,512]{1,0:T(8,128)(2,1)S(1)} %slice.38), channel_id=1, source_target_pairs={{0,2},{1,3},{2,4},{3,5},{4,6},{5,7},{6,0},{7,1},{8,10},{9,11},{10,... | collective-permute-start | bytes 983048 | tf_op jit(solution)/shard_map/ppermute | solution.py:47
  97.5 27.0 %copy-start.3 = (bf16[640,512]{1,0:T(8,128)(2,1)}, bf16[640,512]{1,0:T(8,128)(2,1)S(1)}, u32[]{:S(2)}) copy-start(bf16[640,512]{1,0:T(8,128)(2,1)S(1)} %collective-permute-done.4.refs_3_) | copy-start | bytes 1966084
  97.5 12.6 %collective-permute-start.8 = (bf16[320,512]{1,0:T(8,128)(2,1)S(1)}, bf16[320,512]{1,0:T(8,128)(2,1)S(1)}, u32[]{:S(2)}, u32[]{:S(2)}) collective-permute-start(bf16[320,512]{1,0:T(8,128)(2,1)S(1)} %slice.39), channel_id=1, source_target_pairs={{0,6},{1,7},{2,0},{3,1},{4,2},{5,3},{6,4},{7,5},{8,14},{9,15},{10,... | collective-permute-start | bytes 983048 | tf_op jit(solution)/shard_map/ppermute | solution.py:47
  100.9 21.6 %collective-permute-start.5 = (bf16[640,512]{1,0:T(8,128)(2,1)}, bf16[640,512]{1,0:T(8,128)(2,1)S(1)}, u32[]{:S(2)}, u32[]{:S(2)}) collective-permute-start(bf16[640,512]{1,0:T(8,128)(2,1)} %collective-permute-done.2.refs_1_), channel_id=1, source_target_pairs={{0,2},{1,3},{2,4},{3,5},{4,6},{5,7},{6,0},{7,1},{8,10},{9,11},{10,... | collective-permute-start | bytes 1966088 | tf_op jit(solution)/shard_map/ppermute | solution.py:47
  100.9 21.6 %collective-permute-start.6 = (bf16[640,512]{1,0:T(8,128)(2,1)}, bf16[640,512]{1,0:T(8,128)(2,1)S(1)}, u32[]{:S(2)}, u32[]{:S(2)}) collective-permute-start(bf16[640,512]{1,0:T(8,128)(2,1)} %collective-permute-done.2.refs_1_), channel_id=1, source_target_pairs={{0,6},{1,7},{2,0},{3,1},{4,2},{5,3},{6,4},{7,5},{8,14},{9,15},{10,... | collective-permute-start | bytes 1966088 | tf_op jit(solution)/shard_map/ppermute | solution.py:47
  109.2 15.3 %copy-start.10 = (bf16[320,512]{1,0:T(8,128)(2,1)}, bf16[320,512]{1,0:T(8,128)(2,1)S(1)}, u32[]{:S(2)}) copy-start(bf16[320,512]{1,0:T(8,128)(2,1)S(1)} %collective-permute-done.7.refs_6_) | copy-start | bytes 983044
  109.2 13.3 %collective-permute-start.9 = (bf16[320,512]{1,0:T(8,128)(2,1)S(1)}, bf16[320,512]{1,0:T(8,128)(2,1)S(1)}, u32[]{:S(2)}, u32[]{:S(2)}) collective-permute-start(bf16[320,512]{1,0:T(8,128)(2,1)S(1)} %collective-permute-done.7.refs_6_), channel_id=1, source_target_pairs={{0,1},{1,0},{2,3},{3,2},{4,5},{5,4},{6,7},{7,6},{8,9},{9,8},{10,11... | collective-permute-start | bytes 983048 | tf_op jit(solution)/shard_map/ppermute | solution.py:47
  110.1 12.4 %copy-start.11 = (bf16[320,512]{1,0:T(8,128)(2,1)}, bf16[320,512]{1,0:T(8,128)(2,1)S(1)}, u32[]{:S(2)}) copy-start(bf16[320,512]{1,0:T(8,128)(2,1)S(1)} %collective-permute-done.8.refs_7_) | copy-start | bytes 983044
  110.1 14.4 %collective-permute-start.10 = (bf16[320,512]{1,0:T(8,128)(2,1)S(1)}, bf16[320,512]{1,0:T(8,128)(2,1)}, u32[]{:S(2)}, u32[]{:S(2)}) collective-permute-start(bf16[320,512]{1,0:T(8,128)(2,1)S(1)} %collective-permute-done.8.refs_7_), channel_id=1, source_target_pairs={{0,1},{1,0},{2,3},{3,2},{4,5},{5,4},{6,7},{7,6},{8,9},{9,8},{10,11... | collective-permute-start | bytes 983048 | tf_op jit(solution)/shard_map/ppermute | solution.py:47
  122.5 2.0 %copy-start.6 = (bf16[640,512]{1,0:T(8,128)(2,1)}, bf16[640,512]{1,0:T(8,128)(2,1)S(1)}, u32[]{:S(2)}) copy-start(bf16[640,512]{1,0:T(8,128)(2,1)S(1)} %collective-permute-done.5.refs_4_) | copy-start | bytes 1966084
  122.5 2.0 %copy-start.7 = (bf16[640,512]{1,0:T(8,128)(2,1)}, bf16[640,512]{1,0:T(8,128)(2,1)S(1)}, u32[]{:S(2)}) copy-start(bf16[640,512]{1,0:T(8,128)(2,1)S(1)} %collective-permute-done.6.refs_5_) | copy-start | bytes 1966084
  122.5 0.8 copy-start.12
  136.7 17.7 %collective-permute-start.12 = (bf16[320,896]{1,0:T(8,128)(2,1)}, bf16[320,896]{1,0:T(8,128)(2,1)S(1)}, u32[]{:S(2)}, u32[]{:S(2)}) collective-permute-start(bf16[320,896]{1,0:T(8,128)(2,1)} %get-tuple-element.70), channel_id=1, source_target_pairs={{0,64},{1,65},{2,66},{3,67},{4,68},{5,69},{6,70},{7,71},{8,72},{9,... | collective-permute-start | bytes 1720328 | tf_op jit(solution)/shard_map/ppermute | solution.py:47
  136.8 9.9 %slice-start = ((s8[5242880]{0:T(1024)(128)(4,1)}), s8[4194304]{0:T(1024)(128)(4,1)S(1)}, s32[]{:S(2)}) async-start(s8[5242880]{0:T(1024)(128)(4,1)} %bitcast.50), calls=%async_computation.6 | async-start | bytes 8388608
  136.8 9.9 %slice-start.2 = ((s8[5242880]{0:T(1024)(128)(4,1)}), s8[4194304]{0:T(1024)(128)(4,1)S(1)}, s32[]{:S(2)}) async-start(s8[5242880]{0:T(1024)(128)(4,1)} %bitcast.52), calls=%async_computation.8 | async-start | bytes 8388608
  136.9 9.9 %slice-start.1 = ((s8[5242880]{0:T(1024)(128)(4,1)}), s8[1048576]{0:T(1024)(128)(4,1)S(1)}, s32[]{:S(2)}) async-start(s8[5242880]{0:T(1024)(128)(4,1)} %bitcast.50), calls=%async_computation.7 | async-start | bytes 2097152
  136.9 9.9 %slice-start.3 = ((s8[5242880]{0:T(1024)(128)(4,1)}), s8[1048576]{0:T(1024)(128)(4,1)S(1)}, s32[]{:S(2)}) async-start(s8[5242880]{0:T(1024)(128)(4,1)} %bitcast.52), calls=%async_computation.9 | async-start | bytes 2097152
  143.1 16.9 %collective-permute-start.11 = (bf16[320,512]{1,0:T(8,128)(2,1)S(1)}, bf16[320,512]{1,0:T(8,128)(2,1)S(1)}, u32[]{:S(2)}, u32[]{:S(2)}) collective-permute-start(bf16[320,512]{1,0:T(8,128)(2,1)S(1)} %dynamic-slice_convert_fusion), channel_id=1, source_target_pairs={{0,64},{1,65},{2,66},{3,67},{4,68},{5,69},{6,70},{7,71},{8,72},{9,... | collective-permute-start | bytes 983048 | tf_op jit(solution)/shard_map/ppermute | solution.py:47
  147.6 6.8 %copy-start = (f32[320,896]{1,0:T(8,128)S(1)}, f32[320,896]{1,0:T(8,128)}, u32[]{:S(2)}) copy-start(f32[320,896]{1,0:T(8,128)} %get-tuple-element.75) | copy-start | bytes 3440644
Sparse Core Ops, SparseCore 0:
  60.4 41.3 all-gather.2
  103.5 32.1 all-gather.4
